TPU v7x, 32 devices: a whole 2x2x4 slice. The times are simulated.
32 devices in a mesh: grp: 2 (over y), pan: 16 (over z, x, core).
Axes of the slice: x: 2, y: 2, z: 4, core: 2. Of those that a mesh axis runs over, the one named last changes fastest.
Arguments:
- blocks: bfloat16 [1280, 512, 128], P(('grp', 'pan')), parts along dimension 0, may hold values from -6 to 6
- first_block: int32 [1280], P(('grp', 'pan')), parts along dimension 0, may hold values from 0 to 751
- second_block: int32 [1280], P(('grp', 'pan')), parts along dimension 0, may hold values from 0 to 1503
- slot_counts: int32 [32], P(('grp', 'pan')), parts along dimension 0, may hold values from 1 to 40, 240 in all
- ket_first: int32 [8], P('grp'), parts along dimension 0, may hold values from 0 to 751
- ket_second: int32 [8], P('grp'), parts along dimension 0, may hold values from 0 to 1503
- coefficients: bfloat16 [24064, 2000], P(('grp', 'pan')), parts along dimension 0, may hold values from -2 to 2
- mo_index: int32 [128], P('grp'), parts along dimension 0, may hold values from 0 to 1999, as said below
Outputs:
- integrals: float32 [8192, 4096], P(('grp', 'pan')), parts along dimension 0
There are 2 independent parts, one for each index of `grp`. A program takes and returns all parts, laid end to end along the dimension named above; each array names one. Nothing has to cross between parts.
Inputs may be any that keep to these rules, and one draw needn't show every extreme that they name: `slot_counts`: the counts sum to 240; the largest is exactly 40. `mo_index`: distinct orbital numbers.
All inputs are finite; a program needn't handle non-finite values. No bound on the sum of `slot_counts` on one device may be relied on, other than what follows from the above.
Results may differ from a plain program's by a relative error of at most 0.005.
Values may be sent and summed in bfloat16 or wider, within the bound.
No kernel may reach another device: no remote copies, remote signals or barrier semaphores. Data moves between devices by JAX's collectives and lax.ppermute only.
A program may use at most 128 MiB of HBM per device.

v0:
```python
import functools

import jax
import jax.numpy as jnp
from jax import lax
from jax.experimental import pallas as pl
from jax.experimental.pallas import tpu as pltpu
from jax.sharding import PartitionSpec as P

GROUP = 32
STEP = 8
LANES = 128
BF = jnp.bfloat16
F32 = jnp.float32
VMEM_LIMIT = 58 * 2**20


def spread(kind):
    row = lax.broadcasted_iota(jnp.int32, (LANES, LANES), 0)
    col = lax.broadcasted_iota(jnp.int32, (LANES, LANES), 1)
    source = col // 8 if kind == "a" else col % 8
    return (row == source).astype(F32).astype(BF)


def table_piece(table, place, target):
    core, z, x, lane = place
    inside = lane & (LANES - 1)
    start = pl.multiple_of(lane - inside, LANES)
    piece = table[core, z, x, :, pl.ds(start, LANES)].astype(F32)
    return pltpu.roll(piece, (target - inside) & (LANES - 1), 1)


def load_table(regions, parts, table, sems):
    return [
        pltpu.make_async_copy(part, table.at[region], sems.at[n])
        for n, (region, part) in enumerate(zip(regions, parts))
    ]


def bra_kernel(regions, locate, chunk, pieces, me_ref, mine, theirs, firsts, seconds, *refs):
    parts, refs = refs[: len(regions)], refs[len(regions) :]
    own, other = refs[:2]
    outs, ket = refs[2 : 2 + len(pieces)], refs[2 + len(pieces)]
    table, blk, picked, wide, half, second, ready, table_sems, block_sems, out_sems = refs[
        3 + len(pieces) :
    ]
    orbitals = second.shape[1]
    capacity = own.shape[0]
    kh = blk.shape[1]
    me = me_ref[0]
    own_live, other_live = mine[2 * capacity], theirs[2 * capacity]
    k_start = pl.multiple_of((me & 1) * kh, LANES)
    live = own_live + other_live

    copies = load_table(regions, parts, table, table_sems)
    for copy in copies:
        copy.start()

    def start_own(n, carry):
        pltpu.make_async_copy(
            own.at[n, pl.ds(k_start, kh)], blk.at[n], block_sems.at[n // STEP]
        ).start()
        return carry

    def start_other(n, carry):
        pltpu.make_async_copy(
            other.at[n - own_live, pl.ds(k_start, kh)], blk.at[n], block_sems.at[n // STEP]
        ).start()
        return carry

    lax.fori_loop(0, own_live, start_own, 0)
    lax.fori_loop(own_live, live, start_other, 0)
    lanes = lax.broadcasted_iota(jnp.int32, (8, LANES), 1)
    diagonal = (lanes % 8 == lax.broadcasted_iota(jnp.int32, (8, LANES), 0)).astype(F32)
    empty = jnp.zeros((8, LANES), F32)
    spread_a = spread("a")
    groups = (live + GROUP - 1) // GROUP
    steps = (live + STEP - 1) // STEP
    second[...] = jnp.zeros_like(second)

    def number(n, column):
        ours = mine[column * capacity + jnp.minimum(n, own_live - 1)]
        partners = theirs[column * capacity + jnp.maximum(n - own_live, 0)]
        return jnp.where(n < own_live, ours, partners)

    for copy in copies:
        copy.wait()

    count = ket.shape[1]
    for n in range(count):
        kb = (n + (me & 1) * (count // 2)) & (count - 1)
        piece = table_piece(table, locate(firsts[kb] * 2, me), 0)
        ket[0, n] = jnp.dot(piece.astype(BF), spread_a, preferred_element_type=F32)
        piece = table_piece(table, locate(seconds[kb], me), 0)
        ket[1, n] = jnp.dot(piece.astype(BF), spread("b"), preferred_element_type=F32)

    def do_step(o, carry):
        start = o * STEP

        def wait_one(n, carry):
            pltpu.make_async_copy(
                own.at[0, pl.ds(k_start, kh)], blk.at[n], block_sems.at[o]
            ).wait()
            return carry

        lax.fori_loop(start, jnp.minimum(start + STEP, live), wait_one, 0)
        slots = [jnp.minimum(start + u, live - 1) for u in range(STEP)]
        for u, n in enumerate(slots):
            piece = table_piece(table, locate(number(n, 0) * 2, me), 0)
            picked[u * orbitals : (u + 1) * orbitals] = piece.astype(BF)
        wide[...] = jnp.dot(picked[...], spread_a, preferred_element_type=F32)

        cover = 8 * STEP
        parity = o & (LANES // cover - 1)
        wanted = lax.broadcasted_iota(jnp.int32, (orbitals, LANES), 1)
        place = (wanted % cover) // 8
        merged = jnp.zeros((orbitals, LANES), F32)
        for u, n in enumerate(slots):
            where = locate(number(n, 1), me)
            piece = table_piece(table, where, parity * cover + 8 * u)
            merged = jnp.where(place == u, piece, merged)
        keep = (wanted // cover == parity) & (start + place < live)
        at = o // (LANES // cover)
        second[at] = jnp.where(keep, merged, second[at])

        for p in range(STEP // 2):
            rows = []
            for i in range(orbitals):
                x, y = (
                    jnp.broadcast_to(wide[u * orbitals + i : u * orbitals + i + 1, :], (8, LANES))
                    * diagonal
                    for u in (2 * p, 2 * p + 1)
                )
                rows.append(jnp.concatenate([x, empty], axis=1))
                rows.append(jnp.concatenate([empty, y], axis=1))
            factor = jnp.concatenate(rows, axis=0).astype(BF)
            data = jnp.concatenate([blk[slots[2 * p]], blk[slots[2 * p + 1]]], axis=1)
            result = lax.dot_general(
                factor, data, (((1,), (1,)), ((), ())), preferred_element_type=F32
            )
            at = pl.multiple_of(o * cover + 16 * p, 16)
            half[:, pl.ds(at, 16), :] = result.astype(BF).reshape(orbitals, 16, kh)
        return carry

    lax.fori_loop(0, steps, do_step, 0)

    def clear(o, carry):
        at = pl.multiple_of(o * 8 * STEP, 8 * STEP)
        half[:, pl.ds(at, 8 * STEP), :] = jnp.zeros((orbitals, 8 * STEP, kh), BF)
        return carry

    lax.fori_loop(steps, groups * (GROUP // STEP), clear, 0)

    def leave(n):
        s, low, high = pieces[n]
        return pltpu.make_async_copy(
            ready.at[s, :, pl.ds(low, high - low)], outs[n], out_sems.at[n]
        )

    def finish(count):
        weights = jnp.concatenate([second[n] for n in range(2 * count)], axis=1).astype(BF)
        for s in dict.fromkeys(piece[0] for piece in pieces):
            first = 0
            if len(pieces) > 1:
                first = ((me >> 2) ^ (s & 3)) * 2 * chunk + (((me >> 1) & 1) ^ (1 - (s >> 2))) * chunk
            for r in range(chunk):
                piece = half[first + r, 0 : 8 * GROUP * count, :]
                ready[s, r * orbitals : (r + 1) * orbitals, :] = jnp.dot(
                    weights, piece, preferred_element_type=F32
                ).astype(ready.dtype)
            for n in range(len(pieces)):
                if pieces[n][0] == s:
                    leave(n).start()

    for count in range(1, half.shape[1] // (8 * GROUP) + 1):
        pl.when(groups == count)(functools.partial(finish, count))
    for n in range(len(pieces)):
        leave(n).wait()


def bra_transform(
    regions, locate, parts, own, other, numbers, ket_numbers, me, orbitals, chunk, pieces, kind
):
    capacity, kp, pair = own.shape
    kh = kp // 2
    groups = -(-2 * capacity // GROUP)
    rows = chunk * orbitals
    hbm = pl.BlockSpec(memory_space=pltpu.HBM)
    return pl.pallas_call(
        functools.partial(bra_kernel, regions, locate, chunk, pieces),
        out_shape=[jax.ShapeDtypeStruct((rows, high - low), kind) for _, low, high in pieces]
        + [jax.ShapeDtypeStruct((2, kp // LANES, orbitals, LANES), F32)],
        grid_spec=pltpu.PrefetchScalarGridSpec(
            num_scalar_prefetch=5,
            grid=(),
            in_specs=[hbm] * (len(parts) + 2),
            out_specs=[hbm] * len(pieces) + [pl.BlockSpec(memory_space=pltpu.VMEM)],
            scratch_shapes=[
                pltpu.VMEM(table_shape(parts, orbitals), BF),
                pltpu.VMEM((2 * capacity, kh, pair), BF),
                pltpu.VMEM((STEP * orbitals, LANES), BF),
                pltpu.VMEM((STEP * orbitals, LANES), F32),
                pltpu.VMEM((orbitals, 8 * GROUP * groups, kh), BF),
                pltpu.VMEM((2 * groups, orbitals, LANES), F32),
                pltpu.VMEM((orbitals // chunk, rows, kh), kind),
                pltpu.SemaphoreType.DMA((len(parts),)),
                pltpu.SemaphoreType.DMA((-(-2 * capacity // STEP),)),
                pltpu.SemaphoreType.DMA((len(pieces),)),
            ],
        ),
        compiler_params=pltpu.CompilerParams(vmem_limit_bytes=VMEM_LIMIT),
        cost_estimate=pl.CostEstimate(
            flops=4 * capacity * 8 * orbitals * pair * kh, bytes_accessed=8 * 2**20, transcendentals=0
        ),
        name="bra_transform",
    )(me, *numbers, *ket_numbers, *parts, own, other)


def table_shape(parts, orbitals):
    if len(parts) == 1:
        return (1, 1, 1, orbitals, parts[0].shape[-1])
    return (2, 4, 2, orbitals, parts[0].shape[-1])


def last_kernel(own, other, ket, out, tiles, results, sems):
    count, orbitals = ket.shape[1:3]
    group = tiles.shape[1] // orbitals
    half_rounded = jnp.concatenate([own[...], other[...]], axis=1)
    copies = []
    for t in range(orbitals // group):
        tile = tiles.at[t % 2]
        for n in range(count):
            last = ket[1, n]
            for r in range(group):
                row = jnp.broadcast_to(ket[0, n, t * group + r : t * group + r + 1, :], last.shape)
                tile[r * orbitals : (r + 1) * orbitals, n * LANES : (n + 1) * LANES] = (
                    row * last
                ).astype(BF)
        results[t] = lax.dot_general(
            half_rounded, tile[...], (((1,), (1,)), ((), ())), preferred_element_type=F32
        )
        columns = group * orbitals
        copies.append(
            pltpu.make_async_copy(
                results.at[t], out.at[:, pl.ds(t * columns, columns)], sems.at[t]
            )
        )
        copies[-1].start()
    for copy in copies:
        copy.wait()


def last_step(own, other, ket):
    rows, kh = own.shape
    orbitals = ket.shape[2]
    group = 8
    count = orbitals // group
    vmem = pl.BlockSpec(memory_space=pltpu.VMEM)
    return pl.pallas_call(
        last_kernel,
        out_shape=jax.ShapeDtypeStruct((rows, orbitals * orbitals), F32),
        in_specs=[vmem] * 3,
        out_specs=pl.BlockSpec(memory_space=pltpu.HBM),
        scratch_shapes=[
            pltpu.VMEM((2, group * orbitals, 2 * kh), BF),
            pltpu.VMEM((count, rows, group * orbitals), F32),
            pltpu.SemaphoreType.DMA((count,)),
        ],
        compiler_params=pltpu.CompilerParams(vmem_limit_bytes=16 * 2**20),
        name="last_step",
    )(own, other, ket)


def permute(array, mask, count):
    return lax.ppermute(array, "pan", [(i, i ^ mask) for i in range(count)])


def added(*arrays):
    result = arrays[0].astype(F32)
    for array in arrays[1:]:
        result = result + array.astype(F32)
    return result.astype(BF)


def gather_small(mine, nothing, count):
    middle = mine.shape[0] // 2
    a, b = mine[:middle], mine[middle:]
    b_x = permute(b, 2, count)
    a_z = {s: permute(a, 4 * s, count) for s in (3, 2, 1)}
    b_pair = jnp.stack([b, b_x])
    b_z = {s: permute(b_pair, 4 * s, count) for s in (3, 2, 1)}
    near = jnp.stack([a, a_z[1], a_z[2], a_z[3]]) + nothing
    far = permute(near, 2, count)
    rest = jnp.stack([b_pair, b_z[1], b_z[2], b_z[3]])
    upper, lower = pl.ds(0, middle), pl.ds(middle, middle)
    everything = slice(None)
    parts, regions = [], []
    for x, part in ((0, near), (1, far)):
        for core in range(2):
            parts.append(permute(part, 1, count) if core else part)
            regions.append((core, everything, x, upper))
    for core in range(2):
        parts.append(permute(rest, 1, count) if core else rest)
        regions.append((core, everything, everything, lower))
    return parts, regions


def shards(
    count, blocks, first_block, second_block, slot_counts, ket_first, ket_second, coefficients, mo_index
):
    me = lax.axis_index("pan").astype(jnp.int32)
    core = me % 2
    me_array = me.reshape(1)
    capacity, kp, pair = blocks.shape
    kh = kp // 2
    own_ao, nmo = coefficients.shape
    swap = functools.partial(permute, mask=1, count=count)

    numbers = jnp.concatenate([first_block, second_block, slot_counts])
    other_numbers = swap(numbers)
    picks = (mo_index[:, None] == jnp.arange(nmo, dtype=jnp.int32)[None, :]).astype(BF)
    mine = lax.dot_general(
        picks, coefficients, (((1,), (1,)), ((), ())), preferred_element_type=F32
    ).astype(BF)
    orbitals = mine.shape[0]

    units = own_ao // 8
    factor = -(-(2**20) // max(units, 1))
    other = swap(blocks)

    small = count == 16 and own_ao % 16 == 0
    if small:
        nothing = (other_numbers[0] < 0).astype(BF)
        mine = jnp.pad(mine, ((0, 0), (0, -own_ao % LANES)))
        parts, regions = gather_small(mine, nothing, count)

        def locate(unit, me):
            owner = (unit * factor) >> 20
            away = owner ^ me
            return away & 1, away >> 2, (away >> 1) & 1, (unit - owner * units) * 8
    else:
        parts = [lax.all_gather(mine, "pan", axis=1, tiled=True)]
        regions = [(0, 0, 0)]

        def locate(unit, me):
            return 0, 0, 0, unit * 8

    bra = functools.partial(
        bra_transform,
        regions,
        locate,
        parts,
        blocks,
        other,
        (numbers, other_numbers),
        (ket_first, ket_second),
        me_array,
        orbitals,
    )

    if small:
        chunk, side = orbitals // 8, kh // 2
        order = ((3, 0, side), (2, 0, side), (3, side, kh), (2, side, kh), (1, 0, kh), (0, 0, kh))
        pieces = order + tuple((s + 4, a, b) for s, a, b in order)
        *partial, ket = bra(chunk, pieces, BF)
        there, here = partial[:6], partial[6:]
        one = permute(here[4], 4, count)
        three_a = added(here[0], permute(there[0], 2, count))
        two_a = added(here[1], permute(there[1], 2, count), permute(three_a, 4, count))
        three_b = added(here[2], permute(there[2], 2, count))
        two_b = added(here[3], permute(there[3], 2, count), permute(three_b, 4, count))
        nothing = (three_a[0, 0] != three_a[0, 0]).astype(BF)
        other_one = permute(there[4] + nothing, 4, count)
        zero = permute(added(there[5], other_one), 2, count)
        two = jnp.concatenate([permute(two_a, 8, count), permute(two_b, 8, count)], axis=1)
        done = added(here[5], zero, one, two)
    else:
        partial, ket = bra(orbitals, ((0, 0, kh),), F32)
        sides = [list(range(c, count, 2)) for c in range(2)]
        done = lax.psum_scatter(
            partial, "pan", scatter_dimension=0, tiled=True, axis_index_groups=sides
        ).astype(BF)
    rows = done.shape[0] // 2
    keep = lax.dynamic_slice_in_dim(done, core * rows, rows, axis=0)
    give = lax.dynamic_slice_in_dim(done, (1 - core) * rows, rows, axis=0)
    return last_step(keep, swap(give), ket)


def solution(mesh):
    placed = (
        P(("grp", "pan"), None, None),
        P(("grp", "pan")),
        P(("grp", "pan")),
        P(("grp", "pan")),
        P("grp"),
        P("grp"),
        P(("grp", "pan"), None),
        P("grp"),
    )
    return jax.shard_map(
        functools.partial(shards, mesh.shape["pan"]),
        mesh=mesh,
        in_specs=placed,
        out_specs=P(("grp", "pan"), None),
        check_vma=False,
    )
```

profile of v0, /device:TPU:0, one launch (start us, length us, event | category | flops | bytes accessed | tf_op | source)
XLA Modules:
  0.0 81.4 jit_solution(792711905481051278)
XLA Ops:
  0.5 1.3 %copy-done = bf16[752,2000]{0,1:T(8,128)(2,1)S(1)} copy-done((bf16[752,2000]{0,1:T(8,128)(2,1)S(1)}, bf16[752,2000]{0,1:T(8,128)(2,1)}, u32[]{:S(2)}) %copy-start) | copy-done | bytes 3008024
  1.9 1.3 %convolution_convert_fusion = bf16[64,752]{1,0:T(8,128)(2,1)S(1)} fusion(bf16[752,2000]{0,1:T(8,128)(2,1)S(1)} %copy-done, s32[64]{0:T(128)} %param.15), kind=kOutput, calls=%fused_computation | convolution fusion | flops 192688128 | bytes 3104512 | tf_op jit(solution)/shard_map/dot_general | solution.py:322
  3.2 3.0 %collective-permute-start.7 = (bf16[32,768]{1,0:T(8,128)(2,1)S(1)}, bf16[32,768]{1,0:T(8,128)(2,1)S(1)}, u32[]{:S(2)}, u32[]{:S(2)}) collective-permute-start(bf16[32,768]{1,0:T(8,128)(2,1)S(1)} %get-tuple-element.37), channel_id=1, source_target_pairs={{0,2},{1,3},{2,0},{3,1},{4,6},{5,7},{6,4},{7,5},{8,10},{9,11},{10,... | collective-permute-start | bytes 147464 | tf_op jit(solution)/shard_map/ppermute | solution.py:275
  7.0 1.6 %collective-permute-start.1 = (bf16[32,768]{1,0:T(8,128)(2,1)S(1)}, bf16[32,768]{1,0:T(8,128)(2,1)S(1)}, u32[]{:S(2)}, u32[]{:S(2)}) collective-permute-start(bf16[32,768]{1,0:T(8,128)(2,1)S(1)} %get-tuple-element.38), channel_id=1, source_target_pairs={{0,4},{1,5},{2,6},{3,7},{4,0},{5,1},{6,2},{7,3},{8,12},{9,13},{10,... | collective-permute-start | bytes 147464 | tf_op jit(solution)/shard_map/ppermute | solution.py:275
  8.7 2.6 %collective-permute-start.2 = (bf16[32,768]{1,0:T(8,128)(2,1)S(1)}, bf16[32,768]{1,0:T(8,128)(2,1)S(1)}, u32[]{:S(2)}, u32[]{:S(2)}) collective-permute-start(bf16[32,768]{1,0:T(8,128)(2,1)S(1)} %get-tuple-element.38), channel_id=1, source_target_pairs={{0,8},{1,9},{2,10},{3,11},{4,12},{5,13},{6,14},{7,15},{8,0},{9,1},... | collective-permute-start | bytes 147464 | tf_op jit(solution)/shard_map/ppermute | solution.py:275
  11.3 2.5 %collective-permute-start.3 = (bf16[32,768]{1,0:T(8,128)(2,1)S(1)}, bf16[32,768]{1,0:T(8,128)(2,1)S(1)}, u32[]{:S(2)}, u32[]{:S(2)}) collective-permute-start(bf16[32,768]{1,0:T(8,128)(2,1)S(1)} %get-tuple-element.38), channel_id=1, source_target_pairs={{0,12},{1,13},{2,14},{3,15},{4,8},{5,9},{6,10},{7,11},{8,4},{9,5},... | collective-permute-start | bytes 147464 | tf_op jit(solution)/shard_map/ppermute | solution.py:275
  13.9 1.9 %collective-permute-start.10 = (bf16[2,32,768]{2,1,0:T(8,128)(2,1)S(1)}, bf16[2,32,768]{2,1,0:T(8,128)(2,1)S(1)}, u32[]{:S(2)}, u32[]{:S(2)}) collective-permute-start(bf16[2,32,768]{2,1,0:T(8,128)(2,1)S(1)} %get-tuple-element.34), channel_id=1, source_target_pairs={{0,12},{1,13},{2,14},{3,15},{4,8},{5,9},{6,10},{7,11},{8,4},{9,5},... | collective-permute-start | bytes 294920 | tf_op jit(solution)/shard_map/ppermute | solution.py:275
  15.8 1.6 %collective-permute-start.8 = (bf16[2,32,768]{2,1,0:T(8,128)(2,1)S(1)}, bf16[2,32,768]{2,1,0:T(8,128)(2,1)S(1)}, u32[]{:S(2)}, u32[]{:S(2)}) collective-permute-start(bf16[2,32,768]{2,1,0:T(8,128)(2,1)S(1)} %get-tuple-element.34), channel_id=1, source_target_pairs={{0,4},{1,5},{2,6},{3,7},{4,0},{5,1},{6,2},{7,3},{8,12},{9,13},{10,... | collective-permute-start | bytes 294920 | tf_op jit(solution)/shard_map/ppermute | solution.py:275
  19.6 3.6 %collective-permute-done.9 = bf16[2,32,768]{2,1,0:T(8,128)(2,1)S(1)} collective-permute-done((bf16[2,32,768]{2,1,0:T(8,128)(2,1)S(1)}, bf16[2,32,768]{2,1,0:T(8,128)(2,1)S(1)}, u32[]{:S(2)}, u32[]{:S(2)}) %collective-permute-start.9) | collective-permute-done | bytes 98336 | tf_op jit(solution)/shard_map/ppermute | solution.py:275
  24.8 1.8 %collective-permute-done.4.refs_1_ = bf16[4,32,768]{2,1,0:T(8,128)(2,1)} collective-permute-done((bf16[4,32,768]{2,1,0:T(8,128)(2,1)}, bf16[4,32,768]{2,1,0:T(8,128)(2,1)}, u32[]{:S(2)}, u32[]{:S(2)}) %collective-permute-start.4) | collective-permute-done | bytes 196640 | tf_op jit(solution)/shard_map/ppermute | solution.py:275
  26.9 12.8 %bra_transform.1 = (bf16[512,128]{1,0:T(8,128)(2,1)}, bf16[512,128]{1,0:T(8,128)(2,1)}, bf16[512,128]{1,0:T(8,128)(2,1)}, bf16[512,128]{1,0:T(8,128)(2,1)}, bf16...) custom-call(s32[1]{0:T(128)} %bitcast.me_ref, ...), custom_call_target="tpu_custom_call" | custom-call | flops 2684354560 | bytes 8388608 | tf_op jit(solution)/shard_map/bra_transform/pallas_call | solution.py:189
  39.8 2.0 %collective-permute-start.17 = (bf16[512,128]{1,0:T(8,128)(2,1)}, bf16[512,128]{1,0:T(8,128)(2,1)S(1)}, u32[]{:S(2)}, u32[]{:S(2)}) collective-permute-start(bf16[512,128]{1,0:T(8,128)(2,1)} %get-tuple-element.25), channel_id=1, source_target_pairs={{0,2},{1,3},{2,0},{3,1},{4,6},{5,7},{6,4},{7,5},{8,10},{9,11},{10,... | collective-permute-start | bytes 393224 | tf_op jit(solution)/shard_map/ppermute | solution.py:275
  41.9 1.9 %collective-permute-start.20 = (bf16[512,128]{1,0:T(8,128)(2,1)}, bf16[512,128]{1,0:T(8,128)(2,1)S(1)}, u32[]{:S(2)}, u32[]{:S(2)}) collective-permute-start(bf16[512,128]{1,0:T(8,128)(2,1)} %get-tuple-element.27), channel_id=1, source_target_pairs={{0,2},{1,3},{2,0},{3,1},{4,6},{5,7},{6,4},{7,5},{8,10},{9,11},{10,... | collective-permute-start | bytes 393224 | tf_op jit(solution)/shard_map/ppermute | solution.py:275
  43.9 1.8 %collective-permute-start.16 = (bf16[512,256]{1,0:T(8,128)(2,1)}, bf16[512,256]{1,0:T(8,128)(2,1)}, u32[]{:S(2)}, u32[]{:S(2)}) collective-permute-start(bf16[512,256]{1,0:T(8,128)(2,1)} %get-tuple-element.23), channel_id=1, source_target_pairs={{0,4},{1,5},{2,6},{3,7},{4,0},{5,1},{6,2},{7,3},{8,12},{9,13},{10,... | collective-permute-start | bytes 786440 | tf_op jit(solution)/shard_map/ppermute | solution.py:275
  47.3 1.8 %collective-permute-start.18 = (bf16[512,128]{1,0:T(8,128)(2,1)S(1)}, bf16[512,128]{1,0:T(8,128)(2,1)S(1)}, u32[]{:S(2)}, u32[]{:S(2)}) collective-permute-start(bf16[512,128]{1,0:T(8,128)(2,1)S(1)} %add_convert_fusion.5), channel_id=1, source_target_pairs={{0,4},{1,5},{2,6},{3,7},{4,0},{5,1},{6,2},{7,3},{8,12},{9,13},{10,... | collective-permute-start | bytes 393224 | tf_op jit(solution)/shard_map/ppermute | solution.py:275
  52.0 1.8 %collective-permute-start.14 = (bf16[512,256]{1,0:T(8,128)(2,1)S(1)}, bf16[512,256]{1,0:T(8,128)(2,1)S(1)}, u32[]{:S(2)}, u32[]{:S(2)}) collective-permute-start(bf16[512,256]{1,0:T(8,128)(2,1)S(1)} %broadcast_add_fusion), channel_id=1, source_target_pairs={{0,4},{1,5},{2,6},{3,7},{4,0},{5,1},{6,2},{7,3},{8,12},{9,13},{10,... | collective-permute-start | bytes 786440 | tf_op jit(solution)/shard_map/ppermute | solution.py:275
  55.1 1.6 %add_convert_fusion.4 = bf16[512,128]{1,0:T(8,128)(2,1)} fusion(bf16[512,128]{1,0:T(8,128)(2,1)S(1)} %collective-permute-done.18, bf16[512,128]{1,0:T(8,128)(2,1)S(1)} %collective-permute-done.17, bf16[512,128]{1,0:T(8,128)(2,1)} %get-tuple-element.24), kind=kLoop, calls=%fused_computation.7 | loop fusion | flops 393216 | bytes 524288 | tf_op jit(solution)/shard_map/convert_element_type | solution.py:282
  56.7 3.7 %collective-permute-start.19 = (bf16[512,128]{1,0:T(8,128)(2,1)}, bf16[512,128]{1,0:T(8,128)(2,1)S(1)}, u32[]{:S(2)}, u32[]{:S(2)}) collective-permute-start(bf16[512,128]{1,0:T(8,128)(2,1)} %add_convert_fusion.4), channel_id=1, source_target_pairs={{0,8},{1,9},{2,10},{3,11},{4,12},{5,13},{6,14},{7,15},{8,0},{9,1},... | collective-permute-start | bytes 393224 | tf_op jit(solution)/shard_map/ppermute | solution.py:275
  60.5 3.6 %collective-permute-done.14 = bf16[512,256]{1,0:T(8,128)(2,1)S(1)} collective-permute-done((bf16[512,256]{1,0:T(8,128)(2,1)S(1)}, bf16[512,256]{1,0:T(8,128)(2,1)S(1)}, u32[]{:S(2)}, u32[]{:S(2)}) %collective-permute-start.14) | collective-permute-done | bytes 262176 | tf_op jit(solution)/shard_map/ppermute | solution.py:275
  64.0 1.7 %add_convert_fusion.1 = bf16[512,256]{1,0:T(8,128)(2,1)} fusion(bf16[512,256]{1,0:T(8,128)(2,1)S(1)} %collective-permute-done.14, bf16[512,256]{1,0:T(8,128)(2,1)} %get-tuple-element.19), kind=kLoop, calls=%fused_computation.2 | loop fusion | flops 524288 | bytes 786432 | tf_op jit(solution)/shard_map/convert_element_type | solution.py:282
  65.8 1.8 %collective-permute-start.15 = (bf16[512,256]{1,0:T(8,128)(2,1)}, bf16[512,256]{1,0:T(8,128)(2,1)}, u32[]{:S(2)}, u32[]{:S(2)}) collective-permute-start(bf16[512,256]{1,0:T(8,128)(2,1)} %add_convert_fusion.1), channel_id=1, source_target_pairs={{0,2},{1,3},{2,0},{3,1},{4,6},{5,7},{6,4},{7,5},{8,10},{9,11},{10,... | collective-permute-start | bytes 786440 | tf_op jit(solution)/shard_map/ppermute | solution.py:275
  67.6 1.6 %add_convert_fusion.2 = bf16[512,128]{1,0:T(8,128)(2,1)} fusion(bf16[512,128]{1,0:T(8,128)(2,1)S(1)} %collective-permute-done.22, bf16[512,128]{1,0:T(8,128)(2,1)S(1)} %collective-permute-done.20, bf16[512,128]{1,0:T(8,128)(2,1)} %get-tuple-element.26), kind=kLoop, calls=%fused_computation.5 | loop fusion | flops 393216 | bytes 524288 | tf_op jit(solution)/shard_map/convert_element_type | solution.py:282
  69.4 6.4 %collective-permute-done.23 = bf16[512,128]{1,0:T(8,128)(2,1)} collective-permute-done((bf16[512,128]{1,0:T(8,128)(2,1)}, bf16[512,128]{1,0:T(8,128)(2,1)}, u32[]{:S(2)}, u32[]{:S(2)}) %collective-permute-start.23) | collective-permute-done | bytes 131104 | tf_op jit(solution)/shard_map/ppermute | solution.py:275
  78.5 2.8 %last_step.1 = f32[256,4096]{1,0:T(8,128)} custom-call(bf16[256,256]{1,0:T(8,128)(2,1)S(1)} %get-tuple-element.32.own, bf16[256,256]{1,0:T(8,128)(2,1)S(1)} %collective-permute-done.24.other, f32[2,4,64,128]{3,2,1,0:T(8,128)S(1)} %copy-done.1), custom_call_target="tpu_custom_call" | custom-call | tf_op jit(solution)/shard_map/last_step/pallas_call | solution.py:259
  (57 shorter events, 12.4 us)
Async XLA Ops:
  0.0 26.9 %collective-permute-start.12 = (bf16[40,512,128]{2,1,0:T(8,128)(2,1)}, bf16[40,512,128]{2,1,0:T(8,128)(2,1)}, u32[]{:S(2)}, u32[]{:S(2)}) collective-permute-start(bf16[40,512,128]{2,1,0:T(8,128)(2,1)} %refs_6_.1), channel_id=1, source_target_pairs={{0,1},{1,0},{2,3},{3,2},{4,5},{5,4},{6,7},{7,6},{8,9},{9,8},{10,11... | collective-permute-start | bytes 15728648 | tf_op jit(solution)/shard_map/ppermute | solution.py:275
  3.2 10.6 %collective-permute-start.7 = (bf16[32,768]{1,0:T(8,128)(2,1)S(1)}, bf16[32,768]{1,0:T(8,128)(2,1)S(1)}, u32[]{:S(2)}, u32[]{:S(2)}) collective-permute-start(bf16[32,768]{1,0:T(8,128)(2,1)S(1)} %get-tuple-element.37), channel_id=1, source_target_pairs={{0,2},{1,3},{2,0},{3,1},{4,6},{5,7},{6,4},{7,5},{8,10},{9,11},{10,... | collective-permute-start | bytes 147464 | tf_op jit(solution)/shard_map/ppermute | solution.py:275
  7.0 4.3 %collective-permute-start = (s32[81]{0:T(128)S(1)}, s32[81]{0:T(128)S(1)}, u32[]{:S(2)}, u32[]{:S(2)}) collective-permute-start(s32[81]{0:T(128)S(1)} %pad_add_fusion.mine), channel_id=1, source_target_pairs={{0,1},{1,0},{2,3},{3,2},{4,5},{5,4},{6,7},{7,6},{8,9},{9,8},{10,11... | collective-permute-start | bytes 980 | tf_op jit(solution)/shard_map/ppermute | solution.py:275
  7.0 6.9 %collective-permute-start.1 = (bf16[32,768]{1,0:T(8,128)(2,1)S(1)}, bf16[32,768]{1,0:T(8,128)(2,1)S(1)}, u32[]{:S(2)}, u32[]{:S(2)}) collective-permute-start(bf16[32,768]{1,0:T(8,128)(2,1)S(1)} %get-tuple-element.38), channel_id=1, source_target_pairs={{0,4},{1,5},{2,6},{3,7},{4,0},{5,1},{6,2},{7,3},{8,12},{9,13},{10,... | collective-permute-start | bytes 147464 | tf_op jit(solution)/shard_map/ppermute | solution.py:275
  8.7 7.2 %collective-permute-start.2 = (bf16[32,768]{1,0:T(8,128)(2,1)S(1)}, bf16[32,768]{1,0:T(8,128)(2,1)S(1)}, u32[]{:S(2)}, u32[]{:S(2)}) collective-permute-start(bf16[32,768]{1,0:T(8,128)(2,1)S(1)} %get-tuple-element.38), channel_id=1, source_target_pairs={{0,8},{1,9},{2,10},{3,11},{4,12},{5,13},{6,14},{7,15},{8,0},{9,1},... | collective-permute-start | bytes 147464 | tf_op jit(solution)/shard_map/ppermute | solution.py:275
  11.3 6.3 %collective-permute-start.3 = (bf16[32,768]{1,0:T(8,128)(2,1)S(1)}, bf16[32,768]{1,0:T(8,128)(2,1)S(1)}, u32[]{:S(2)}, u32[]{:S(2)}) collective-permute-start(bf16[32,768]{1,0:T(8,128)(2,1)S(1)} %get-tuple-element.38), channel_id=1, source_target_pairs={{0,12},{1,13},{2,14},{3,15},{4,8},{5,9},{6,10},{7,11},{8,4},{9,5},... | collective-permute-start | bytes 147464 | tf_op jit(solution)/shard_map/ppermute | solution.py:275
  13.8 9.4 %collective-permute-start.9 = (bf16[2,32,768]{2,1,0:T(8,128)(2,1)S(1)}, bf16[2,32,768]{2,1,0:T(8,128)(2,1)S(1)}, u32[]{:S(2)}, u32[]{:S(2)}) collective-permute-start(bf16[2,32,768]{2,1,0:T(8,128)(2,1)S(1)} %get-tuple-element.34), channel_id=1, source_target_pairs={{0,8},{1,9},{2,10},{3,11},{4,12},{5,13},{6,14},{7,15},{8,0},{9,1},... | collective-permute-start | bytes 294920 | tf_op jit(solution)/shard_map/ppermute | solution.py:275
  13.9 9.3 %collective-permute-start.10 = (bf16[2,32,768]{2,1,0:T(8,128)(2,1)S(1)}, bf16[2,32,768]{2,1,0:T(8,128)(2,1)S(1)}, u32[]{:S(2)}, u32[]{:S(2)}) collective-permute-start(bf16[2,32,768]{2,1,0:T(8,128)(2,1)S(1)} %get-tuple-element.34), channel_id=1, source_target_pairs={{0,12},{1,13},{2,14},{3,15},{4,8},{5,9},{6,10},{7,11},{8,4},{9,5},... | collective-permute-start | bytes 294920 | tf_op jit(solution)/shard_map/ppermute | solution.py:275
  15.8 8.3 %collective-permute-start.8 = (bf16[2,32,768]{2,1,0:T(8,128)(2,1)S(1)}, bf16[2,32,768]{2,1,0:T(8,128)(2,1)S(1)}, u32[]{:S(2)}, u32[]{:S(2)}) collective-permute-start(bf16[2,32,768]{2,1,0:T(8,128)(2,1)S(1)} %get-tuple-element.34), channel_id=1, source_target_pairs={{0,4},{1,5},{2,6},{3,7},{4,0},{5,1},{6,2},{7,3},{8,12},{9,13},{10,... | collective-permute-start | bytes 294920 | tf_op jit(solution)/shard_map/ppermute | solution.py:275
  18.3 6.4 %collective-permute-start.5 = (bf16[4,32,768]{2,1,0:T(8,128)(2,1)}, bf16[4,32,768]{2,1,0:T(8,128)(2,1)}, u32[]{:S(2)}, u32[]{:S(2)}) collective-permute-start(bf16[4,32,768]{2,1,0:T(8,128)(2,1)} %maximum_add_fusion.refs_0_), channel_id=1, source_target_pairs={{0,2},{1,3},{2,0},{3,1},{4,6},{5,7},{6,4},{7,5},{8,10},{9,11},{10,... | collective-permute-start | bytes 589832 | tf_op jit(solution)/shard_map/ppermute | solution.py:275
  24.2 2.7 %collective-permute-start.11 = (bf16[4,2,32,768]{3,2,1,0:T(8,128)(2,1)S(1)}, bf16[4,2,32,768]{3,2,1,0:T(8,128)(2,1)}, u32[]{:S(2)}, u32[]{:S(2)}) collective-permute-start(bf16[4,2,32,768]{3,2,1,0:T(8,128)(2,1)S(1)} %pad_maximum_fusion.refs_4_), channel_id=1, source_target_pairs={{0,1},{1,0},{2,3},{3,2},{4,5},{5,4},{6,7},{7,6},{8,9},{9,8},{10,11... | collective-permute-start | bytes 1179656 | tf_op jit(solution)/shard_map/ppermute | solution.py:275
  24.2 2.3 %collective-permute-start.4 = (bf16[4,32,768]{2,1,0:T(8,128)(2,1)}, bf16[4,32,768]{2,1,0:T(8,128)(2,1)}, u32[]{:S(2)}, u32[]{:S(2)}) collective-permute-start(bf16[4,32,768]{2,1,0:T(8,128)(2,1)} %maximum_add_fusion.refs_0_), channel_id=1, source_target_pairs={{0,1},{1,0},{2,3},{3,2},{4,5},{5,4},{6,7},{7,6},{8,9},{9,8},{10,11... | collective-permute-start | bytes 589832 | tf_op jit(solution)/shard_map/ppermute | solution.py:275
  24.7 2.1 %collective-permute-start.6 = (bf16[4,32,768]{2,1,0:T(8,128)(2,1)}, bf16[4,32,768]{2,1,0:T(8,128)(2,1)}, u32[]{:S(2)}, u32[]{:S(2)}) collective-permute-start(bf16[4,32,768]{2,1,0:T(8,128)(2,1)} %collective-permute-done.5.refs_2_), channel_id=1, source_target_pairs={{0,1},{1,0},{2,3},{3,2},{4,5},{5,4},{6,7},{7,6},{8,9},{9,8},{10,11... | collective-permute-start | bytes 589832 | tf_op jit(solution)/shard_map/ppermute | solution.py:275
  39.7 6.6 %collective-permute-start.13 = (bf16[512,128]{1,0:T(8,128)(2,1)}, bf16[512,128]{1,0:T(8,128)(2,1)S(1)}, u32[]{:S(2)}, u32[]{:S(2)}) collective-permute-start(bf16[512,128]{1,0:T(8,128)(2,1)} %get-tuple-element.22), channel_id=1, source_target_pairs={{0,2},{1,3},{2,0},{3,1},{4,6},{5,7},{6,4},{7,5},{8,10},{9,11},{10,... | collective-permute-start | bytes 393224 | tf_op jit(solution)/shard_map/ppermute | solution.py:275
  39.8 14.9 %collective-permute-start.17 = (bf16[512,128]{1,0:T(8,128)(2,1)}, bf16[512,128]{1,0:T(8,128)(2,1)S(1)}, u32[]{:S(2)}, u32[]{:S(2)}) collective-permute-start(bf16[512,128]{1,0:T(8,128)(2,1)} %get-tuple-element.25), channel_id=1, source_target_pairs={{0,2},{1,3},{2,0},{3,1},{4,6},{5,7},{6,4},{7,5},{8,10},{9,11},{10,... | collective-permute-start | bytes 393224 | tf_op jit(solution)/shard_map/ppermute | solution.py:275
  41.8 10.1 %collective-permute-start.21 = (bf16[512,128]{1,0:T(8,128)(2,1)}, bf16[512,128]{1,0:T(8,128)(2,1)S(1)}, u32[]{:S(2)}, u32[]{:S(2)}) collective-permute-start(bf16[512,128]{1,0:T(8,128)(2,1)} %get-tuple-element.29), channel_id=1, source_target_pairs={{0,2},{1,3},{2,0},{3,1},{4,6},{5,7},{6,4},{7,5},{8,10},{9,11},{10,... | collective-permute-start | bytes 393224 | tf_op jit(solution)/shard_map/ppermute | solution.py:275
  41.9 25.7 %collective-permute-start.20 = (bf16[512,128]{1,0:T(8,128)(2,1)}, bf16[512,128]{1,0:T(8,128)(2,1)S(1)}, u32[]{:S(2)}, u32[]{:S(2)}) collective-permute-start(bf16[512,128]{1,0:T(8,128)(2,1)} %get-tuple-element.27), channel_id=1, source_target_pairs={{0,2},{1,3},{2,0},{3,1},{4,6},{5,7},{6,4},{7,5},{8,10},{9,11},{10,... | collective-permute-start | bytes 393224 | tf_op jit(solution)/shard_map/ppermute | solution.py:275
  43.9 25.5 %collective-permute-start.16 = (bf16[512,256]{1,0:T(8,128)(2,1)}, bf16[512,256]{1,0:T(8,128)(2,1)}, u32[]{:S(2)}, u32[]{:S(2)}) collective-permute-start(bf16[512,256]{1,0:T(8,128)(2,1)} %get-tuple-element.23), channel_id=1, source_target_pairs={{0,4},{1,5},{2,6},{3,7},{4,0},{5,1},{6,2},{7,3},{8,12},{9,13},{10,... | collective-permute-start | bytes 786440 | tf_op jit(solution)/shard_map/ppermute | solution.py:275
  47.3 7.8 %collective-permute-start.18 = (bf16[512,128]{1,0:T(8,128)(2,1)S(1)}, bf16[512,128]{1,0:T(8,128)(2,1)S(1)}, u32[]{:S(2)}, u32[]{:S(2)}) collective-permute-start(bf16[512,128]{1,0:T(8,128)(2,1)S(1)} %add_convert_fusion.5), channel_id=1, source_target_pairs={{0,4},{1,5},{2,6},{3,7},{4,0},{5,1},{6,2},{7,3},{8,12},{9,13},{10,... | collective-permute-start | bytes 393224 | tf_op jit(solution)/shard_map/ppermute | solution.py:275
  52.0 12.1 %collective-permute-start.14 = (bf16[512,256]{1,0:T(8,128)(2,1)S(1)}, bf16[512,256]{1,0:T(8,128)(2,1)S(1)}, u32[]{:S(2)}, u32[]{:S(2)}) collective-permute-start(bf16[512,256]{1,0:T(8,128)(2,1)S(1)} %broadcast_add_fusion), channel_id=1, source_target_pairs={{0,4},{1,5},{2,6},{3,7},{4,0},{5,1},{6,2},{7,3},{8,12},{9,13},{10,... | collective-permute-start | bytes 786440 | tf_op jit(solution)/shard_map/ppermute | solution.py:275
  54.7 12.9 %collective-permute-start.22 = (bf16[512,128]{1,0:T(8,128)(2,1)S(1)}, bf16[512,128]{1,0:T(8,128)(2,1)S(1)}, u32[]{:S(2)}, u32[]{:S(2)}) collective-permute-start(bf16[512,128]{1,0:T(8,128)(2,1)S(1)} %add_convert_fusion.3), channel_id=1, source_target_pairs={{0,4},{1,5},{2,6},{3,7},{4,0},{5,1},{6,2},{7,3},{8,12},{9,13},{10,... | collective-permute-start | bytes 393224 | tf_op jit(solution)/shard_map/ppermute | solution.py:275
  56.7 12.6 %collective-permute-start.19 = (bf16[512,128]{1,0:T(8,128)(2,1)}, bf16[512,128]{1,0:T(8,128)(2,1)S(1)}, u32[]{:S(2)}, u32[]{:S(2)}) collective-permute-start(bf16[512,128]{1,0:T(8,128)(2,1)} %add_convert_fusion.4), channel_id=1, source_target_pairs={{0,8},{1,9},{2,10},{3,11},{4,12},{5,13},{6,14},{7,15},{8,0},{9,1},... | collective-permute-start | bytes 393224 | tf_op jit(solution)/shard_map/ppermute | solution.py:275
  65.8 10.0 %collective-permute-start.15 = (bf16[512,256]{1,0:T(8,128)(2,1)}, bf16[512,256]{1,0:T(8,128)(2,1)}, u32[]{:S(2)}, u32[]{:S(2)}) collective-permute-start(bf16[512,256]{1,0:T(8,128)(2,1)} %add_convert_fusion.1), channel_id=1, source_target_pairs={{0,2},{1,3},{2,0},{3,1},{4,6},{5,7},{6,4},{7,5},{8,10},{9,11},{10,... | collective-permute-start | bytes 786440 | tf_op jit(solution)/shard_map/ppermute | solution.py:275
  69.2 6.6 %collective-permute-start.23 = (bf16[512,128]{1,0:T(8,128)(2,1)}, bf16[512,128]{1,0:T(8,128)(2,1)}, u32[]{:S(2)}, u32[]{:S(2)}) collective-permute-start(bf16[512,128]{1,0:T(8,128)(2,1)} %add_convert_fusion.2), channel_id=1, source_target_pairs={{0,8},{1,9},{2,10},{3,11},{4,12},{5,13},{6,14},{7,15},{8,0},{9,1},... | collective-permute-start | bytes 393224 | tf_op jit(solution)/shard_map/ppermute | solution.py:275
  (8 other events, 94.0 us)
where the time goes:
time: 81.9 us; the launch traced here: 81.4 us
  starting transfers between devices  31.3 us (38%)
  waiting for transfers between devices  19 us (23%)
  Pallas kernels  15.6 us (19%)
  other arithmetic  9.93 us (12%)
  between operations  2.36 us (3%)
  local copies, waits for them, and re-layouts  1.92 us (2%)
  matrix products  1.35 us (2%)
    ppermute x25, starting transfers between devices, permute(): return lax.ppermute(array, 'pan', [(i, i ^ mask) for i in range(count)])  31.3 us
    ppermute x25, waiting for transfers between devices, permute(): return lax.ppermute(array, 'pan', [(i, i ^ mask) for i in range(count)])  19 us
    pallas_call x1, Pallas kernels, bra_transform(): pl.pallas_call(functools.partial(bra_kernel, regions, locate, chunk, piec...  12.8 us
    convert_element_type x6, other arithmetic, added(): return result.astype(BF)  8.12 us
    pallas_call x1, Pallas kernels, last_step(): pl.pallas_call(last_kernel, out_shape=jax.ShapeDtypeStruct((rows, orbital...  2.76 us
  transfers between devices with their start and end apart: 25, of which 11 were waited for; matrix products, arithmetic and copies ran while one was open for 13% of the time, Pallas kernels for 0%

commit v1 on v0

--- a/solution.py
+++ b/solution.py
@@ -12,7 +12,7 @@
 LANES = 128
 BF = jnp.bfloat16
 F32 = jnp.float32
-VMEM_LIMIT = 58 * 2**20
+VMEM_LIMIT = 51 * 2**20
 
 
 def spread(kind):
@@ -364,14 +364,13 @@
         pieces = order + tuple((s + 4, a, b) for s, a, b in order)
         *partial, ket = bra(chunk, pieces, BF)
         there, here = partial[:6], partial[6:]
-        one = permute(here[4], 4, count)
         three_a = added(here[0], permute(there[0], 2, count))
         two_a = added(here[1], permute(there[1], 2, count), permute(three_a, 4, count))
         three_b = added(here[2], permute(there[2], 2, count))
-        two_b = added(here[3], permute(there[3], 2, count), permute(three_b, 4, count))
         nothing = (three_a[0, 0] != three_a[0, 0]).astype(BF)
-        other_one = permute(there[4] + nothing, 4, count)
-        zero = permute(added(there[5], other_one), 2, count)
+        two_b = added(here[3], permute(there[3] + nothing, 2, count), permute(three_b, 4, count))
+        one = permute(added(here[4], permute(there[4], 2, count)), 4, count)
+        zero = permute(there[5] + nothing, 2, count)
         two = jnp.concatenate([permute(two_a, 8, count), permute(two_b, 8, count)], axis=1)
         done = added(here[5], zero, one, two)
     else:

time: 81.9 us -> 80.7 us (0.985); the launches traced: 81.4 us -> 81.9 us
  starting transfers between devices: 31.3 us -> 39 us
  other arithmetic: 9.93 us -> 5.22 us
  Pallas kernels: 15.6 us -> 12.1 us
    ppermute x25, starting transfers between devices: 31.3 us -> 39 us  [permute(): return lax.ppermute(array, 'pan', [(i, i ^ mask) for i in range(count)])]
    convert_element_type x6, other arithmetic: 8.12 us -> 3.55 us  [added(): return result.astype(BF)]
    pallas_call x1, Pallas kernels: 12.8 us -> 9.36 us  [bra_transform(): pl.pallas_call(functools.partial(bra_kernel, regions, locate, chunk, piec...]
  transfers between devices with their start and end apart: 25 -> 25, of which waited for: 11 -> 11; matrix products, arithmetic and copies ran while one was open for 13% -> 7% of each run, Pallas kernels for 0% -> 0%
where the time goes in v1:
time: 80.7 us; the launch traced here: 81.9 us
  starting transfers between devices  39 us (48%)
  waiting for transfers between devices  19.3 us (24%)
  Pallas kernels  12.1 us (15%)
  other arithmetic  5.22 us (6%)
  local copies, waits for them, and re-layouts  2.58 us (3%)
  between operations  2.33 us (3%)
  matrix products  1.35 us (2%)
    ppermute x25, starting transfers between devices, permute(): return lax.ppermute(array, 'pan', [(i, i ^ mask) for i in range(count)])  39 us
    ppermute x25, waiting for transfers between devices, permute(): return lax.ppermute(array, 'pan', [(i, i ^ mask) for i in range(count)])  19.3 us
    pallas_call x1, Pallas kernels, bra_transform(): pl.pallas_call(functools.partial(bra_kernel, regions, locate, chunk, piec...  9.36 us
    convert_element_type x6, other arithmetic, added(): return result.astype(BF)  3.55 us
    pallas_call x1, Pallas kernels, last_step(): pl.pallas_call(last_kernel, out_shape=jax.ShapeDtypeStruct((rows, orbital...  2.77 us
    unnamed x14, local copies, waits for them, and re-layouts  2.03 us
  transfers between devices with their start and end apart: 25, of which 11 were waited for; matrix products, arithmetic and copies ran while one was open for 7% of the time, Pallas kernels for 0%

profile of v1, /device:TPU:0, one launch (start us, length us, event | category | flops | bytes accessed | tf_op | source)
XLA Modules:
  0.0 81.9 jit_solution(8790406104162435511)
XLA Ops:
  1.9 1.3 %convolution_convert_fusion = bf16[64,752]{1,0:T(8,128)(2,1)S(1)} fusion(bf16[752,2000]{0,1:T(8,128)(2,1)S(1)} %copy-done, s32[64]{0:T(128)} %param.15), kind=kOutput, calls=%fused_computation | convolution fusion | flops 192688128 | bytes 3104512 | tf_op jit(solution)/shard_map/dot_general | solution.py:322
  3.2 3.0 %collective-permute-start.7 = (bf16[32,768]{1,0:T(8,128)(2,1)S(1)}, bf16[32,768]{1,0:T(8,128)(2,1)S(1)}, u32[]{:S(2)}, u32[]{:S(2)}) collective-permute-start(bf16[32,768]{1,0:T(8,128)(2,1)S(1)} %get-tuple-element.37), channel_id=1, source_target_pairs={{0,2},{1,3},{2,0},{3,1},{4,6},{5,7},{6,4},{7,5},{8,10},{9,11},{10,... | collective-permute-start | bytes 147464 | tf_op jit(solution)/shard_map/ppermute | solution.py:275
  7.0 1.6 %collective-permute-start.1 = (bf16[32,768]{1,0:T(8,128)(2,1)S(1)}, bf16[32,768]{1,0:T(8,128)(2,1)S(1)}, u32[]{:S(2)}, u32[]{:S(2)}) collective-permute-start(bf16[32,768]{1,0:T(8,128)(2,1)S(1)} %get-tuple-element.38), channel_id=1, source_target_pairs={{0,4},{1,5},{2,6},{3,7},{4,0},{5,1},{6,2},{7,3},{8,12},{9,13},{10,... | collective-permute-start | bytes 147464 | tf_op jit(solution)/shard_map/ppermute | solution.py:275
  8.7 2.6 %collective-permute-start.2 = (bf16[32,768]{1,0:T(8,128)(2,1)S(1)}, bf16[32,768]{1,0:T(8,128)(2,1)S(1)}, u32[]{:S(2)}, u32[]{:S(2)}) collective-permute-start(bf16[32,768]{1,0:T(8,128)(2,1)S(1)} %get-tuple-element.38), channel_id=1, source_target_pairs={{0,8},{1,9},{2,10},{3,11},{4,12},{5,13},{6,14},{7,15},{8,0},{9,1},... | collective-permute-start | bytes 147464 | tf_op jit(solution)/shard_map/ppermute | solution.py:275
  11.2 2.5 %collective-permute-start.3 = (bf16[32,768]{1,0:T(8,128)(2,1)S(1)}, bf16[32,768]{1,0:T(8,128)(2,1)S(1)}, u32[]{:S(2)}, u32[]{:S(2)}) collective-permute-start(bf16[32,768]{1,0:T(8,128)(2,1)S(1)} %get-tuple-element.38), channel_id=1, source_target_pairs={{0,12},{1,13},{2,14},{3,15},{4,8},{5,9},{6,10},{7,11},{8,4},{9,5},... | collective-permute-start | bytes 147464 | tf_op jit(solution)/shard_map/ppermute | solution.py:275
  13.9 1.9 %collective-permute-start.10 = (bf16[2,32,768]{2,1,0:T(8,128)(2,1)S(1)}, bf16[2,32,768]{2,1,0:T(8,128)(2,1)S(1)}, u32[]{:S(2)}, u32[]{:S(2)}) collective-permute-start(bf16[2,32,768]{2,1,0:T(8,128)(2,1)S(1)} %get-tuple-element.34), channel_id=1, source_target_pairs={{0,12},{1,13},{2,14},{3,15},{4,8},{5,9},{6,10},{7,11},{8,4},{9,5},... | collective-permute-start | bytes 294920 | tf_op jit(solution)/shard_map/ppermute | solution.py:275
  15.8 1.6 %collective-permute-start.8 = (bf16[2,32,768]{2,1,0:T(8,128)(2,1)S(1)}, bf16[2,32,768]{2,1,0:T(8,128)(2,1)S(1)}, u32[]{:S(2)}, u32[]{:S(2)}) collective-permute-start(bf16[2,32,768]{2,1,0:T(8,128)(2,1)S(1)} %get-tuple-element.34), channel_id=1, source_target_pairs={{0,4},{1,5},{2,6},{3,7},{4,0},{5,1},{6,2},{7,3},{8,12},{9,13},{10,... | collective-permute-start | bytes 294920 | tf_op jit(solution)/shard_map/ppermute | solution.py:275
  19.0 4.2 %collective-permute-done.9 = bf16[2,32,768]{2,1,0:T(8,128)(2,1)S(1)} collective-permute-done((bf16[2,32,768]{2,1,0:T(8,128)(2,1)S(1)}, bf16[2,32,768]{2,1,0:T(8,128)(2,1)S(1)}, u32[]{:S(2)}, u32[]{:S(2)}) %collective-permute-start.9) | collective-permute-done | bytes 98336 | tf_op jit(solution)/shard_map/ppermute | solution.py:275
  25.4 1.4 %collective-permute-done.4.refs_1_ = bf16[4,32,768]{2,1,0:T(8,128)(2,1)} collective-permute-done((bf16[4,32,768]{2,1,0:T(8,128)(2,1)S(1)}, bf16[4,32,768]{2,1,0:T(8,128)(2,1)}, u32[]{:S(2)}, u32[]{:S(2)}) %collective-permute-start.4) | collective-permute-done | bytes 196640 | tf_op jit(solution)/shard_map/ppermute | solution.py:275
  27.5 9.4 %bra_transform.1 = (bf16[512,128]{1,0:T(8,128)(2,1)S(1)}, bf16[512,128]{1,0:T(8,128)(2,1)S(1)}, bf16[512,128]{1,0:T(8,128)(2,1)S(1)}, bf16[512,128]{1,0:T(8,128)...) custom-call(s32[1]{0:T(128)} %bitcast.me_ref, ...), custom_call_target="tpu_custom_call" | custom-call | flops 2684354560 | bytes 8388608 | tf_op jit(solution)/shard_map/bra_transform/pallas_call | solution.py:189
  37.6 2.0 %collective-permute-start.17 = (bf16[512,128]{1,0:T(8,128)(2,1)S(1)}, bf16[512,128]{1,0:T(8,128)(2,1)S(1)}, u32[]{:S(2)}, u32[]{:S(2)}) collective-permute-start(bf16[512,128]{1,0:T(8,128)(2,1)S(1)} %get-tuple-element.25), channel_id=1, source_target_pairs={{0,2},{1,3},{2,0},{3,1},{4,6},{5,7},{6,4},{7,5},{8,10},{9,11},{10,... | collective-permute-start | bytes 393224 | tf_op jit(solution)/shard_map/ppermute | solution.py:275
  39.7 2.0 %collective-permute-start.15 = (bf16[512,256]{1,0:T(8,128)(2,1)S(1)}, bf16[512,256]{1,0:T(8,128)(2,1)S(1)}, u32[]{:S(2)}, u32[]{:S(2)}) collective-permute-start(bf16[512,256]{1,0:T(8,128)(2,1)S(1)} %get-tuple-element.23), channel_id=1, source_target_pairs={{0,2},{1,3},{2,0},{3,1},{4,6},{5,7},{6,4},{7,5},{8,10},{9,11},{10,... | collective-permute-start | bytes 786440 | tf_op jit(solution)/shard_map/ppermute | solution.py:275
  41.6 2.3 %collective-permute-done.13 = bf16[512,128]{1,0:T(8,128)(2,1)S(1)} collective-permute-done((bf16[512,128]{1,0:T(8,128)(2,1)S(1)}, bf16[512,128]{1,0:T(8,128)(2,1)S(1)}, u32[]{:S(2)}, u32[]{:S(2)}) %collective-permute-start.13) | collective-permute-done | bytes 131104 | tf_op jit(solution)/shard_map/ppermute | solution.py:275
  44.0 5.6 %collective-permute-start.18 = (bf16[512,128]{1,0:T(8,128)(2,1)S(1)}, bf16[512,128]{1,0:T(8,128)(2,1)S(1)}, u32[]{:S(2)}, u32[]{:S(2)}) collective-permute-start(bf16[512,128]{1,0:T(8,128)(2,1)S(1)} %add_convert_fusion.5), channel_id=1, source_target_pairs={{0,4},{1,5},{2,6},{3,7},{4,0},{5,1},{6,2},{7,3},{8,12},{9,13},{10,... | collective-permute-start | bytes 393224 | tf_op jit(solution)/shard_map/ppermute | solution.py:275
  51.4 2.0 %collective-permute-start.20 = (bf16[512,128]{1,0:T(8,128)(2,1)S(1)}, bf16[512,128]{1,0:T(8,128)(2,1)S(1)}, u32[]{:S(2)}, u32[]{:S(2)}) collective-permute-start(bf16[512,128]{1,0:T(8,128)(2,1)S(1)} %broadcast_add_fusion.1), channel_id=1, source_target_pairs={{0,2},{1,3},{2,0},{3,1},{4,6},{5,7},{6,4},{7,5},{8,10},{9,11},{10,... | collective-permute-start | bytes 393224 | tf_op jit(solution)/shard_map/ppermute | solution.py:275
  53.4 1.7 %collective-permute-start.22 = (bf16[512,128]{1,0:T(8,128)(2,1)S(1)}, bf16[512,128]{1,0:T(8,128)(2,1)S(1)}, u32[]{:S(2)}, u32[]{:S(2)}) collective-permute-start(bf16[512,128]{1,0:T(8,128)(2,1)S(1)} %add_convert_fusion.3), channel_id=1, source_target_pairs={{0,4},{1,5},{2,6},{3,7},{4,0},{5,1},{6,2},{7,3},{8,12},{9,13},{10,... | collective-permute-start | bytes 393224 | tf_op jit(solution)/shard_map/ppermute | solution.py:275
  55.9 1.9 %collective-permute-start.14 = (bf16[512,256]{1,0:T(8,128)(2,1)}, bf16[512,256]{1,0:T(8,128)(2,1)}, u32[]{:S(2)}, u32[]{:S(2)}) collective-permute-start(bf16[512,256]{1,0:T(8,128)(2,1)} %broadcast_add_fusion), channel_id=1, source_target_pairs={{0,2},{1,3},{2,0},{3,1},{4,6},{5,7},{6,4},{7,5},{8,10},{9,11},{10,... | collective-permute-start | bytes 786440 | tf_op jit(solution)/shard_map/ppermute | solution.py:275
  58.5 6.1 %collective-permute-start.19 = (bf16[512,128]{1,0:T(8,128)(2,1)}, bf16[512,128]{1,0:T(8,128)(2,1)S(1)}, u32[]{:S(2)}, u32[]{:S(2)}) collective-permute-start(bf16[512,128]{1,0:T(8,128)(2,1)} %add_convert_fusion.4), channel_id=1, source_target_pairs={{0,8},{1,9},{2,10},{3,11},{4,12},{5,13},{6,14},{7,15},{8,0},{9,1},... | collective-permute-start | bytes 393224 | tf_op jit(solution)/shard_map/ppermute | solution.py:275
  66.1 2.0 %collective-permute-start.23 = (bf16[512,128]{1,0:T(8,128)(2,1)}, bf16[512,128]{1,0:T(8,128)(2,1)}, u32[]{:S(2)}, u32[]{:S(2)}) collective-permute-start(bf16[512,128]{1,0:T(8,128)(2,1)} %add_convert_fusion.2), channel_id=1, source_target_pairs={{0,8},{1,9},{2,10},{3,11},{4,12},{5,13},{6,14},{7,15},{8,0},{9,1},... | collective-permute-start | bytes 393224 | tf_op jit(solution)/shard_map/ppermute | solution.py:275
  68.1 2.1 %collective-permute-done.19 = bf16[512,128]{1,0:T(8,128)(2,1)S(1)} collective-permute-done((bf16[512,128]{1,0:T(8,128)(2,1)}, bf16[512,128]{1,0:T(8,128)(2,1)S(1)}, u32[]{:S(2)}, u32[]{:S(2)}) %collective-permute-start.19) | collective-permute-done | bytes 131104 | tf_op jit(solution)/shard_map/ppermute | solution.py:275
  70.2 4.1 %collective-permute-done.23 = bf16[512,128]{1,0:T(8,128)(2,1)} collective-permute-done((bf16[512,128]{1,0:T(8,128)(2,1)}, bf16[512,128]{1,0:T(8,128)(2,1)}, u32[]{:S(2)}, u32[]{:S(2)}) %collective-permute-start.23) | collective-permute-done | bytes 131104 | tf_op jit(solution)/shard_map/ppermute | solution.py:275
  74.3 2.0 %collective-permute-done.16 = bf16[512,256]{1,0:T(8,128)(2,1)} collective-permute-done((bf16[512,256]{1,0:T(8,128)(2,1)}, bf16[512,256]{1,0:T(8,128)(2,1)}, u32[]{:S(2)}, u32[]{:S(2)}) %collective-permute-start.16) | collective-permute-done | bytes 262176 | tf_op jit(solution)/shard_map/ppermute | solution.py:275
  77.6 1.3 %collective-permute-done.24.other = bf16[256,256]{1,0:T(8,128)(2,1)S(1)} collective-permute-done((bf16[256,256]{1,0:T(8,128)(2,1)S(1)}, bf16[256,256]{1,0:T(8,128)(2,1)S(1)}, u32[]{:S(2)}, u32[]{:S(2)}) %collective-permute-start.24) | collective-permute-done | bytes 131104 | tf_op jit(solution)/shard_map/ppermute | solution.py:275
  79.0 2.8 %last_step.1 = f32[256,4096]{1,0:T(8,128)} custom-call(bf16[256,256]{1,0:T(8,128)(2,1)S(1)} %get-tuple-element.32.own, bf16[256,256]{1,0:T(8,128)(2,1)S(1)} %collective-permute-done.24.other, f32[2,4,64,128]{3,2,1,0:T(8,128)S(1)} %copy-done.1), custom_call_target="tpu_custom_call" | custom-call | tf_op jit(solution)/shard_map/last_step/pallas_call | solution.py:259
  (58 shorter events, 12.2 us)
Async XLA Ops:
  0.0 27.5 %collective-permute-start.12 = (bf16[40,512,128]{2,1,0:T(8,128)(2,1)}, bf16[40,512,128]{2,1,0:T(8,128)(2,1)}, u32[]{:S(2)}, u32[]{:S(2)}) collective-permute-start(bf16[40,512,128]{2,1,0:T(8,128)(2,1)} %refs_6_.1), channel_id=1, source_target_pairs={{0,1},{1,0},{2,3},{3,2},{4,5},{5,4},{6,7},{7,6},{8,9},{9,8},{10,11... | collective-permute-start | bytes 15728648 | tf_op jit(solution)/shard_map/ppermute | solution.py:275
  3.2 10.6 %collective-permute-start.7 = (bf16[32,768]{1,0:T(8,128)(2,1)S(1)}, bf16[32,768]{1,0:T(8,128)(2,1)S(1)}, u32[]{:S(2)}, u32[]{:S(2)}) collective-permute-start(bf16[32,768]{1,0:T(8,128)(2,1)S(1)} %get-tuple-element.37), channel_id=1, source_target_pairs={{0,2},{1,3},{2,0},{3,1},{4,6},{5,7},{6,4},{7,5},{8,10},{9,11},{10,... | collective-permute-start | bytes 147464 | tf_op jit(solution)/shard_map/ppermute | solution.py:275
  7.0 4.3 %collective-permute-start = (s32[81]{0:T(128)S(1)}, s32[81]{0:T(128)S(1)}, u32[]{:S(2)}, u32[]{:S(2)}) collective-permute-start(s32[81]{0:T(128)S(1)} %pad_add_fusion.mine), channel_id=1, source_target_pairs={{0,1},{1,0},{2,3},{3,2},{4,5},{5,4},{6,7},{7,6},{8,9},{9,8},{10,11... | collective-permute-start | bytes 980 | tf_op jit(solution)/shard_map/ppermute | solution.py:275
  7.0 6.9 %collective-permute-start.1 = (bf16[32,768]{1,0:T(8,128)(2,1)S(1)}, bf16[32,768]{1,0:T(8,128)(2,1)S(1)}, u32[]{:S(2)}, u32[]{:S(2)}) collective-permute-start(bf16[32,768]{1,0:T(8,128)(2,1)S(1)} %get-tuple-element.38), channel_id=1, source_target_pairs={{0,4},{1,5},{2,6},{3,7},{4,0},{5,1},{6,2},{7,3},{8,12},{9,13},{10,... | collective-permute-start | bytes 147464 | tf_op jit(solution)/shard_map/ppermute | solution.py:275
  8.7 7.2 %collective-permute-start.2 = (bf16[32,768]{1,0:T(8,128)(2,1)S(1)}, bf16[32,768]{1,0:T(8,128)(2,1)S(1)}, u32[]{:S(2)}, u32[]{:S(2)}) collective-permute-start(bf16[32,768]{1,0:T(8,128)(2,1)S(1)} %get-tuple-element.38), channel_id=1, source_target_pairs={{0,8},{1,9},{2,10},{3,11},{4,12},{5,13},{6,14},{7,15},{8,0},{9,1},... | collective-permute-start | bytes 147464 | tf_op jit(solution)/shard_map/ppermute | solution.py:275
  11.2 6.4 %collective-permute-start.3 = (bf16[32,768]{1,0:T(8,128)(2,1)S(1)}, bf16[32,768]{1,0:T(8,128)(2,1)S(1)}, u32[]{:S(2)}, u32[]{:S(2)}) collective-permute-start(bf16[32,768]{1,0:T(8,128)(2,1)S(1)} %get-tuple-element.38), channel_id=1, source_target_pairs={{0,12},{1,13},{2,14},{3,15},{4,8},{5,9},{6,10},{7,11},{8,4},{9,5},... | collective-permute-start | bytes 147464 | tf_op jit(solution)/shard_map/ppermute | solution.py:275
  13.8 9.4 %collective-permute-start.9 = (bf16[2,32,768]{2,1,0:T(8,128)(2,1)S(1)}, bf16[2,32,768]{2,1,0:T(8,128)(2,1)S(1)}, u32[]{:S(2)}, u32[]{:S(2)}) collective-permute-start(bf16[2,32,768]{2,1,0:T(8,128)(2,1)S(1)} %get-tuple-element.34), channel_id=1, source_target_pairs={{0,8},{1,9},{2,10},{3,11},{4,12},{5,13},{6,14},{7,15},{8,0},{9,1},... | collective-permute-start | bytes 294920 | tf_op jit(solution)/shard_map/ppermute | solution.py:275
  13.9 9.3 %collective-permute-start.10 = (bf16[2,32,768]{2,1,0:T(8,128)(2,1)S(1)}, bf16[2,32,768]{2,1,0:T(8,128)(2,1)S(1)}, u32[]{:S(2)}, u32[]{:S(2)}) collective-permute-start(bf16[2,32,768]{2,1,0:T(8,128)(2,1)S(1)} %get-tuple-element.34), channel_id=1, source_target_pairs={{0,12},{1,13},{2,14},{3,15},{4,8},{5,9},{6,10},{7,11},{8,4},{9,5},... | collective-permute-start | bytes 294920 | tf_op jit(solution)/shard_map/ppermute | solution.py:275
  15.8 8.3 %collective-permute-start.8 = (bf16[2,32,768]{2,1,0:T(8,128)(2,1)S(1)}, bf16[2,32,768]{2,1,0:T(8,128)(2,1)S(1)}, u32[]{:S(2)}, u32[]{:S(2)}) collective-permute-start(bf16[2,32,768]{2,1,0:T(8,128)(2,1)S(1)} %get-tuple-element.34), channel_id=1, source_target_pairs={{0,4},{1,5},{2,6},{3,7},{4,0},{5,1},{6,2},{7,3},{8,12},{9,13},{10,... | collective-permute-start | bytes 294920 | tf_op jit(solution)/shard_map/ppermute | solution.py:275
  17.7 7.7 %collective-permute-start.5 = (bf16[4,32,768]{2,1,0:T(8,128)(2,1)S(1)}, bf16[4,32,768]{2,1,0:T(8,128)(2,1)S(1)}, u32[]{:S(2)}, u32[]{:S(2)}) collective-permute-start(bf16[4,32,768]{2,1,0:T(8,128)(2,1)S(1)} %maximum_add_fusion.refs_0_), channel_id=1, source_target_pairs={{0,2},{1,3},{2,0},{3,1},{4,6},{5,7},{6,4},{7,5},{8,10},{9,11},{10,... | collective-permute-start | bytes 589832 | tf_op jit(solution)/shard_map/ppermute | solution.py:275
  24.9 2.6 %collective-permute-start.11 = (bf16[4,2,32,768]{3,2,1,0:T(8,128)(2,1)}, bf16[4,2,32,768]{3,2,1,0:T(8,128)(2,1)}, u32[]{:S(2)}, u32[]{:S(2)}) collective-permute-start(bf16[4,2,32,768]{3,2,1,0:T(8,128)(2,1)} %pad_maximum_fusion.refs_4_), channel_id=1, source_target_pairs={{0,1},{1,0},{2,3},{3,2},{4,5},{5,4},{6,7},{7,6},{8,9},{9,8},{10,11... | collective-permute-start | bytes 1179656 | tf_op jit(solution)/shard_map/ppermute | solution.py:275
  24.9 1.9 %collective-permute-start.4 = (bf16[4,32,768]{2,1,0:T(8,128)(2,1)S(1)}, bf16[4,32,768]{2,1,0:T(8,128)(2,1)}, u32[]{:S(2)}, u32[]{:S(2)}) collective-permute-start(bf16[4,32,768]{2,1,0:T(8,128)(2,1)S(1)} %maximum_add_fusion.refs_0_), channel_id=1, source_target_pairs={{0,1},{1,0},{2,3},{3,2},{4,5},{5,4},{6,7},{7,6},{8,9},{9,8},{10,11... | collective-permute-start | bytes 589832 | tf_op jit(solution)/shard_map/ppermute | solution.py:275
  25.4 1.9 %collective-permute-start.6 = (bf16[4,32,768]{2,1,0:T(8,128)(2,1)S(1)}, bf16[4,32,768]{2,1,0:T(8,128)(2,1)}, u32[]{:S(2)}, u32[]{:S(2)}) collective-permute-start(bf16[4,32,768]{2,1,0:T(8,128)(2,1)S(1)} %collective-permute-done.5.refs_2_), channel_id=1, source_target_pairs={{0,1},{1,0},{2,3},{3,2},{4,5},{5,4},{6,7},{7,6},{8,9},{9,8},{10,11... | collective-permute-start | bytes 589832 | tf_op jit(solution)/shard_map/ppermute | solution.py:275
  37.6 6.3 %collective-permute-start.13 = (bf16[512,128]{1,0:T(8,128)(2,1)S(1)}, bf16[512,128]{1,0:T(8,128)(2,1)S(1)}, u32[]{:S(2)}, u32[]{:S(2)}) collective-permute-start(bf16[512,128]{1,0:T(8,128)(2,1)S(1)} %get-tuple-element.21), channel_id=1, source_target_pairs={{0,2},{1,3},{2,0},{3,1},{4,6},{5,7},{6,4},{7,5},{8,10},{9,11},{10,... | collective-permute-start | bytes 393224 | tf_op jit(solution)/shard_map/ppermute | solution.py:275
  37.6 18.3 %collective-permute-start.17 = (bf16[512,128]{1,0:T(8,128)(2,1)S(1)}, bf16[512,128]{1,0:T(8,128)(2,1)S(1)}, u32[]{:S(2)}, u32[]{:S(2)}) collective-permute-start(bf16[512,128]{1,0:T(8,128)(2,1)S(1)} %get-tuple-element.25), channel_id=1, source_target_pairs={{0,2},{1,3},{2,0},{3,1},{4,6},{5,7},{6,4},{7,5},{8,10},{9,11},{10,... | collective-permute-start | bytes 393224 | tf_op jit(solution)/shard_map/ppermute | solution.py:275
  39.6 13.8 %collective-permute-start.21 = (bf16[512,128]{1,0:T(8,128)(2,1)S(1)}, bf16[512,128]{1,0:T(8,128)(2,1)S(1)}, u32[]{:S(2)}, u32[]{:S(2)}) collective-permute-start(bf16[512,128]{1,0:T(8,128)(2,1)S(1)} %get-tuple-element.29), channel_id=1, source_target_pairs={{0,2},{1,3},{2,0},{3,1},{4,6},{5,7},{6,4},{7,5},{8,10},{9,11},{10,... | collective-permute-start | bytes 393224 | tf_op jit(solution)/shard_map/ppermute | solution.py:275
  39.7 24.9 %collective-permute-start.15 = (bf16[512,256]{1,0:T(8,128)(2,1)S(1)}, bf16[512,256]{1,0:T(8,128)(2,1)S(1)}, u32[]{:S(2)}, u32[]{:S(2)}) collective-permute-start(bf16[512,256]{1,0:T(8,128)(2,1)S(1)} %get-tuple-element.23), channel_id=1, source_target_pairs={{0,2},{1,3},{2,0},{3,1},{4,6},{5,7},{6,4},{7,5},{8,10},{9,11},{10,... | collective-permute-start | bytes 786440 | tf_op jit(solution)/shard_map/ppermute | solution.py:275
  44.0 13.9 %collective-permute-start.18 = (bf16[512,128]{1,0:T(8,128)(2,1)S(1)}, bf16[512,128]{1,0:T(8,128)(2,1)S(1)}, u32[]{:S(2)}, u32[]{:S(2)}) collective-permute-start(bf16[512,128]{1,0:T(8,128)(2,1)S(1)} %add_convert_fusion.5), channel_id=1, source_target_pairs={{0,4},{1,5},{2,6},{3,7},{4,0},{5,1},{6,2},{7,3},{8,12},{9,13},{10,... | collective-permute-start | bytes 393224 | tf_op jit(solution)/shard_map/ppermute | solution.py:275
  51.4 14.0 %collective-permute-start.20 = (bf16[512,128]{1,0:T(8,128)(2,1)S(1)}, bf16[512,128]{1,0:T(8,128)(2,1)S(1)}, u32[]{:S(2)}, u32[]{:S(2)}) collective-permute-start(bf16[512,128]{1,0:T(8,128)(2,1)S(1)} %broadcast_add_fusion.1), channel_id=1, source_target_pairs={{0,2},{1,3},{2,0},{3,1},{4,6},{5,7},{6,4},{7,5},{8,10},{9,11},{10,... | collective-permute-start | bytes 393224 | tf_op jit(solution)/shard_map/ppermute | solution.py:275
  53.4 12.0 %collective-permute-start.22 = (bf16[512,128]{1,0:T(8,128)(2,1)S(1)}, bf16[512,128]{1,0:T(8,128)(2,1)S(1)}, u32[]{:S(2)}, u32[]{:S(2)}) collective-permute-start(bf16[512,128]{1,0:T(8,128)(2,1)S(1)} %add_convert_fusion.3), channel_id=1, source_target_pairs={{0,4},{1,5},{2,6},{3,7},{4,0},{5,1},{6,2},{7,3},{8,12},{9,13},{10,... | collective-permute-start | bytes 393224 | tf_op jit(solution)/shard_map/ppermute | solution.py:275
  55.9 18.4 %collective-permute-start.14 = (bf16[512,256]{1,0:T(8,128)(2,1)}, bf16[512,256]{1,0:T(8,128)(2,1)}, u32[]{:S(2)}, u32[]{:S(2)}) collective-permute-start(bf16[512,256]{1,0:T(8,128)(2,1)} %broadcast_add_fusion), channel_id=1, source_target_pairs={{0,2},{1,3},{2,0},{3,1},{4,6},{5,7},{6,4},{7,5},{8,10},{9,11},{10,... | collective-permute-start | bytes 786440 | tf_op jit(solution)/shard_map/ppermute | solution.py:275
  58.5 11.6 %collective-permute-start.19 = (bf16[512,128]{1,0:T(8,128)(2,1)}, bf16[512,128]{1,0:T(8,128)(2,1)S(1)}, u32[]{:S(2)}, u32[]{:S(2)}) collective-permute-start(bf16[512,128]{1,0:T(8,128)(2,1)} %add_convert_fusion.4), channel_id=1, source_target_pairs={{0,8},{1,9},{2,10},{3,11},{4,12},{5,13},{6,14},{7,15},{8,0},{9,1},... | collective-permute-start | bytes 393224 | tf_op jit(solution)/shard_map/ppermute | solution.py:275
  65.4 10.9 %collective-permute-start.16 = (bf16[512,256]{1,0:T(8,128)(2,1)}, bf16[512,256]{1,0:T(8,128)(2,1)}, u32[]{:S(2)}, u32[]{:S(2)}) collective-permute-start(bf16[512,256]{1,0:T(8,128)(2,1)} %add_convert_fusion.1), channel_id=1, source_target_pairs={{0,4},{1,5},{2,6},{3,7},{4,0},{5,1},{6,2},{7,3},{8,12},{9,13},{10,... | collective-permute-start | bytes 786440 | tf_op jit(solution)/shard_map/ppermute | solution.py:275
  66.1 8.2 %collective-permute-start.23 = (bf16[512,128]{1,0:T(8,128)(2,1)}, bf16[512,128]{1,0:T(8,128)(2,1)}, u32[]{:S(2)}, u32[]{:S(2)}) collective-permute-start(bf16[512,128]{1,0:T(8,128)(2,1)} %add_convert_fusion.2), channel_id=1, source_target_pairs={{0,8},{1,9},{2,10},{3,11},{4,12},{5,13},{6,14},{7,15},{8,0},{9,1},... | collective-permute-start | bytes 393224 | tf_op jit(solution)/shard_map/ppermute | solution.py:275
  (8 other events, 114.2 us)

commit v2 on v1

--- a/solution.py
+++ b/solution.py
@@ -7,7 +7,7 @@
 from jax.experimental.pallas import tpu as pltpu
 from jax.sharding import PartitionSpec as P
 
-GROUP = 32
+HALF = 16
 STEP = 8
 LANES = 128
 BF = jnp.bfloat16
@@ -41,9 +41,8 @@
     parts, refs = refs[: len(regions)], refs[len(regions) :]
     own, other = refs[:2]
     outs, ket = refs[2 : 2 + len(pieces)], refs[2 + len(pieces)]
-    table, blk, picked, wide, half, second, ready, table_sems, block_sems, out_sems = refs[
-        3 + len(pieces) :
-    ]
+    table, blk, picked_a, wide_a, picked_b, wide_b, half, second, ready = refs[3 + len(pieces) : -3]
+    table_sems, block_sems, out_sems = refs[-3:]
     orbitals = second.shape[1]
     capacity = own.shape[0]
     kh = blk.shape[1]
@@ -74,7 +73,7 @@
     diagonal = (lanes % 8 == lax.broadcasted_iota(jnp.int32, (8, LANES), 0)).astype(F32)
     empty = jnp.zeros((8, LANES), F32)
     spread_a = spread("a")
-    groups = (live + GROUP - 1) // GROUP
+    groups = (live + HALF - 1) // HALF
     steps = (live + STEP - 1) // STEP
     second[...] = jnp.zeros_like(second)
 
@@ -94,35 +93,31 @@
         piece = table_piece(table, locate(seconds[kb], me), 0)
         ket[1, n] = jnp.dot(piece.astype(BF), spread("b"), preferred_element_type=F32)
 
-    def do_step(o, carry):
-        start = o * STEP
-
-        def wait_one(n, carry):
-            pltpu.make_async_copy(
-                own.at[0, pl.ds(k_start, kh)], blk.at[n], block_sems.at[o]
-            ).wait()
-            return carry
-
-        lax.fori_loop(start, jnp.minimum(start + STEP, live), wait_one, 0)
-        slots = [jnp.minimum(start + u, live - 1) for u in range(STEP)]
+    cover = 8 * STEP
+    wanted = lax.broadcasted_iota(jnp.int32, (orbitals, LANES), 1)
+    place = (wanted & (cover - 1)) >> 3
+
+    def slots_of(o):
+        return [jnp.minimum(o * STEP + u, live - 1) for u in range(STEP)]
+
+    def prepare(o, picked, wide):
+        slots = slots_of(o)
         for u, n in enumerate(slots):
             piece = table_piece(table, locate(number(n, 0) * 2, me), 0)
             picked[u * orbitals : (u + 1) * orbitals] = piece.astype(BF)
         wide[...] = jnp.dot(picked[...], spread_a, preferred_element_type=F32)
-
-        cover = 8 * STEP
         parity = o & (LANES // cover - 1)
-        wanted = lax.broadcasted_iota(jnp.int32, (orbitals, LANES), 1)
-        place = (wanted % cover) // 8
         merged = jnp.zeros((orbitals, LANES), F32)
         for u, n in enumerate(slots):
             where = locate(number(n, 1), me)
             piece = table_piece(table, where, parity * cover + 8 * u)
             merged = jnp.where(place == u, piece, merged)
-        keep = (wanted // cover == parity) & (start + place < live)
+        keep = (wanted // cover == parity) & (o * STEP + place < live)
         at = o // (LANES // cover)
         second[at] = jnp.where(keep, merged, second[at])
 
+    def products(o, wide):
+        slots = slots_of(o)
         for p in range(STEP // 2):
             rows = []
             for i in range(orbitals):
@@ -135,21 +130,48 @@
                 rows.append(jnp.concatenate([empty, y], axis=1))
             factor = jnp.concatenate(rows, axis=0).astype(BF)
             data = jnp.concatenate([blk[slots[2 * p]], blk[slots[2 * p + 1]]], axis=1)
-            result = lax.dot_general(
-                factor, data, (((1,), (1,)), ((), ())), preferred_element_type=F32
-            )
             at = pl.multiple_of(o * cover + 16 * p, 16)
-            half[:, pl.ds(at, 16), :] = result.astype(BF).reshape(orbitals, 16, kh)
+            part = orbitals // 2
+            for h in range(2):
+                result = lax.dot_general(
+                    factor[h * part * 16 : (h + 1) * part * 16],
+                    data,
+                    (((1,), (1,)), ((), ())),
+                    preferred_element_type=F32,
+                )
+                half[h * part : (h + 1) * part, pl.ds(at, 16), :] = result.astype(BF).reshape(
+                    part, 16, kh
+                )
+
+    def do_step(o, now, later):
+        def wait_one(n, carry):
+            pltpu.make_async_copy(
+                own.at[0, pl.ds(k_start, kh)], blk.at[n], block_sems.at[o]
+            ).wait()
+            return carry
+
+        lax.fori_loop(o * STEP, jnp.minimum((o + 1) * STEP, live), wait_one, 0)
+        prepare(jnp.minimum(o + 1, steps - 1), *later)
+        products(o, now[1])
+
+    def two_steps(h, carry):
+        do_step(2 * h, (picked_a, wide_a), (picked_b, wide_b))
+
+        @pl.when(2 * h + 1 < steps)
+        def _():
+            do_step(2 * h + 1, (picked_b, wide_b), (picked_a, wide_a))
+
         return carry
 
-    lax.fori_loop(0, steps, do_step, 0)
+    prepare(0, picked_a, wide_a)
+    lax.fori_loop(0, (steps + 1) // 2, two_steps, 0)
 
     def clear(o, carry):
         at = pl.multiple_of(o * 8 * STEP, 8 * STEP)
         half[:, pl.ds(at, 8 * STEP), :] = jnp.zeros((orbitals, 8 * STEP, kh), BF)
         return carry
 
-    lax.fori_loop(steps, groups * (GROUP // STEP), clear, 0)
+    lax.fori_loop(steps, groups * (HALF // STEP), clear, 0)
 
     def leave(n):
         s, low, high = pieces[n]
@@ -158,13 +180,13 @@
         )
 
     def finish(count):
-        weights = jnp.concatenate([second[n] for n in range(2 * count)], axis=1).astype(BF)
+        weights = jnp.concatenate([second[n] for n in range(count)], axis=1).astype(BF)
         for s in dict.fromkeys(piece[0] for piece in pieces):
             first = 0
             if len(pieces) > 1:
                 first = ((me >> 2) ^ (s & 3)) * 2 * chunk + (((me >> 1) & 1) ^ (1 - (s >> 2))) * chunk
             for r in range(chunk):
-                piece = half[first + r, 0 : 8 * GROUP * count, :]
+                piece = half[first + r, 0 : 8 * HALF * count, :]
                 ready[s, r * orbitals : (r + 1) * orbitals, :] = jnp.dot(
                     weights, piece, preferred_element_type=F32
                 ).astype(ready.dtype)
@@ -172,7 +194,7 @@
                 if pieces[n][0] == s:
                     leave(n).start()
 
-    for count in range(1, half.shape[1] // (8 * GROUP) + 1):
+    for count in range(1, half.shape[1] // (8 * HALF) + 1):
         pl.when(groups == count)(functools.partial(finish, count))
     for n in range(len(pieces)):
         leave(n).wait()
@@ -183,7 +205,7 @@
 ):
     capacity, kp, pair = own.shape
     kh = kp // 2
-    groups = -(-2 * capacity // GROUP)
+    groups = -(-2 * capacity // HALF)
     rows = chunk * orbitals
     hbm = pl.BlockSpec(memory_space=pltpu.HBM)
     return pl.pallas_call(
@@ -200,8 +222,10 @@
                 pltpu.VMEM((2 * capacity, kh, pair), BF),
                 pltpu.VMEM((STEP * orbitals, LANES), BF),
                 pltpu.VMEM((STEP * orbitals, LANES), F32),
-                pltpu.VMEM((orbitals, 8 * GROUP * groups, kh), BF),
-                pltpu.VMEM((2 * groups, orbitals, LANES), F32),
+                pltpu.VMEM((STEP * orbitals, LANES), BF),
+                pltpu.VMEM((STEP * orbitals, LANES), F32),
+                pltpu.VMEM((orbitals, 8 * HALF * groups, kh), BF),
+                pltpu.VMEM((groups, orbitals, LANES), F32),
                 pltpu.VMEM((orbitals // chunk, rows, kh), kind),
                 pltpu.SemaphoreType.DMA((len(parts),)),
                 pltpu.SemaphoreType.DMA((-(-2 * capacity // STEP),)),

time: 80.7 us -> 77.4 us (0.959)
  starting transfers between devices: 39 us -> 30.2 us
  waiting for transfers between devices: 19.3 us -> 24.4 us
    ppermute x25, starting transfers between devices: 39 us -> 30.2 us  [permute(): return lax.ppermute(array, 'pan', [(i, i ^ mask) for i in range(count)])]
    ppermute x25, waiting for transfers between devices: 19.3 us -> 24.4 us  [permute(): return lax.ppermute(array, 'pan', [(i, i ^ mask) for i in range(count)])]
  transfers between devices with their start and end apart: 25 -> 25, of which waited for: 11 -> 13; matrix products, arithmetic and copies ran while one was open for 7% -> 7% of each run, Pallas kernels for 0% -> 0%
where the time goes in v2:
time: 77.4 us; the launch traced here: 77.8 us
  starting transfers between devices  30.2 us (39%)
  waiting for transfers between devices  24.4 us (32%)
  Pallas kernels  11.8 us (15%)
  other arithmetic  5.22 us (7%)
  local copies, waits for them, and re-layouts  2.58 us (3%)
  between operations  2.33 us (3%)
  matrix products  1.35 us (2%)
    ppermute x25, starting transfers between devices, permute(): return lax.ppermute(array, 'pan', [(i, i ^ mask) for i in range(count)])  30.2 us
    ppermute x25, waiting for transfers between devices, permute(): return lax.ppermute(array, 'pan', [(i, i ^ mask) for i in range(count)])  24.4 us
    pallas_call x1, Pallas kernels, bra_transform(): pl.pallas_call(functools.partial(bra_kernel, regions, locate, chunk, piec...  9.02 us
    convert_element_type x6, other arithmetic, added(): return result.astype(BF)  3.55 us
    pallas_call x1, Pallas kernels, last_step(): pl.pallas_call(last_kernel, out_shape=jax.ShapeDtypeStruct((rows, orbital...  2.77 us
    unnamed x14, local copies, waits for them, and re-layouts  2.03 us
  transfers between devices with their start and end apart: 25, of which 13 were waited for; matrix products, arithmetic and copies ran while one was open for 7% of the time, Pallas kernels for 0%

profile of v2, /device:TPU:0, one launch (start us, length us, event | category | flops | bytes accessed | tf_op | source)
XLA Modules:
  0.0 77.8 jit_solution(12261760522611118790)
XLA Ops:
  0.5 1.3 %copy-done = bf16[752,2000]{0,1:T(8,128)(2,1)S(1)} copy-done((bf16[752,2000]{0,1:T(8,128)(2,1)S(1)}, bf16[752,2000]{0,1:T(8,128)(2,1)}, u32[]{:S(2)}) %copy-start) | copy-done | bytes 3008024
  1.9 1.3 %convolution_convert_fusion = bf16[64,752]{1,0:T(8,128)(2,1)S(1)} fusion(bf16[752,2000]{0,1:T(8,128)(2,1)S(1)} %copy-done, s32[64]{0:T(128)} %param.15), kind=kOutput, calls=%fused_computation | convolution fusion | flops 192688128 | bytes 3104512 | tf_op jit(solution)/shard_map/dot_general | solution.py:346
  3.2 3.0 %collective-permute-start.7 = (bf16[32,768]{1,0:T(8,128)(2,1)S(1)}, bf16[32,768]{1,0:T(8,128)(2,1)S(1)}, u32[]{:S(2)}, u32[]{:S(2)}) collective-permute-start(bf16[32,768]{1,0:T(8,128)(2,1)S(1)} %get-tuple-element.37), channel_id=1, source_target_pairs={{0,2},{1,3},{2,0},{3,1},{4,6},{5,7},{6,4},{7,5},{8,10},{9,11},{10,... | collective-permute-start | bytes 147464 | tf_op jit(solution)/shard_map/ppermute | solution.py:299
  7.0 1.6 %collective-permute-start.1 = (bf16[32,768]{1,0:T(8,128)(2,1)S(1)}, bf16[32,768]{1,0:T(8,128)(2,1)S(1)}, u32[]{:S(2)}, u32[]{:S(2)}) collective-permute-start(bf16[32,768]{1,0:T(8,128)(2,1)S(1)} %get-tuple-element.38), channel_id=1, source_target_pairs={{0,4},{1,5},{2,6},{3,7},{4,0},{5,1},{6,2},{7,3},{8,12},{9,13},{10,... | collective-permute-start | bytes 147464 | tf_op jit(solution)/shard_map/ppermute | solution.py:299
  8.7 2.6 %collective-permute-start.2 = (bf16[32,768]{1,0:T(8,128)(2,1)S(1)}, bf16[32,768]{1,0:T(8,128)(2,1)S(1)}, u32[]{:S(2)}, u32[]{:S(2)}) collective-permute-start(bf16[32,768]{1,0:T(8,128)(2,1)S(1)} %get-tuple-element.38), channel_id=1, source_target_pairs={{0,8},{1,9},{2,10},{3,11},{4,12},{5,13},{6,14},{7,15},{8,0},{9,1},... | collective-permute-start | bytes 147464 | tf_op jit(solution)/shard_map/ppermute | solution.py:299
  11.2 2.5 %collective-permute-start.3 = (bf16[32,768]{1,0:T(8,128)(2,1)S(1)}, bf16[32,768]{1,0:T(8,128)(2,1)S(1)}, u32[]{:S(2)}, u32[]{:S(2)}) collective-permute-start(bf16[32,768]{1,0:T(8,128)(2,1)S(1)} %get-tuple-element.38), channel_id=1, source_target_pairs={{0,12},{1,13},{2,14},{3,15},{4,8},{5,9},{6,10},{7,11},{8,4},{9,5},... | collective-permute-start | bytes 147464 | tf_op jit(solution)/shard_map/ppermute | solution.py:299
  13.9 1.9 %collective-permute-start.10 = (bf16[2,32,768]{2,1,0:T(8,128)(2,1)S(1)}, bf16[2,32,768]{2,1,0:T(8,128)(2,1)S(1)}, u32[]{:S(2)}, u32[]{:S(2)}) collective-permute-start(bf16[2,32,768]{2,1,0:T(8,128)(2,1)S(1)} %get-tuple-element.34), channel_id=1, source_target_pairs={{0,12},{1,13},{2,14},{3,15},{4,8},{5,9},{6,10},{7,11},{8,4},{9,5},... | collective-permute-start | bytes 294920 | tf_op jit(solution)/shard_map/ppermute | solution.py:299
  15.8 1.6 %collective-permute-start.8 = (bf16[2,32,768]{2,1,0:T(8,128)(2,1)S(1)}, bf16[2,32,768]{2,1,0:T(8,128)(2,1)S(1)}, u32[]{:S(2)}, u32[]{:S(2)}) collective-permute-start(bf16[2,32,768]{2,1,0:T(8,128)(2,1)S(1)} %get-tuple-element.34), channel_id=1, source_target_pairs={{0,4},{1,5},{2,6},{3,7},{4,0},{5,1},{6,2},{7,3},{8,12},{9,13},{10,... | collective-permute-start | bytes 294920 | tf_op jit(solution)/shard_map/ppermute | solution.py:299
  19.0 4.2 %collective-permute-done.9 = bf16[2,32,768]{2,1,0:T(8,128)(2,1)S(1)} collective-permute-done((bf16[2,32,768]{2,1,0:T(8,128)(2,1)S(1)}, bf16[2,32,768]{2,1,0:T(8,128)(2,1)S(1)}, u32[]{:S(2)}, u32[]{:S(2)}) %collective-permute-start.9) | collective-permute-done | bytes 98336 | tf_op jit(solution)/shard_map/ppermute | solution.py:299
  25.4 1.4 %collective-permute-done.4.refs_1_ = bf16[4,32,768]{2,1,0:T(8,128)(2,1)} collective-permute-done((bf16[4,32,768]{2,1,0:T(8,128)(2,1)S(1)}, bf16[4,32,768]{2,1,0:T(8,128)(2,1)}, u32[]{:S(2)}, u32[]{:S(2)}) %collective-permute-start.4) | collective-permute-done | bytes 196640 | tf_op jit(solution)/shard_map/ppermute | solution.py:299
  27.5 9.0 %bra_transform.1 = (bf16[512,128]{1,0:T(8,128)(2,1)S(1)}, bf16[512,128]{1,0:T(8,128)(2,1)S(1)}, bf16[512,128]{1,0:T(8,128)(2,1)S(1)}, bf16[512,128]{1,0:T(8,128)...) custom-call(s32[1]{0:T(128)} %bitcast.me_ref, ...), custom_call_target="tpu_custom_call" | custom-call | flops 2684354560 | bytes 8388608 | tf_op jit(solution)/shard_map/bra_transform/pallas_call | solution.py:211
  37.2 6.7 %collective-permute-start.13 = (bf16[512,128]{1,0:T(8,128)(2,1)S(1)}, bf16[512,128]{1,0:T(8,128)(2,1)S(1)}, u32[]{:S(2)}, u32[]{:S(2)}) collective-permute-start(bf16[512,128]{1,0:T(8,128)(2,1)S(1)} %get-tuple-element.21), channel_id=1, source_target_pairs={{0,2},{1,3},{2,0},{3,1},{4,6},{5,7},{6,4},{7,5},{8,10},{9,11},{10,... | collective-permute-start | bytes 393224 | tf_op jit(solution)/shard_map/ppermute | solution.py:299
  44.0 2.0 %collective-permute-start.21 = (bf16[512,128]{1,0:T(8,128)(2,1)S(1)}, bf16[512,128]{1,0:T(8,128)(2,1)S(1)}, u32[]{:S(2)}, u32[]{:S(2)}) collective-permute-start(bf16[512,128]{1,0:T(8,128)(2,1)S(1)} %get-tuple-element.29), channel_id=1, source_target_pairs={{0,2},{1,3},{2,0},{3,1},{4,6},{5,7},{6,4},{7,5},{8,10},{9,11},{10,... | collective-permute-start | bytes 393224 | tf_op jit(solution)/shard_map/ppermute | solution.py:299
  46.0 2.2 %collective-permute-done.13 = bf16[512,128]{1,0:T(8,128)(2,1)S(1)} collective-permute-done((bf16[512,128]{1,0:T(8,128)(2,1)S(1)}, bf16[512,128]{1,0:T(8,128)(2,1)S(1)}, u32[]{:S(2)}, u32[]{:S(2)}) %collective-permute-start.13) | collective-permute-done | bytes 131104 | tf_op jit(solution)/shard_map/ppermute | solution.py:299
  50.6 1.7 %collective-permute-start.20 = (bf16[512,128]{1,0:T(8,128)(2,1)S(1)}, bf16[512,128]{1,0:T(8,128)(2,1)S(1)}, u32[]{:S(2)}, u32[]{:S(2)}) collective-permute-start(bf16[512,128]{1,0:T(8,128)(2,1)S(1)} %broadcast_add_fusion.1), channel_id=1, source_target_pairs={{0,2},{1,3},{2,0},{3,1},{4,6},{5,7},{6,4},{7,5},{8,10},{9,11},{10,... | collective-permute-start | bytes 393224 | tf_op jit(solution)/shard_map/ppermute | solution.py:299
  52.3 1.5 %collective-permute-done.21 = bf16[512,128]{1,0:T(8,128)(2,1)S(1)} collective-permute-done((bf16[512,128]{1,0:T(8,128)(2,1)S(1)}, bf16[512,128]{1,0:T(8,128)(2,1)S(1)}, u32[]{:S(2)}, u32[]{:S(2)}) %collective-permute-start.21) | collective-permute-done | bytes 131104 | tf_op jit(solution)/shard_map/ppermute | solution.py:299
  55.2 1.6 %collective-permute-start.14 = (bf16[512,256]{1,0:T(8,128)(2,1)}, bf16[512,256]{1,0:T(8,128)(2,1)}, u32[]{:S(2)}, u32[]{:S(2)}) collective-permute-start(bf16[512,256]{1,0:T(8,128)(2,1)} %broadcast_add_fusion), channel_id=1, source_target_pairs={{0,2},{1,3},{2,0},{3,1},{4,6},{5,7},{6,4},{7,5},{8,10},{9,11},{10,... | collective-permute-start | bytes 786440 | tf_op jit(solution)/shard_map/ppermute | solution.py:299
  57.5 2.0 %collective-permute-done.15 = bf16[512,256]{1,0:T(8,128)(2,1)S(1)} collective-permute-done((bf16[512,256]{1,0:T(8,128)(2,1)S(1)}, bf16[512,256]{1,0:T(8,128)(2,1)S(1)}, u32[]{:S(2)}, u32[]{:S(2)}) %collective-permute-start.15) | collective-permute-done | bytes 262176 | tf_op jit(solution)/shard_map/ppermute | solution.py:299
  60.7 1.6 %collective-permute-done.20 = bf16[512,128]{1,0:T(8,128)(2,1)S(1)} collective-permute-done((bf16[512,128]{1,0:T(8,128)(2,1)S(1)}, bf16[512,128]{1,0:T(8,128)(2,1)S(1)}, u32[]{:S(2)}, u32[]{:S(2)}) %collective-permute-start.20) | collective-permute-done | bytes 131104 | tf_op jit(solution)/shard_map/ppermute | solution.py:299
  63.9 6.7 %collective-permute-done.23 = bf16[512,128]{1,0:T(8,128)(2,1)} collective-permute-done((bf16[512,128]{1,0:T(8,128)(2,1)}, bf16[512,128]{1,0:T(8,128)(2,1)}, u32[]{:S(2)}, u32[]{:S(2)}) %collective-permute-start.23) | collective-permute-done | bytes 131104 | tf_op jit(solution)/shard_map/ppermute | solution.py:299
  70.6 1.6 %collective-permute-done.16 = bf16[512,256]{1,0:T(8,128)(2,1)} collective-permute-done((bf16[512,256]{1,0:T(8,128)(2,1)}, bf16[512,256]{1,0:T(8,128)(2,1)}, u32[]{:S(2)}, u32[]{:S(2)}) %collective-permute-start.16) | collective-permute-done | bytes 262176 | tf_op jit(solution)/shard_map/ppermute | solution.py:299
  72.2 1.3 %add_convert_fusion = bf16[512,256]{1,0:T(8,128)(2,1)S(1)} fusion(bf16[512,256]{1,0:T(8,128)(2,1)} %collective-permute-done.16, bf16[512,256]{1,0:T(8,128)(2,1)} %collective-permute-done.14, bf16[512,256]{1,0:T(8,128)(2,1)} %copy-done.2, bf16[512,128]{1,0:T(8,128)(2,1)} %collective-permute-done.23, bf16[512,128]{1,0:T(8,128)(2,1)S(1)} %collective-permute-done.19), kind=kLoop, calls=%fused_computation.1 | loop fusion | flops 1441792 | bytes 1310720 | tf_op jit(solution)/shard_map/convert_element_type | solution.py:306
  73.6 1.3 %collective-permute-done.24.other = bf16[256,256]{1,0:T(8,128)(2,1)S(1)} collective-permute-done((bf16[256,256]{1,0:T(8,128)(2,1)S(1)}, bf16[256,256]{1,0:T(8,128)(2,1)S(1)}, u32[]{:S(2)}, u32[]{:S(2)}) %collective-permute-start.24) | collective-permute-done | bytes 131104 | tf_op jit(solution)/shard_map/ppermute | solution.py:299
  74.9 2.8 %last_step.1 = f32[256,4096]{1,0:T(8,128)} custom-call(bf16[256,256]{1,0:T(8,128)(2,1)S(1)} %get-tuple-element.32.own, bf16[256,256]{1,0:T(8,128)(2,1)S(1)} %collective-permute-done.24.other, f32[2,4,64,128]{3,2,1,0:T(8,128)S(1)} %copy-done.1), custom_call_target="tpu_custom_call" | custom-call | tf_op jit(solution)/shard_map/last_step/pallas_call | solution.py:283
  (58 shorter events, 12.0 us)
Async XLA Ops:
  0.0 27.5 %collective-permute-start.12 = (bf16[40,512,128]{2,1,0:T(8,128)(2,1)}, bf16[40,512,128]{2,1,0:T(8,128)(2,1)}, u32[]{:S(2)}, u32[]{:S(2)}) collective-permute-start(bf16[40,512,128]{2,1,0:T(8,128)(2,1)} %refs_6_.1), channel_id=1, source_target_pairs={{0,1},{1,0},{2,3},{3,2},{4,5},{5,4},{6,7},{7,6},{8,9},{9,8},{10,11... | collective-permute-start | bytes 15728648 | tf_op jit(solution)/shard_map/ppermute | solution.py:299
  3.2 10.6 %collective-permute-start.7 = (bf16[32,768]{1,0:T(8,128)(2,1)S(1)}, bf16[32,768]{1,0:T(8,128)(2,1)S(1)}, u32[]{:S(2)}, u32[]{:S(2)}) collective-permute-start(bf16[32,768]{1,0:T(8,128)(2,1)S(1)} %get-tuple-element.37), channel_id=1, source_target_pairs={{0,2},{1,3},{2,0},{3,1},{4,6},{5,7},{6,4},{7,5},{8,10},{9,11},{10,... | collective-permute-start | bytes 147464 | tf_op jit(solution)/shard_map/ppermute | solution.py:299
  7.0 4.3 %collective-permute-start = (s32[81]{0:T(128)S(1)}, s32[81]{0:T(128)S(1)}, u32[]{:S(2)}, u32[]{:S(2)}) collective-permute-start(s32[81]{0:T(128)S(1)} %pad_add_fusion.mine), channel_id=1, source_target_pairs={{0,1},{1,0},{2,3},{3,2},{4,5},{5,4},{6,7},{7,6},{8,9},{9,8},{10,11... | collective-permute-start | bytes 980 | tf_op jit(solution)/shard_map/ppermute | solution.py:299
  7.0 6.9 %collective-permute-start.1 = (bf16[32,768]{1,0:T(8,128)(2,1)S(1)}, bf16[32,768]{1,0:T(8,128)(2,1)S(1)}, u32[]{:S(2)}, u32[]{:S(2)}) collective-permute-start(bf16[32,768]{1,0:T(8,128)(2,1)S(1)} %get-tuple-element.38), channel_id=1, source_target_pairs={{0,4},{1,5},{2,6},{3,7},{4,0},{5,1},{6,2},{7,3},{8,12},{9,13},{10,... | collective-permute-start | bytes 147464 | tf_op jit(solution)/shard_map/ppermute | solution.py:299
  8.7 7.2 %collective-permute-start.2 = (bf16[32,768]{1,0:T(8,128)(2,1)S(1)}, bf16[32,768]{1,0:T(8,128)(2,1)S(1)}, u32[]{:S(2)}, u32[]{:S(2)}) collective-permute-start(bf16[32,768]{1,0:T(8,128)(2,1)S(1)} %get-tuple-element.38), channel_id=1, source_target_pairs={{0,8},{1,9},{2,10},{3,11},{4,12},{5,13},{6,14},{7,15},{8,0},{9,1},... | collective-permute-start | bytes 147464 | tf_op jit(solution)/shard_map/ppermute | solution.py:299
  11.2 6.4 %collective-permute-start.3 = (bf16[32,768]{1,0:T(8,128)(2,1)S(1)}, bf16[32,768]{1,0:T(8,128)(2,1)S(1)}, u32[]{:S(2)}, u32[]{:S(2)}) collective-permute-start(bf16[32,768]{1,0:T(8,128)(2,1)S(1)} %get-tuple-element.38), channel_id=1, source_target_pairs={{0,12},{1,13},{2,14},{3,15},{4,8},{5,9},{6,10},{7,11},{8,4},{9,5},... | collective-permute-start | bytes 147464 | tf_op jit(solution)/shard_map/ppermute | solution.py:299
  13.8 9.4 %collective-permute-start.9 = (bf16[2,32,768]{2,1,0:T(8,128)(2,1)S(1)}, bf16[2,32,768]{2,1,0:T(8,128)(2,1)S(1)}, u32[]{:S(2)}, u32[]{:S(2)}) collective-permute-start(bf16[2,32,768]{2,1,0:T(8,128)(2,1)S(1)} %get-tuple-element.34), channel_id=1, source_target_pairs={{0,8},{1,9},{2,10},{3,11},{4,12},{5,13},{6,14},{7,15},{8,0},{9,1},... | collective-permute-start | bytes 294920 | tf_op jit(solution)/shard_map/ppermute | solution.py:299
  13.9 9.3 %collective-permute-start.10 = (bf16[2,32,768]{2,1,0:T(8,128)(2,1)S(1)}, bf16[2,32,768]{2,1,0:T(8,128)(2,1)S(1)}, u32[]{:S(2)}, u32[]{:S(2)}) collective-permute-start(bf16[2,32,768]{2,1,0:T(8,128)(2,1)S(1)} %get-tuple-element.34), channel_id=1, source_target_pairs={{0,12},{1,13},{2,14},{3,15},{4,8},{5,9},{6,10},{7,11},{8,4},{9,5},... | collective-permute-start | bytes 294920 | tf_op jit(solution)/shard_map/ppermute | solution.py:299
  15.8 8.3 %collective-permute-start.8 = (bf16[2,32,768]{2,1,0:T(8,128)(2,1)S(1)}, bf16[2,32,768]{2,1,0:T(8,128)(2,1)S(1)}, u32[]{:S(2)}, u32[]{:S(2)}) collective-permute-start(bf16[2,32,768]{2,1,0:T(8,128)(2,1)S(1)} %get-tuple-element.34), channel_id=1, source_target_pairs={{0,4},{1,5},{2,6},{3,7},{4,0},{5,1},{6,2},{7,3},{8,12},{9,13},{10,... | collective-permute-start | bytes 294920 | tf_op jit(solution)/shard_map/ppermute | solution.py:299
  17.7 7.7 %collective-permute-start.5 = (bf16[4,32,768]{2,1,0:T(8,128)(2,1)S(1)}, bf16[4,32,768]{2,1,0:T(8,128)(2,1)S(1)}, u32[]{:S(2)}, u32[]{:S(2)}) collective-permute-start(bf16[4,32,768]{2,1,0:T(8,128)(2,1)S(1)} %maximum_add_fusion.refs_0_), channel_id=1, source_target_pairs={{0,2},{1,3},{2,0},{3,1},{4,6},{5,7},{6,4},{7,5},{8,10},{9,11},{10,... | collective-permute-start | bytes 589832 | tf_op jit(solution)/shard_map/ppermute | solution.py:299
  24.9 2.6 %collective-permute-start.11 = (bf16[4,2,32,768]{3,2,1,0:T(8,128)(2,1)}, bf16[4,2,32,768]{3,2,1,0:T(8,128)(2,1)}, u32[]{:S(2)}, u32[]{:S(2)}) collective-permute-start(bf16[4,2,32,768]{3,2,1,0:T(8,128)(2,1)} %pad_maximum_fusion.refs_4_), channel_id=1, source_target_pairs={{0,1},{1,0},{2,3},{3,2},{4,5},{5,4},{6,7},{7,6},{8,9},{9,8},{10,11... | collective-permute-start | bytes 1179656 | tf_op jit(solution)/shard_map/ppermute | solution.py:299
  24.9 1.9 %collective-permute-start.4 = (bf16[4,32,768]{2,1,0:T(8,128)(2,1)S(1)}, bf16[4,32,768]{2,1,0:T(8,128)(2,1)}, u32[]{:S(2)}, u32[]{:S(2)}) collective-permute-start(bf16[4,32,768]{2,1,0:T(8,128)(2,1)S(1)} %maximum_add_fusion.refs_0_), channel_id=1, source_target_pairs={{0,1},{1,0},{2,3},{3,2},{4,5},{5,4},{6,7},{7,6},{8,9},{9,8},{10,11... | collective-permute-start | bytes 589832 | tf_op jit(solution)/shard_map/ppermute | solution.py:299
  25.4 1.9 %collective-permute-start.6 = (bf16[4,32,768]{2,1,0:T(8,128)(2,1)S(1)}, bf16[4,32,768]{2,1,0:T(8,128)(2,1)}, u32[]{:S(2)}, u32[]{:S(2)}) collective-permute-start(bf16[4,32,768]{2,1,0:T(8,128)(2,1)S(1)} %collective-permute-done.5.refs_2_), channel_id=1, source_target_pairs={{0,1},{1,0},{2,3},{3,2},{4,5},{5,4},{6,7},{7,6},{8,9},{9,8},{10,11... | collective-permute-start | bytes 589832 | tf_op jit(solution)/shard_map/ppermute | solution.py:299
  37.2 11.0 %collective-permute-start.13 = (bf16[512,128]{1,0:T(8,128)(2,1)S(1)}, bf16[512,128]{1,0:T(8,128)(2,1)S(1)}, u32[]{:S(2)}, u32[]{:S(2)}) collective-permute-start(bf16[512,128]{1,0:T(8,128)(2,1)S(1)} %get-tuple-element.21), channel_id=1, source_target_pairs={{0,2},{1,3},{2,0},{3,1},{4,6},{5,7},{6,4},{7,5},{8,10},{9,11},{10,... | collective-permute-start | bytes 393224 | tf_op jit(solution)/shard_map/ppermute | solution.py:299
  44.0 11.2 %collective-permute-start.17 = (bf16[512,128]{1,0:T(8,128)(2,1)S(1)}, bf16[512,128]{1,0:T(8,128)(2,1)S(1)}, u32[]{:S(2)}, u32[]{:S(2)}) collective-permute-start(bf16[512,128]{1,0:T(8,128)(2,1)S(1)} %get-tuple-element.25), channel_id=1, source_target_pairs={{0,2},{1,3},{2,0},{3,1},{4,6},{5,7},{6,4},{7,5},{8,10},{9,11},{10,... | collective-permute-start | bytes 393224 | tf_op jit(solution)/shard_map/ppermute | solution.py:299
  44.0 9.9 %collective-permute-start.21 = (bf16[512,128]{1,0:T(8,128)(2,1)S(1)}, bf16[512,128]{1,0:T(8,128)(2,1)S(1)}, u32[]{:S(2)}, u32[]{:S(2)}) collective-permute-start(bf16[512,128]{1,0:T(8,128)(2,1)S(1)} %get-tuple-element.29), channel_id=1, source_target_pairs={{0,2},{1,3},{2,0},{3,1},{4,6},{5,7},{6,4},{7,5},{8,10},{9,11},{10,... | collective-permute-start | bytes 393224 | tf_op jit(solution)/shard_map/ppermute | solution.py:299
  46.0 13.5 %collective-permute-start.15 = (bf16[512,256]{1,0:T(8,128)(2,1)S(1)}, bf16[512,256]{1,0:T(8,128)(2,1)S(1)}, u32[]{:S(2)}, u32[]{:S(2)}) collective-permute-start(bf16[512,256]{1,0:T(8,128)(2,1)S(1)} %get-tuple-element.23), channel_id=1, source_target_pairs={{0,2},{1,3},{2,0},{3,1},{4,6},{5,7},{6,4},{7,5},{8,10},{9,11},{10,... | collective-permute-start | bytes 786440 | tf_op jit(solution)/shard_map/ppermute | solution.py:299
  48.3 8.5 %collective-permute-start.18 = (bf16[512,128]{1,0:T(8,128)(2,1)S(1)}, bf16[512,128]{1,0:T(8,128)(2,1)S(1)}, u32[]{:S(2)}, u32[]{:S(2)}) collective-permute-start(bf16[512,128]{1,0:T(8,128)(2,1)S(1)} %add_convert_fusion.5), channel_id=1, source_target_pairs={{0,4},{1,5},{2,6},{3,7},{4,0},{5,1},{6,2},{7,3},{8,12},{9,13},{10,... | collective-permute-start | bytes 393224 | tf_op jit(solution)/shard_map/ppermute | solution.py:299
  50.6 11.7 %collective-permute-start.20 = (bf16[512,128]{1,0:T(8,128)(2,1)S(1)}, bf16[512,128]{1,0:T(8,128)(2,1)S(1)}, u32[]{:S(2)}, u32[]{:S(2)}) collective-permute-start(bf16[512,128]{1,0:T(8,128)(2,1)S(1)} %broadcast_add_fusion.1), channel_id=1, source_target_pairs={{0,2},{1,3},{2,0},{3,1},{4,6},{5,7},{6,4},{7,5},{8,10},{9,11},{10,... | collective-permute-start | bytes 393224 | tf_op jit(solution)/shard_map/ppermute | solution.py:299
  53.9 8.4 %collective-permute-start.22 = (bf16[512,128]{1,0:T(8,128)(2,1)S(1)}, bf16[512,128]{1,0:T(8,128)(2,1)S(1)}, u32[]{:S(2)}, u32[]{:S(2)}) collective-permute-start(bf16[512,128]{1,0:T(8,128)(2,1)S(1)} %add_convert_fusion.3), channel_id=1, source_target_pairs={{0,4},{1,5},{2,6},{3,7},{4,0},{5,1},{6,2},{7,3},{8,12},{9,13},{10,... | collective-permute-start | bytes 393224 | tf_op jit(solution)/shard_map/ppermute | solution.py:299
  55.2 15.4 %collective-permute-start.14 = (bf16[512,256]{1,0:T(8,128)(2,1)}, bf16[512,256]{1,0:T(8,128)(2,1)}, u32[]{:S(2)}, u32[]{:S(2)}) collective-permute-start(bf16[512,256]{1,0:T(8,128)(2,1)} %broadcast_add_fusion), channel_id=1, source_target_pairs={{0,2},{1,3},{2,0},{3,1},{4,6},{5,7},{6,4},{7,5},{8,10},{9,11},{10,... | collective-permute-start | bytes 786440 | tf_op jit(solution)/shard_map/ppermute | solution.py:299
  57.5 6.4 %collective-permute-start.19 = (bf16[512,128]{1,0:T(8,128)(2,1)}, bf16[512,128]{1,0:T(8,128)(2,1)S(1)}, u32[]{:S(2)}, u32[]{:S(2)}) collective-permute-start(bf16[512,128]{1,0:T(8,128)(2,1)} %add_convert_fusion.4), channel_id=1, source_target_pairs={{0,8},{1,9},{2,10},{3,11},{4,12},{5,13},{6,14},{7,15},{8,0},{9,1},... | collective-permute-start | bytes 393224 | tf_op jit(solution)/shard_map/ppermute | solution.py:299
  60.2 11.9 %collective-permute-start.16 = (bf16[512,256]{1,0:T(8,128)(2,1)}, bf16[512,256]{1,0:T(8,128)(2,1)}, u32[]{:S(2)}, u32[]{:S(2)}) collective-permute-start(bf16[512,256]{1,0:T(8,128)(2,1)} %add_convert_fusion.1), channel_id=1, source_target_pairs={{0,4},{1,5},{2,6},{3,7},{4,0},{5,1},{6,2},{7,3},{8,12},{9,13},{10,... | collective-permute-start | bytes 786440 | tf_op jit(solution)/shard_map/ppermute | solution.py:299
  63.0 7.6 %collective-permute-start.23 = (bf16[512,128]{1,0:T(8,128)(2,1)}, bf16[512,128]{1,0:T(8,128)(2,1)}, u32[]{:S(2)}, u32[]{:S(2)}) collective-permute-start(bf16[512,128]{1,0:T(8,128)(2,1)} %add_convert_fusion.2), channel_id=1, source_target_pairs={{0,8},{1,9},{2,10},{3,11},{4,12},{5,13},{6,14},{7,15},{8,0},{9,1},... | collective-permute-start | bytes 393224 | tf_op jit(solution)/shard_map/ppermute | solution.py:299
  (8 other events, 110.4 us)

commit v3 on v2

--- a/solution.py
+++ b/solution.py
@@ -306,14 +306,14 @@
     return result.astype(BF)
 
 
-def gather_small(mine, nothing, count):
+def gather_small(mine, count):
     middle = mine.shape[0] // 2
     a, b = mine[:middle], mine[middle:]
     b_x = permute(b, 2, count)
     a_z = {s: permute(a, 4 * s, count) for s in (3, 2, 1)}
     b_pair = jnp.stack([b, b_x])
     b_z = {s: permute(b_pair, 4 * s, count) for s in (3, 2, 1)}
-    near = jnp.stack([a, a_z[1], a_z[2], a_z[3]]) + nothing
+    near = jnp.stack([a, a_z[1], a_z[2], a_z[3]])
     far = permute(near, 2, count)
     rest = jnp.stack([b_pair, b_z[1], b_z[2], b_z[3]])
     upper, lower = pl.ds(0, middle), pl.ds(middle, middle)
@@ -342,10 +342,8 @@
 
     numbers = jnp.concatenate([first_block, second_block, slot_counts])
     other_numbers = swap(numbers)
-    picks = (mo_index[:, None] == jnp.arange(nmo, dtype=jnp.int32)[None, :]).astype(BF)
-    mine = lax.dot_general(
-        picks, coefficients, (((1,), (1,)), ((), ())), preferred_element_type=F32
-    ).astype(BF)
+    nothing = (other_numbers[0] < 0).astype(BF)
+    mine = coefficients.T.at[mo_index].get(mode="promise_in_bounds") + nothing
     orbitals = mine.shape[0]
 
     units = own_ao // 8
@@ -354,9 +352,8 @@
 
     small = count == 16 and own_ao % 16 == 0
     if small:
-        nothing = (other_numbers[0] < 0).astype(BF)
         mine = jnp.pad(mine, ((0, 0), (0, -own_ao % LANES)))
-        parts, regions = gather_small(mine, nothing, count)
+        parts, regions = gather_small(mine, count)
 
         def locate(unit, me):
             owner = (unit * factor) >> 20

time: 77.4 us -> 83 us (1.072)
  starting transfers between devices: 30.2 us -> 36.5 us
  waiting for transfers between devices: 24.4 us -> 22.7 us
  matrix products: 1.35 us -> 0 us
  other arithmetic: 5.22 us -> 6.56 us
    ppermute x25, starting transfers between devices: 30.2 us -> 36.5 us  [permute(): return lax.ppermute(array, 'pan', [(i, i ^ mask) for i in range(count)])]
    ppermute x25, waiting for transfers between devices: 24.4 us -> 22.7 us  [permute(): return lax.ppermute(array, 'pan', [(i, i ^ mask) for i in range(count)])]
    dot_general x1 -> x0, matrix products: 1.35 us -> none  [shards(): lax.dot_general(picks, coefficients, (((1,), (1,)), ((), ())), preferred_...]
    unnamed x14 -> x10, local copies, waits for them, and re-layouts: 2.03 us -> 2 us
  transfers between devices with their start and end apart: 25 -> 25, of which waited for: 13 -> 10; matrix products, arithmetic and copies ran while one was open for 7% -> 8% of each run, Pallas kernels for 0% -> 0%
where the time goes in v3:
time: 83 us; the launch traced here: 84.1 us
  starting transfers between devices  36.5 us (44%)
  waiting for transfers between devices  22.7 us (27%)
  Pallas kernels  12.5 us (15%)
  other arithmetic  6.56 us (8%)
  local copies, waits for them, and re-layouts  3.26 us (4%)
  between operations  2.51 us (3%)
    ppermute x25, starting transfers between devices, permute(): return lax.ppermute(array, 'pan', [(i, i ^ mask) for i in range(count)])  36.5 us
    ppermute x25, waiting for transfers between devices, permute(): return lax.ppermute(array, 'pan', [(i, i ^ mask) for i in range(count)])  22.7 us
    pallas_call x1, Pallas kernels, bra_transform(): pl.pallas_call(functools.partial(bra_kernel, regions, locate, chunk, piec...  9.77 us
    convert_element_type x6, other arithmetic, added(): return result.astype(BF)  3.54 us
    pallas_call x1, Pallas kernels, last_step(): pl.pallas_call(last_kernel, out_shape=jax.ShapeDtypeStruct((rows, orbital...  2.77 us
    unnamed x10, local copies, waits for them, and re-layouts  2 us
  transfers between devices with their start and end apart: 25, of which 10 were waited for; matrix products, arithmetic and copies ran while one was open for 8% of the time, Pallas kernels for 0%

profile of v3, /device:TPU:0, one launch (start us, length us, event | category | flops | bytes accessed | tf_op | source)
XLA Modules:
  0.0 84.1 jit_solution(2688331101596298102)
XLA Ops:
  1.3 0.7 pad_add_fusion.mine
  3.5 5.2 %collective-permute-done.theirs = s32[81]{0:T(128)S(1)} collective-permute-done((s32[81]{0:T(128)S(1)}, s32[81]{0:T(128)S(1)}, u32[]{:S(2)}, u32[]{:S(2)}) %collective-permute-start) | collective-permute-done | bytes 356 | tf_op jit(solution)/shard_map/ppermute | solution.py:299
  8.8 2.9 %collective-permute-start.7 = (bf16[32,768]{1,0:T(8,128)(2,1)S(1)}, bf16[32,768]{1,0:T(8,128)(2,1)S(1)}, u32[]{:S(2)}, u32[]{:S(2)}) collective-permute-start(bf16[32,768]{1,0:T(8,128)(2,1)S(1)} %get-tuple-element.37), channel_id=1, source_target_pairs={{0,2},{1,3},{2,0},{3,1},{4,6},{5,7},{6,4},{7,5},{8,10},{9,11},{10,... | collective-permute-start | bytes 147464 | tf_op jit(solution)/shard_map/ppermute | solution.py:299
  11.7 1.6 %collective-permute-start.1 = (bf16[32,768]{1,0:T(8,128)(2,1)S(1)}, bf16[32,768]{1,0:T(8,128)(2,1)S(1)}, u32[]{:S(2)}, u32[]{:S(2)}) collective-permute-start(bf16[32,768]{1,0:T(8,128)(2,1)S(1)} %get-tuple-element.38), channel_id=1, source_target_pairs={{0,4},{1,5},{2,6},{3,7},{4,0},{5,1},{6,2},{7,3},{8,12},{9,13},{10,... | collective-permute-start | bytes 147464 | tf_op jit(solution)/shard_map/ppermute | solution.py:299
  13.3 2.6 %collective-permute-start.2 = (bf16[32,768]{1,0:T(8,128)(2,1)S(1)}, bf16[32,768]{1,0:T(8,128)(2,1)S(1)}, u32[]{:S(2)}, u32[]{:S(2)}) collective-permute-start(bf16[32,768]{1,0:T(8,128)(2,1)S(1)} %get-tuple-element.38), channel_id=1, source_target_pairs={{0,8},{1,9},{2,10},{3,11},{4,12},{5,13},{6,14},{7,15},{8,0},{9,1},... | collective-permute-start | bytes 147464 | tf_op jit(solution)/shard_map/ppermute | solution.py:299
  16.9 3.5 %collective-permute-start.9 = (bf16[2,32,768]{2,1,0:T(8,128)(2,1)S(1)}, bf16[2,32,768]{2,1,0:T(8,128)(2,1)S(1)}, u32[]{:S(2)}, u32[]{:S(2)}) collective-permute-start(bf16[2,32,768]{2,1,0:T(8,128)(2,1)S(1)} %get-tuple-element.34), channel_id=1, source_target_pairs={{0,8},{1,9},{2,10},{3,11},{4,12},{5,13},{6,14},{7,15},{8,0},{9,1},... | collective-permute-start | bytes 294920 | tf_op jit(solution)/shard_map/ppermute | solution.py:299
  20.4 1.4 %collective-permute-start.10 = (bf16[2,32,768]{2,1,0:T(8,128)(2,1)S(1)}, bf16[2,32,768]{2,1,0:T(8,128)(2,1)S(1)}, u32[]{:S(2)}, u32[]{:S(2)}) collective-permute-start(bf16[2,32,768]{2,1,0:T(8,128)(2,1)S(1)} %get-tuple-element.34), channel_id=1, source_target_pairs={{0,12},{1,13},{2,14},{3,15},{4,8},{5,9},{6,10},{7,11},{8,4},{9,5},... | collective-permute-start | bytes 294920 | tf_op jit(solution)/shard_map/ppermute | solution.py:299
  23.1 5.1 %collective-permute-done.9 = bf16[2,32,768]{2,1,0:T(8,128)(2,1)S(1)} collective-permute-done((bf16[2,32,768]{2,1,0:T(8,128)(2,1)S(1)}, bf16[2,32,768]{2,1,0:T(8,128)(2,1)S(1)}, u32[]{:S(2)}, u32[]{:S(2)}) %collective-permute-start.9) | collective-permute-done | bytes 98336 | tf_op jit(solution)/shard_map/ppermute | solution.py:299
  28.2 0.8 pad_maximum_fusion.refs_4_
  29.5 1.4 %collective-permute-done.4.refs_1_ = bf16[4,32,768]{2,1,0:T(8,128)(2,1)} collective-permute-done((bf16[4,32,768]{2,1,0:T(8,128)(2,1)S(1)}, bf16[4,32,768]{2,1,0:T(8,128)(2,1)}, u32[]{:S(2)}, u32[]{:S(2)}) %collective-permute-start.4) | collective-permute-done | bytes 196640 | tf_op jit(solution)/shard_map/ppermute | solution.py:299
  32.9 9.8 %bra_transform.1 = (bf16[512,128]{1,0:T(8,128)(2,1)S(1)}, bf16[512,128]{1,0:T(8,128)(2,1)S(1)}, bf16[512,128]{1,0:T(8,128)(2,1)S(1)}, bf16[512,128]{1,0:T(8,128)...) custom-call(s32[1]{0:T(128)} %bitcast.me_ref, ...), custom_call_target="tpu_custom_call" | custom-call | flops 2684354560 | bytes 8388608 | tf_op jit(solution)/shard_map/bra_transform/pallas_call | solution.py:211
  43.4 2.0 %collective-permute-start.17 = (bf16[512,128]{1,0:T(8,128)(2,1)S(1)}, bf16[512,128]{1,0:T(8,128)(2,1)S(1)}, u32[]{:S(2)}, u32[]{:S(2)}) collective-permute-start(bf16[512,128]{1,0:T(8,128)(2,1)S(1)} %get-tuple-element.25), channel_id=1, source_target_pairs={{0,2},{1,3},{2,0},{3,1},{4,6},{5,7},{6,4},{7,5},{8,10},{9,11},{10,... | collective-permute-start | bytes 393224 | tf_op jit(solution)/shard_map/ppermute | solution.py:299
  45.5 2.0 %collective-permute-start.15 = (bf16[512,256]{1,0:T(8,128)(2,1)S(1)}, bf16[512,256]{1,0:T(8,128)(2,1)S(1)}, u32[]{:S(2)}, u32[]{:S(2)}) collective-permute-start(bf16[512,256]{1,0:T(8,128)(2,1)S(1)} %get-tuple-element.23), channel_id=1, source_target_pairs={{0,2},{1,3},{2,0},{3,1},{4,6},{5,7},{6,4},{7,5},{8,10},{9,11},{10,... | collective-permute-start | bytes 786440 | tf_op jit(solution)/shard_map/ppermute | solution.py:299
  47.4 2.3 %collective-permute-done.13 = bf16[512,128]{1,0:T(8,128)(2,1)S(1)} collective-permute-done((bf16[512,128]{1,0:T(8,128)(2,1)S(1)}, bf16[512,128]{1,0:T(8,128)(2,1)S(1)}, u32[]{:S(2)}, u32[]{:S(2)}) %collective-permute-start.13) | collective-permute-done | bytes 131104 | tf_op jit(solution)/shard_map/ppermute | solution.py:299
  49.8 4.5 %collective-permute-start.18 = (bf16[512,128]{1,0:T(8,128)(2,1)S(1)}, bf16[512,128]{1,0:T(8,128)(2,1)S(1)}, u32[]{:S(2)}, u32[]{:S(2)}) collective-permute-start(bf16[512,128]{1,0:T(8,128)(2,1)S(1)} %add_convert_fusion.5), channel_id=1, source_target_pairs={{0,4},{1,5},{2,6},{3,7},{4,0},{5,1},{6,2},{7,3},{8,12},{9,13},{10,... | collective-permute-start | bytes 393224 | tf_op jit(solution)/shard_map/ppermute | solution.py:299
  56.7 3.1 %collective-permute-start.22 = (bf16[512,128]{1,0:T(8,128)(2,1)S(1)}, bf16[512,128]{1,0:T(8,128)(2,1)S(1)}, u32[]{:S(2)}, u32[]{:S(2)}) collective-permute-start(bf16[512,128]{1,0:T(8,128)(2,1)S(1)} %add_convert_fusion.3), channel_id=1, source_target_pairs={{0,4},{1,5},{2,6},{3,7},{4,0},{5,1},{6,2},{7,3},{8,12},{9,13},{10,... | collective-permute-start | bytes 393224 | tf_op jit(solution)/shard_map/ppermute | solution.py:299
  61.9 5.1 %collective-permute-start.19 = (bf16[512,128]{1,0:T(8,128)(2,1)}, bf16[512,128]{1,0:T(8,128)(2,1)S(1)}, u32[]{:S(2)}, u32[]{:S(2)}) collective-permute-start(bf16[512,128]{1,0:T(8,128)(2,1)} %add_convert_fusion.4), channel_id=1, source_target_pairs={{0,8},{1,9},{2,10},{3,11},{4,12},{5,13},{6,14},{7,15},{8,0},{9,1},... | collective-permute-start | bytes 393224 | tf_op jit(solution)/shard_map/ppermute | solution.py:299
  66.9 0.8 add_convert_fusion.1
  67.7 2.0 %collective-permute-start.16 = (bf16[512,256]{1,0:T(8,128)(2,1)}, bf16[512,256]{1,0:T(8,128)(2,1)}, u32[]{:S(2)}, u32[]{:S(2)}) collective-permute-start(bf16[512,256]{1,0:T(8,128)(2,1)} %add_convert_fusion.1), channel_id=1, source_target_pairs={{0,4},{1,5},{2,6},{3,7},{4,0},{5,1},{6,2},{7,3},{8,12},{9,13},{10,... | collective-permute-start | bytes 786440 | tf_op jit(solution)/shard_map/ppermute | solution.py:299
  70.4 2.0 %collective-permute-start.23 = (bf16[512,128]{1,0:T(8,128)(2,1)}, bf16[512,128]{1,0:T(8,128)(2,1)}, u32[]{:S(2)}, u32[]{:S(2)}) collective-permute-start(bf16[512,128]{1,0:T(8,128)(2,1)} %add_convert_fusion.2), channel_id=1, source_target_pairs={{0,8},{1,9},{2,10},{3,11},{4,12},{5,13},{6,14},{7,15},{8,0},{9,1},... | collective-permute-start | bytes 393224 | tf_op jit(solution)/shard_map/ppermute | solution.py:299
  72.4 5.2 %collective-permute-done.23 = bf16[512,128]{1,0:T(8,128)(2,1)} collective-permute-done((bf16[512,128]{1,0:T(8,128)(2,1)}, bf16[512,128]{1,0:T(8,128)(2,1)}, u32[]{:S(2)}, u32[]{:S(2)}) %collective-permute-start.23) | collective-permute-done | bytes 131104 | tf_op jit(solution)/shard_map/ppermute | solution.py:299
  78.4 1.3 %add_convert_fusion = bf16[512,256]{1,0:T(8,128)(2,1)S(1)} fusion(bf16[512,256]{1,0:T(8,128)(2,1)} %collective-permute-done.16, bf16[512,256]{1,0:T(8,128)(2,1)} %collective-permute-done.14, bf16[512,256]{1,0:T(8,128)(2,1)} %copy-done.2, bf16[512,128]{1,0:T(8,128)(2,1)} %collective-permute-done.23, bf16[512,128]{1,0:T(8,128)(2,1)S(1)} %collective-permute-done.19), kind=kLoop, calls=%fused_computation.1 | loop fusion | flops 1441792 | bytes 1310720 | tf_op jit(solution)/shard_map/convert_element_type | solution.py:306
  79.8 1.3 %collective-permute-done.24.other = bf16[256,256]{1,0:T(8,128)(2,1)S(1)} collective-permute-done((bf16[256,256]{1,0:T(8,128)(2,1)S(1)}, bf16[256,256]{1,0:T(8,128)(2,1)S(1)}, u32[]{:S(2)}, u32[]{:S(2)}) %collective-permute-start.24) | collective-permute-done | bytes 131104 | tf_op jit(solution)/shard_map/ppermute | solution.py:299
  81.1 2.8 %last_step.1 = f32[256,4096]{1,0:T(8,128)} custom-call(bf16[256,256]{1,0:T(8,128)(2,1)S(1)} %get-tuple-element.32.own, bf16[256,256]{1,0:T(8,128)(2,1)S(1)} %collective-permute-done.24.other, f32[2,4,64,128]{3,2,1,0:T(8,128)S(1)} %copy-done.1), custom_call_target="tpu_custom_call" | custom-call | tf_op jit(solution)/shard_map/last_step/pallas_call | solution.py:283
  (57 shorter events, 12.3 us)
Async XLA Ops:
  0.0 31.6 %collective-permute-start.12 = (bf16[40,512,128]{2,1,0:T(8,128)(2,1)}, bf16[40,512,128]{2,1,0:T(8,128)(2,1)}, u32[]{:S(2)}, u32[]{:S(2)}) collective-permute-start(bf16[40,512,128]{2,1,0:T(8,128)(2,1)} %refs_6_.1), channel_id=1, source_target_pairs={{0,1},{1,0},{2,3},{3,2},{4,5},{5,4},{6,7},{7,6},{8,9},{9,8},{10,11... | collective-permute-start | bytes 15728648 | tf_op jit(solution)/shard_map/ppermute | solution.py:299
  2.1 6.7 %collective-permute-start = (s32[81]{0:T(128)S(1)}, s32[81]{0:T(128)S(1)}, u32[]{:S(2)}, u32[]{:S(2)}) collective-permute-start(s32[81]{0:T(128)S(1)} %pad_add_fusion.mine), channel_id=1, source_target_pairs={{0,1},{1,0},{2,3},{3,2},{4,5},{5,4},{6,7},{7,6},{8,9},{9,8},{10,11... | collective-permute-start | bytes 980 | tf_op jit(solution)/shard_map/ppermute | solution.py:299
  8.8 7.3 %collective-permute-start.7 = (bf16[32,768]{1,0:T(8,128)(2,1)S(1)}, bf16[32,768]{1,0:T(8,128)(2,1)S(1)}, u32[]{:S(2)}, u32[]{:S(2)}) collective-permute-start(bf16[32,768]{1,0:T(8,128)(2,1)S(1)} %get-tuple-element.37), channel_id=1, source_target_pairs={{0,2},{1,3},{2,0},{3,1},{4,6},{5,7},{6,4},{7,5},{8,10},{9,11},{10,... | collective-permute-start | bytes 147464 | tf_op jit(solution)/shard_map/ppermute | solution.py:299
  11.7 5.2 %collective-permute-start.1 = (bf16[32,768]{1,0:T(8,128)(2,1)S(1)}, bf16[32,768]{1,0:T(8,128)(2,1)S(1)}, u32[]{:S(2)}, u32[]{:S(2)}) collective-permute-start(bf16[32,768]{1,0:T(8,128)(2,1)S(1)} %get-tuple-element.38), channel_id=1, source_target_pairs={{0,4},{1,5},{2,6},{3,7},{4,0},{5,1},{6,2},{7,3},{8,12},{9,13},{10,... | collective-permute-start | bytes 147464 | tf_op jit(solution)/shard_map/ppermute | solution.py:299
  13.3 7.1 %collective-permute-start.2 = (bf16[32,768]{1,0:T(8,128)(2,1)S(1)}, bf16[32,768]{1,0:T(8,128)(2,1)S(1)}, u32[]{:S(2)}, u32[]{:S(2)}) collective-permute-start(bf16[32,768]{1,0:T(8,128)(2,1)S(1)} %get-tuple-element.38), channel_id=1, source_target_pairs={{0,8},{1,9},{2,10},{3,11},{4,12},{5,13},{6,14},{7,15},{8,0},{9,1},... | collective-permute-start | bytes 147464 | tf_op jit(solution)/shard_map/ppermute | solution.py:299
  15.9 6.6 %collective-permute-start.3 = (bf16[32,768]{1,0:T(8,128)(2,1)S(1)}, bf16[32,768]{1,0:T(8,128)(2,1)S(1)}, u32[]{:S(2)}, u32[]{:S(2)}) collective-permute-start(bf16[32,768]{1,0:T(8,128)(2,1)S(1)} %get-tuple-element.38), channel_id=1, source_target_pairs={{0,12},{1,13},{2,14},{3,15},{4,8},{5,9},{6,10},{7,11},{8,4},{9,5},... | collective-permute-start | bytes 147464 | tf_op jit(solution)/shard_map/ppermute | solution.py:299
  16.1 7.0 %collective-permute-start.8 = (bf16[2,32,768]{2,1,0:T(8,128)(2,1)S(1)}, bf16[2,32,768]{2,1,0:T(8,128)(2,1)S(1)}, u32[]{:S(2)}, u32[]{:S(2)}) collective-permute-start(bf16[2,32,768]{2,1,0:T(8,128)(2,1)S(1)} %get-tuple-element.34), channel_id=1, source_target_pairs={{0,4},{1,5},{2,6},{3,7},{4,0},{5,1},{6,2},{7,3},{8,12},{9,13},{10,... | collective-permute-start | bytes 294920 | tf_op jit(solution)/shard_map/ppermute | solution.py:299
  16.9 11.3 %collective-permute-start.9 = (bf16[2,32,768]{2,1,0:T(8,128)(2,1)S(1)}, bf16[2,32,768]{2,1,0:T(8,128)(2,1)S(1)}, u32[]{:S(2)}, u32[]{:S(2)}) collective-permute-start(bf16[2,32,768]{2,1,0:T(8,128)(2,1)S(1)} %get-tuple-element.34), channel_id=1, source_target_pairs={{0,8},{1,9},{2,10},{3,11},{4,12},{5,13},{6,14},{7,15},{8,0},{9,1},... | collective-permute-start | bytes 294920 | tf_op jit(solution)/shard_map/ppermute | solution.py:299
  20.4 7.8 %collective-permute-start.10 = (bf16[2,32,768]{2,1,0:T(8,128)(2,1)S(1)}, bf16[2,32,768]{2,1,0:T(8,128)(2,1)S(1)}, u32[]{:S(2)}, u32[]{:S(2)}) collective-permute-start(bf16[2,32,768]{2,1,0:T(8,128)(2,1)S(1)} %get-tuple-element.34), channel_id=1, source_target_pairs={{0,12},{1,13},{2,14},{3,15},{4,8},{5,9},{6,10},{7,11},{8,4},{9,5},... | collective-permute-start | bytes 294920 | tf_op jit(solution)/shard_map/ppermute | solution.py:299
  22.5 7.0 %collective-permute-start.5 = (bf16[4,32,768]{2,1,0:T(8,128)(2,1)S(1)}, bf16[4,32,768]{2,1,0:T(8,128)(2,1)S(1)}, u32[]{:S(2)}, u32[]{:S(2)}) collective-permute-start(bf16[4,32,768]{2,1,0:T(8,128)(2,1)S(1)} %pad_maximum_fusion.1.refs_0_), channel_id=1, source_target_pairs={{0,2},{1,3},{2,0},{3,1},{4,6},{5,7},{6,4},{7,5},{8,10},{9,11},{10,... | collective-permute-start | bytes 589832 | tf_op jit(solution)/shard_map/ppermute | solution.py:299
  29.0 2.6 %collective-permute-start.11 = (bf16[4,2,32,768]{3,2,1,0:T(8,128)(2,1)}, bf16[4,2,32,768]{3,2,1,0:T(8,128)(2,1)}, u32[]{:S(2)}, u32[]{:S(2)}) collective-permute-start(bf16[4,2,32,768]{3,2,1,0:T(8,128)(2,1)} %pad_maximum_fusion.refs_4_), channel_id=1, source_target_pairs={{0,1},{1,0},{2,3},{3,2},{4,5},{5,4},{6,7},{7,6},{8,9},{9,8},{10,11... | collective-permute-start | bytes 1179656 | tf_op jit(solution)/shard_map/ppermute | solution.py:299
  29.0 1.9 %collective-permute-start.4 = (bf16[4,32,768]{2,1,0:T(8,128)(2,1)S(1)}, bf16[4,32,768]{2,1,0:T(8,128)(2,1)}, u32[]{:S(2)}, u32[]{:S(2)}) collective-permute-start(bf16[4,32,768]{2,1,0:T(8,128)(2,1)S(1)} %pad_maximum_fusion.1.refs_0_), channel_id=1, source_target_pairs={{0,1},{1,0},{2,3},{3,2},{4,5},{5,4},{6,7},{7,6},{8,9},{9,8},{10,11... | collective-permute-start | bytes 589832 | tf_op jit(solution)/shard_map/ppermute | solution.py:299
  29.5 1.9 %collective-permute-start.6 = (bf16[4,32,768]{2,1,0:T(8,128)(2,1)S(1)}, bf16[4,32,768]{2,1,0:T(8,128)(2,1)}, u32[]{:S(2)}, u32[]{:S(2)}) collective-permute-start(bf16[4,32,768]{2,1,0:T(8,128)(2,1)S(1)} %collective-permute-done.5.refs_2_), channel_id=1, source_target_pairs={{0,1},{1,0},{2,3},{3,2},{4,5},{5,4},{6,7},{7,6},{8,9},{9,8},{10,11... | collective-permute-start | bytes 589832 | tf_op jit(solution)/shard_map/ppermute | solution.py:299
  43.4 6.3 %collective-permute-start.13 = (bf16[512,128]{1,0:T(8,128)(2,1)S(1)}, bf16[512,128]{1,0:T(8,128)(2,1)S(1)}, u32[]{:S(2)}, u32[]{:S(2)}) collective-permute-start(bf16[512,128]{1,0:T(8,128)(2,1)S(1)} %get-tuple-element.21), channel_id=1, source_target_pairs={{0,2},{1,3},{2,0},{3,1},{4,6},{5,7},{6,4},{7,5},{8,10},{9,11},{10,... | collective-permute-start | bytes 393224 | tf_op jit(solution)/shard_map/ppermute | solution.py:299
  43.4 17.2 %collective-permute-start.17 = (bf16[512,128]{1,0:T(8,128)(2,1)S(1)}, bf16[512,128]{1,0:T(8,128)(2,1)S(1)}, u32[]{:S(2)}, u32[]{:S(2)}) collective-permute-start(bf16[512,128]{1,0:T(8,128)(2,1)S(1)} %get-tuple-element.25), channel_id=1, source_target_pairs={{0,2},{1,3},{2,0},{3,1},{4,6},{5,7},{6,4},{7,5},{8,10},{9,11},{10,... | collective-permute-start | bytes 393224 | tf_op jit(solution)/shard_map/ppermute | solution.py:299
  45.4 11.3 %collective-permute-start.21 = (bf16[512,128]{1,0:T(8,128)(2,1)S(1)}, bf16[512,128]{1,0:T(8,128)(2,1)S(1)}, u32[]{:S(2)}, u32[]{:S(2)}) collective-permute-start(bf16[512,128]{1,0:T(8,128)(2,1)S(1)} %get-tuple-element.29), channel_id=1, source_target_pairs={{0,2},{1,3},{2,0},{3,1},{4,6},{5,7},{6,4},{7,5},{8,10},{9,11},{10,... | collective-permute-start | bytes 393224 | tf_op jit(solution)/shard_map/ppermute | solution.py:299
  45.5 21.5 %collective-permute-start.15 = (bf16[512,256]{1,0:T(8,128)(2,1)S(1)}, bf16[512,256]{1,0:T(8,128)(2,1)S(1)}, u32[]{:S(2)}, u32[]{:S(2)}) collective-permute-start(bf16[512,256]{1,0:T(8,128)(2,1)S(1)} %get-tuple-element.23), channel_id=1, source_target_pairs={{0,2},{1,3},{2,0},{3,1},{4,6},{5,7},{6,4},{7,5},{8,10},{9,11},{10,... | collective-permute-start | bytes 786440 | tf_op jit(solution)/shard_map/ppermute | solution.py:299
  49.8 11.4 %collective-permute-start.18 = (bf16[512,128]{1,0:T(8,128)(2,1)S(1)}, bf16[512,128]{1,0:T(8,128)(2,1)S(1)}, u32[]{:S(2)}, u32[]{:S(2)}) collective-permute-start(bf16[512,128]{1,0:T(8,128)(2,1)S(1)} %add_convert_fusion.5), channel_id=1, source_target_pairs={{0,4},{1,5},{2,6},{3,7},{4,0},{5,1},{6,2},{7,3},{8,12},{9,13},{10,... | collective-permute-start | bytes 393224 | tf_op jit(solution)/shard_map/ppermute | solution.py:299
  56.1 13.7 %collective-permute-start.20 = (bf16[512,128]{1,0:T(8,128)(2,1)S(1)}, bf16[512,128]{1,0:T(8,128)(2,1)S(1)}, u32[]{:S(2)}, u32[]{:S(2)}) collective-permute-start(bf16[512,128]{1,0:T(8,128)(2,1)S(1)} %broadcast_add_fusion.1), channel_id=1, source_target_pairs={{0,2},{1,3},{2,0},{3,1},{4,6},{5,7},{6,4},{7,5},{8,10},{9,11},{10,... | collective-permute-start | bytes 393224 | tf_op jit(solution)/shard_map/ppermute | solution.py:299
  56.7 13.0 %collective-permute-start.22 = (bf16[512,128]{1,0:T(8,128)(2,1)S(1)}, bf16[512,128]{1,0:T(8,128)(2,1)S(1)}, u32[]{:S(2)}, u32[]{:S(2)}) collective-permute-start(bf16[512,128]{1,0:T(8,128)(2,1)S(1)} %add_convert_fusion.3), channel_id=1, source_target_pairs={{0,4},{1,5},{2,6},{3,7},{4,0},{5,1},{6,2},{7,3},{8,12},{9,13},{10,... | collective-permute-start | bytes 393224 | tf_op jit(solution)/shard_map/ppermute | solution.py:299
  60.6 17.1 %collective-permute-start.14 = (bf16[512,256]{1,0:T(8,128)(2,1)}, bf16[512,256]{1,0:T(8,128)(2,1)}, u32[]{:S(2)}, u32[]{:S(2)}) collective-permute-start(bf16[512,256]{1,0:T(8,128)(2,1)} %broadcast_add_fusion), channel_id=1, source_target_pairs={{0,2},{1,3},{2,0},{3,1},{4,6},{5,7},{6,4},{7,5},{8,10},{9,11},{10,... | collective-permute-start | bytes 786440 | tf_op jit(solution)/shard_map/ppermute | solution.py:299
  61.9 10.6 %collective-permute-start.19 = (bf16[512,128]{1,0:T(8,128)(2,1)}, bf16[512,128]{1,0:T(8,128)(2,1)S(1)}, u32[]{:S(2)}, u32[]{:S(2)}) collective-permute-start(bf16[512,128]{1,0:T(8,128)(2,1)} %add_convert_fusion.4), channel_id=1, source_target_pairs={{0,8},{1,9},{2,10},{3,11},{4,12},{5,13},{6,14},{7,15},{8,0},{9,1},... | collective-permute-start | bytes 393224 | tf_op jit(solution)/shard_map/ppermute | solution.py:299
  67.7 10.7 %collective-permute-start.16 = (bf16[512,256]{1,0:T(8,128)(2,1)}, bf16[512,256]{1,0:T(8,128)(2,1)}, u32[]{:S(2)}, u32[]{:S(2)}) collective-permute-start(bf16[512,256]{1,0:T(8,128)(2,1)} %add_convert_fusion.1), channel_id=1, source_target_pairs={{0,4},{1,5},{2,6},{3,7},{4,0},{5,1},{6,2},{7,3},{8,12},{9,13},{10,... | collective-permute-start | bytes 786440 | tf_op jit(solution)/shard_map/ppermute | solution.py:299
  70.4 7.2 %collective-permute-start.23 = (bf16[512,128]{1,0:T(8,128)(2,1)}, bf16[512,128]{1,0:T(8,128)(2,1)}, u32[]{:S(2)}, u32[]{:S(2)}) collective-permute-start(bf16[512,128]{1,0:T(8,128)(2,1)} %add_convert_fusion.2), channel_id=1, source_target_pairs={{0,8},{1,9},{2,10},{3,11},{4,12},{5,13},{6,14},{7,15},{8,0},{9,1},... | collective-permute-start | bytes 393224 | tf_op jit(solution)/shard_map/ppermute | solution.py:299
  (6 other events, 44.0 us)

commit v4 on v3

--- a/solution.py
+++ b/solution.py
@@ -37,7 +37,7 @@
     ]
 
 
-def bra_kernel(regions, locate, chunk, pieces, me_ref, mine, theirs, firsts, seconds, *refs):
+def bra_kernel(regions, locate, chunk, pieces, me_ref, mine, theirs, *refs):
     parts, refs = refs[: len(regions)], refs[len(regions) :]
     own, other = refs[:2]
     outs, ket = refs[2 : 2 + len(pieces)], refs[2 + len(pieces)]
@@ -88,9 +88,9 @@
     count = ket.shape[1]
     for n in range(count):
         kb = (n + (me & 1) * (count // 2)) & (count - 1)
-        piece = table_piece(table, locate(firsts[kb] * 2, me), 0)
+        piece = table_piece(table, locate(mine[2 * capacity + 1 + kb] * 2, me), 0)
         ket[0, n] = jnp.dot(piece.astype(BF), spread_a, preferred_element_type=F32)
-        piece = table_piece(table, locate(seconds[kb], me), 0)
+        piece = table_piece(table, locate(mine[2 * capacity + 1 + count + kb], me), 0)
         ket[1, n] = jnp.dot(piece.astype(BF), spread("b"), preferred_element_type=F32)
 
     cover = 8 * STEP
@@ -201,7 +201,7 @@
 
 
 def bra_transform(
-    regions, locate, parts, own, other, numbers, ket_numbers, me, orbitals, chunk, pieces, kind
+    regions, locate, parts, own, other, numbers, me, orbitals, chunk, pieces, kind
 ):
     capacity, kp, pair = own.shape
     kh = kp // 2
@@ -213,7 +213,7 @@
         out_shape=[jax.ShapeDtypeStruct((rows, high - low), kind) for _, low, high in pieces]
         + [jax.ShapeDtypeStruct((2, kp // LANES, orbitals, LANES), F32)],
         grid_spec=pltpu.PrefetchScalarGridSpec(
-            num_scalar_prefetch=5,
+            num_scalar_prefetch=3,
             grid=(),
             in_specs=[hbm] * (len(parts) + 2),
             out_specs=[hbm] * len(pieces) + [pl.BlockSpec(memory_space=pltpu.VMEM)],
@@ -237,7 +237,7 @@
             flops=4 * capacity * 8 * orbitals * pair * kh, bytes_accessed=8 * 2**20, transcendentals=0
         ),
         name="bra_transform",
-    )(me, *numbers, *ket_numbers, *parts, own, other)
+    )(me, *numbers, *parts, own, other)
 
 
 def table_shape(parts, orbitals):
@@ -306,7 +306,7 @@
     return result.astype(BF)
 
 
-def gather_small(mine, count):
+def gather_small(mine, numbers, other, count):
     middle = mine.shape[0] // 2
     a, b = mine[:middle], mine[middle:]
     b_x = permute(b, 2, count)
@@ -315,7 +315,10 @@
     b_z = {s: permute(b_pair, 4 * s, count) for s in (3, 2, 1)}
     near = jnp.stack([a, a_z[1], a_z[2], a_z[3]])
     far = permute(near, 2, count)
-    rest = jnp.stack([b_pair, b_z[1], b_z[2], b_z[3]])
+    late = (other[0, 0, 0] != other[0, 0, 0]).astype(jnp.int32)
+    other_numbers = permute(numbers + late, 1, count)
+    nothing = (other_numbers[0] < 0).astype(BF)
+    rest = jnp.stack([b_pair, b_z[1], b_z[2], b_z[3]]) + nothing
     upper, lower = pl.ds(0, middle), pl.ds(middle, middle)
     everything = slice(None)
     parts, regions = [], []
@@ -326,7 +329,7 @@
     for core in range(2):
         parts.append(permute(rest, 1, count) if core else rest)
         regions.append((core, everything, everything, lower))
-    return parts, regions
+    return parts, regions, other_numbers
 
 
 def shards(
@@ -340,10 +343,10 @@
     own_ao, nmo = coefficients.shape
     swap = functools.partial(permute, mask=1, count=count)
 
-    numbers = jnp.concatenate([first_block, second_block, slot_counts])
-    other_numbers = swap(numbers)
-    nothing = (other_numbers[0] < 0).astype(BF)
-    mine = coefficients.T.at[mo_index].get(mode="promise_in_bounds") + nothing
+    numbers = jnp.concatenate([first_block, second_block, slot_counts, ket_first, ket_second])
+    mine = coefficients.T.at[mo_index].get(
+        mode="promise_in_bounds", wrap_negative_indices=False
+    )
     orbitals = mine.shape[0]
 
     units = own_ao // 8
@@ -353,13 +356,14 @@
     small = count == 16 and own_ao % 16 == 0
     if small:
         mine = jnp.pad(mine, ((0, 0), (0, -own_ao % LANES)))
-        parts, regions = gather_small(mine, count)
+        parts, regions, other_numbers = gather_small(mine, numbers, other, count)
 
         def locate(unit, me):
             owner = (unit * factor) >> 20
             away = owner ^ me
             return away & 1, away >> 2, (away >> 1) & 1, (unit - owner * units) * 8
     else:
+        other_numbers = swap(numbers)
         parts = [lax.all_gather(mine, "pan", axis=1, tiled=True)]
         regions = [(0, 0, 0)]
 
@@ -374,7 +378,6 @@
         blocks,
         other,
         (numbers, other_numbers),
-        (ket_first, ket_second),
         me_array,
         orbitals,
     )

time: 83 us -> 77.7 us (0.936); the launches traced: 84.1 us -> 77.4 us
  starting transfers between devices: 36.5 us -> 23.1 us
  Pallas kernels: 12.5 us -> 15.2 us
  waiting for transfers between devices: 22.7 us -> 25 us
  local copies, waits for them, and re-layouts: 3.26 us -> 4.48 us
  between operations: 2.51 us -> 3.61 us
    ppermute x25, starting transfers between devices: 36.5 us -> 23.1 us  [permute(): return lax.ppermute(array, 'pan', [(i, i ^ mask) for i in range(count)])]
    pallas_call x1, Pallas kernels: 9.77 us -> 12.4 us  [bra_transform(): pl.pallas_call(functools.partial(bra_kernel, regions, locate, chunk, piec...]
    ppermute x25, waiting for transfers between devices: 22.7 us -> 25 us  [permute(): return lax.ppermute(array, 'pan', [(i, i ^ mask) for i in range(count)])]
    slice x0 -> x1, local copies, waits for them, and re-layouts: none -> 1.19 us  [gather_small(): late = (other[0, 0, 0] != other[0, 0, 0]).astype(jnp.int32)]
    gather x1, other arithmetic: 0.01 us -> 0.89 us  [shards(): coefficients.T.at[mo_index]]
    unnamed x10 -> x6, local copies, waits for them, and re-layouts: 2 us -> 1.24 us
  transfers between devices with their start and end apart: 25 -> 25, of which waited for: 10 -> 13; matrix products, arithmetic and copies ran while one was open for 8% -> 10% of each run, Pallas kernels for 0% -> 0%
where the time goes in v4:
time: 77.7 us; the launch traced here: 77.4 us
  waiting for transfers between devices  25 us (32%)
  starting transfers between devices  23.1 us (30%)
  Pallas kernels  15.2 us (20%)
  other arithmetic  6.01 us (8%)
  local copies, waits for them, and re-layouts  4.48 us (6%)
  between operations  3.61 us (5%)
    ppermute x25, waiting for transfers between devices, permute(): return lax.ppermute(array, 'pan', [(i, i ^ mask) for i in range(count)])  25 us
    ppermute x25, starting transfers between devices, permute(): return lax.ppermute(array, 'pan', [(i, i ^ mask) for i in range(count)])  23.1 us
    pallas_call x1, Pallas kernels, bra_transform(): pl.pallas_call(functools.partial(bra_kernel, regions, locate, chunk, piec...  12.4 us
    convert_element_type x6, other arithmetic, added(): return result.astype(BF)  3.53 us
    pallas_call x1, Pallas kernels, last_step(): pl.pallas_call(last_kernel, out_shape=jax.ShapeDtypeStruct((rows, orbital...  2.77 us
  transfers between devices with their start and end apart: 25, of which 13 were waited for; matrix products, arithmetic and copies ran while one was open for 10% of the time, Pallas kernels for 0%

profile of v4, /device:TPU:0, one launch (start us, length us, event | category | flops | bytes accessed | tf_op | source)
XLA Modules:
  0.0 77.4 jit_solution(10740989676319695669)
XLA Ops:
  0.5 0.9 %pad_clamp_fusion = s32[1024]{0:T(1024)S(1)} fusion(s32[64]{0:T(128)} %param.15), kind=kLoop, calls=%fused_computation.14 | loop fusion | flops 1024 | bytes 4352 | tf_op jit(solution)/shard_map/gather | solution.py:347
  2.6 3.0 %collective-permute-start.8 = (bf16[32,768]{1,0:T(8,128)(2,1)S(1)}, bf16[32,768]{1,0:T(8,128)(2,1)S(1)}, u32[]{:S(2)}, u32[]{:S(2)}) collective-permute-start(bf16[32,768]{1,0:T(8,128)(2,1)S(1)} %get-tuple-element.37), channel_id=1, source_target_pairs={{0,2},{1,3},{2,0},{3,1},{4,6},{5,7},{6,4},{7,5},{8,10},{9,11},{10,... | collective-permute-start | bytes 147464 | tf_op jit(solution)/shard_map/ppermute | solution.py:299
  5.6 1.6 %collective-permute-start.2 = (bf16[32,768]{1,0:T(8,128)(2,1)S(1)}, bf16[32,768]{1,0:T(8,128)(2,1)S(1)}, u32[]{:S(2)}, u32[]{:S(2)}) collective-permute-start(bf16[32,768]{1,0:T(8,128)(2,1)S(1)} %get-tuple-element.38), channel_id=1, source_target_pairs={{0,4},{1,5},{2,6},{3,7},{4,0},{5,1},{6,2},{7,3},{8,12},{9,13},{10,... | collective-permute-start | bytes 147464 | tf_op jit(solution)/shard_map/ppermute | solution.py:299
  7.2 2.6 %collective-permute-start.3 = (bf16[32,768]{1,0:T(8,128)(2,1)S(1)}, bf16[32,768]{1,0:T(8,128)(2,1)S(1)}, u32[]{:S(2)}, u32[]{:S(2)}) collective-permute-start(bf16[32,768]{1,0:T(8,128)(2,1)S(1)} %get-tuple-element.38), channel_id=1, source_target_pairs={{0,8},{1,9},{2,10},{3,11},{4,12},{5,13},{6,14},{7,15},{8,0},{9,1},... | collective-permute-start | bytes 147464 | tf_op jit(solution)/shard_map/ppermute | solution.py:299
  12.2 3.5 %collective-permute-start.10 = (bf16[2,32,768]{2,1,0:T(8,128)(2,1)S(1)}, bf16[2,32,768]{2,1,0:T(8,128)(2,1)S(1)}, u32[]{:S(2)}, u32[]{:S(2)}) collective-permute-start(bf16[2,32,768]{2,1,0:T(8,128)(2,1)S(1)} %get-tuple-element.34), channel_id=1, source_target_pairs={{0,8},{1,9},{2,10},{3,11},{4,12},{5,13},{6,14},{7,15},{8,0},{9,1},... | collective-permute-start | bytes 294920 | tf_op jit(solution)/shard_map/ppermute | solution.py:299
  15.7 1.2 %slice.24 = bf16[1,1,1]{2,1,0:T(2,128)(2,1)} slice(bf16[40,512,128]{2,1,0:T(8,128)(2,1)} %collective-permute-done.refs_7_), slice={[0:1], [0:1], [0:1]} | slice | bytes 4 | tf_op jit(solution)/shard_map/slice | solution.py:318
  19.8 4.9 %collective-permute-done.11 = bf16[2,32,768]{2,1,0:T(8,128)(2,1)S(1)} collective-permute-done((bf16[2,32,768]{2,1,0:T(8,128)(2,1)S(1)}, bf16[2,32,768]{2,1,0:T(8,128)(2,1)S(1)}, u32[]{:S(2)}, u32[]{:S(2)}) %collective-permute-start.11) | collective-permute-done | bytes 98336 | tf_op jit(solution)/shard_map/ppermute | solution.py:299
  24.7 0.8 %maximum_add_fusion.refs_4_ = bf16[4,2,32,768]{3,2,1,0:T(8,128)(2,1)} fusion(bf16[1,2,32,768]{3,2,1,0:T(8,128)(2,1)S(1)} %bitcast.23, bf16[1,2,32,768]{3,2,1,0:T(8,128)(2,1)S(1)} %bitcast.22, bf16[1,2,32,768]{3,2,1,0:T(8,128)(2,1)S(1)} %bitcast.21, bf16[1,2,32,768]{3,2,1,0:T(8,128)(2,1)S(1)} %get-tuple-element.33, bf16[]{:T(256)} %bitcast.13), kind=kLoop, calls=%fused_computation.3 | loop fusion | flops 786432 | bytes 786434 | tf_op jit(solution)/shard_map/add | solution.py:321
  26.0 1.4 %collective-permute-done.5.refs_1_ = bf16[4,32,768]{2,1,0:T(8,128)(2,1)} collective-permute-done((bf16[4,32,768]{2,1,0:T(8,128)(2,1)S(1)}, bf16[4,32,768]{2,1,0:T(8,128)(2,1)}, u32[]{:S(2)}, u32[]{:S(2)}) %collective-permute-start.5) | collective-permute-done | bytes 196640 | tf_op jit(solution)/shard_map/ppermute | solution.py:299
  28.1 12.4 %bra_transform.1 = (bf16[512,128]{1,0:T(8,128)(2,1)S(1)}, bf16[512,128]{1,0:T(8,128)(2,1)S(1)}, bf16[512,128]{1,0:T(8,128)(2,1)S(1)}, bf16[512,128]{1,0:T(8,128)...) custom-call(s32[1]{0:T(128)} %bitcast.me_ref, ...), custom_call_target="tpu_custom_call" | custom-call | flops 2684354560 | bytes 8388608 | tf_op jit(solution)/shard_map/bra_transform/pallas_call | solution.py:211
  41.3 2.3 %collective-permute-start.13 = (bf16[512,128]{1,0:T(8,128)(2,1)S(1)}, bf16[512,128]{1,0:T(8,128)(2,1)S(1)}, u32[]{:S(2)}, u32[]{:S(2)}) collective-permute-start(bf16[512,128]{1,0:T(8,128)(2,1)S(1)} %get-tuple-element.21), channel_id=1, source_target_pairs={{0,2},{1,3},{2,0},{3,1},{4,6},{5,7},{6,4},{7,5},{8,10},{9,11},{10,... | collective-permute-start | bytes 393224 | tf_op jit(solution)/shard_map/ppermute | solution.py:299
  43.6 2.0 %collective-permute-start.21 = (bf16[512,128]{1,0:T(8,128)(2,1)S(1)}, bf16[512,128]{1,0:T(8,128)(2,1)S(1)}, u32[]{:S(2)}, u32[]{:S(2)}) collective-permute-start(bf16[512,128]{1,0:T(8,128)(2,1)S(1)} %get-tuple-element.29), channel_id=1, source_target_pairs={{0,2},{1,3},{2,0},{3,1},{4,6},{5,7},{6,4},{7,5},{8,10},{9,11},{10,... | collective-permute-start | bytes 393224 | tf_op jit(solution)/shard_map/ppermute | solution.py:299
  45.6 2.2 %collective-permute-done.13 = bf16[512,128]{1,0:T(8,128)(2,1)S(1)} collective-permute-done((bf16[512,128]{1,0:T(8,128)(2,1)S(1)}, bf16[512,128]{1,0:T(8,128)(2,1)S(1)}, u32[]{:S(2)}, u32[]{:S(2)}) %collective-permute-start.13) | collective-permute-done | bytes 131104 | tf_op jit(solution)/shard_map/ppermute | solution.py:299
  49.8 2.1 %collective-permute-start.20 = (bf16[512,128]{1,0:T(8,128)(2,1)S(1)}, bf16[512,128]{1,0:T(8,128)(2,1)S(1)}, u32[]{:S(2)}, u32[]{:S(2)}) collective-permute-start(bf16[512,128]{1,0:T(8,128)(2,1)S(1)} %broadcast_add_fusion.1), channel_id=1, source_target_pairs={{0,2},{1,3},{2,0},{3,1},{4,6},{5,7},{6,4},{7,5},{8,10},{9,11},{10,... | collective-permute-start | bytes 393224 | tf_op jit(solution)/shard_map/ppermute | solution.py:299
  51.9 1.5 %collective-permute-done.21 = bf16[512,128]{1,0:T(8,128)(2,1)S(1)} collective-permute-done((bf16[512,128]{1,0:T(8,128)(2,1)S(1)}, bf16[512,128]{1,0:T(8,128)(2,1)S(1)}, u32[]{:S(2)}, u32[]{:S(2)}) %collective-permute-start.21) | collective-permute-done | bytes 131104 | tf_op jit(solution)/shard_map/ppermute | solution.py:299
  54.8 1.6 %collective-permute-start.14 = (bf16[512,256]{1,0:T(8,128)(2,1)}, bf16[512,256]{1,0:T(8,128)(2,1)}, u32[]{:S(2)}, u32[]{:S(2)}) collective-permute-start(bf16[512,256]{1,0:T(8,128)(2,1)} %broadcast_add_fusion), channel_id=1, source_target_pairs={{0,2},{1,3},{2,0},{3,1},{4,6},{5,7},{6,4},{7,5},{8,10},{9,11},{10,... | collective-permute-start | bytes 786440 | tf_op jit(solution)/shard_map/ppermute | solution.py:299
  57.1 2.0 %collective-permute-done.15 = bf16[512,256]{1,0:T(8,128)(2,1)S(1)} collective-permute-done((bf16[512,256]{1,0:T(8,128)(2,1)S(1)}, bf16[512,256]{1,0:T(8,128)(2,1)S(1)}, u32[]{:S(2)}, u32[]{:S(2)}) %collective-permute-start.15) | collective-permute-done | bytes 262176 | tf_op jit(solution)/shard_map/ppermute | solution.py:299
  59.9 2.0 %collective-permute-done.20 = bf16[512,128]{1,0:T(8,128)(2,1)S(1)} collective-permute-done((bf16[512,128]{1,0:T(8,128)(2,1)S(1)}, bf16[512,128]{1,0:T(8,128)(2,1)S(1)}, u32[]{:S(2)}, u32[]{:S(2)}) %collective-permute-start.20) | collective-permute-done | bytes 131104 | tf_op jit(solution)/shard_map/ppermute | solution.py:299
  62.6 0.9 %collective-permute-start.23 = (bf16[512,128]{1,0:T(8,128)(2,1)}, bf16[512,128]{1,0:T(8,128)(2,1)}, u32[]{:S(2)}, u32[]{:S(2)}) collective-permute-start(bf16[512,128]{1,0:T(8,128)(2,1)} %add_convert_fusion.2), channel_id=1, source_target_pairs={{0,8},{1,9},{2,10},{3,11},{4,12},{5,13},{6,14},{7,15},{8,0},{9,1},... | collective-permute-start | bytes 393224 | tf_op jit(solution)/shard_map/ppermute | solution.py:299
  63.5 6.7 %collective-permute-done.23 = bf16[512,128]{1,0:T(8,128)(2,1)} collective-permute-done((bf16[512,128]{1,0:T(8,128)(2,1)}, bf16[512,128]{1,0:T(8,128)(2,1)}, u32[]{:S(2)}, u32[]{:S(2)}) %collective-permute-start.23) | collective-permute-done | bytes 131104 | tf_op jit(solution)/shard_map/ppermute | solution.py:299
  70.2 1.6 %collective-permute-done.16 = bf16[512,256]{1,0:T(8,128)(2,1)} collective-permute-done((bf16[512,256]{1,0:T(8,128)(2,1)}, bf16[512,256]{1,0:T(8,128)(2,1)}, u32[]{:S(2)}, u32[]{:S(2)}) %collective-permute-start.16) | collective-permute-done | bytes 262176 | tf_op jit(solution)/shard_map/ppermute | solution.py:299
  71.8 1.3 %add_convert_fusion = bf16[512,256]{1,0:T(8,128)(2,1)S(1)} fusion(bf16[512,256]{1,0:T(8,128)(2,1)} %collective-permute-done.16, bf16[512,256]{1,0:T(8,128)(2,1)} %collective-permute-done.14, bf16[512,256]{1,0:T(8,128)(2,1)} %copy-done.2, bf16[512,128]{1,0:T(8,128)(2,1)} %collective-permute-done.23, bf16[512,128]{1,0:T(8,128)(2,1)S(1)} %collective-permute-done.19), kind=kLoop, calls=%fused_computation.1 | loop fusion | flops 1441792 | bytes 1310720 | tf_op jit(solution)/shard_map/convert_element_type | solution.py:306
  73.2 1.3 %collective-permute-done.24.other = bf16[256,256]{1,0:T(8,128)(2,1)S(1)} collective-permute-done((bf16[256,256]{1,0:T(8,128)(2,1)S(1)}, bf16[256,256]{1,0:T(8,128)(2,1)S(1)}, u32[]{:S(2)}, u32[]{:S(2)}) %collective-permute-start.24) | collective-permute-done | bytes 131104 | tf_op jit(solution)/shard_map/ppermute | solution.py:299
  74.5 2.8 %last_step.1 = f32[256,4096]{1,0:T(8,128)} custom-call(bf16[256,256]{1,0:T(8,128)(2,1)S(1)} %get-tuple-element.32.own, bf16[256,256]{1,0:T(8,128)(2,1)S(1)} %collective-permute-done.24.other, f32[2,4,64,128]{3,2,1,0:T(8,128)S(1)} %copy-done.1), custom_call_target="tpu_custom_call" | custom-call | tf_op jit(solution)/shard_map/last_step/pallas_call | solution.py:283
  (53 shorter events, 11.3 us)
Async XLA Ops:
  0.0 12.2 %collective-permute-start = (bf16[40,512,128]{2,1,0:T(8,128)(2,1)}, bf16[40,512,128]{2,1,0:T(8,128)(2,1)}, u32[]{:S(2)}, u32[]{:S(2)}) collective-permute-start(bf16[40,512,128]{2,1,0:T(8,128)(2,1)} %refs_6_.1), channel_id=1, source_target_pairs={{0,1},{1,0},{2,3},{3,2},{4,5},{5,4},{6,7},{7,6},{8,9},{9,8},{10,11... | collective-permute-start | bytes 15728648 | tf_op jit(solution)/shard_map/ppermute | solution.py:299
  2.6 8.8 %collective-permute-start.8 = (bf16[32,768]{1,0:T(8,128)(2,1)S(1)}, bf16[32,768]{1,0:T(8,128)(2,1)S(1)}, u32[]{:S(2)}, u32[]{:S(2)}) collective-permute-start(bf16[32,768]{1,0:T(8,128)(2,1)S(1)} %get-tuple-element.37), channel_id=1, source_target_pairs={{0,2},{1,3},{2,0},{3,1},{4,6},{5,7},{6,4},{7,5},{8,10},{9,11},{10,... | collective-permute-start | bytes 147464 | tf_op jit(solution)/shard_map/ppermute | solution.py:299
  5.6 12.6 %collective-permute-start.2 = (bf16[32,768]{1,0:T(8,128)(2,1)S(1)}, bf16[32,768]{1,0:T(8,128)(2,1)S(1)}, u32[]{:S(2)}, u32[]{:S(2)}) collective-permute-start(bf16[32,768]{1,0:T(8,128)(2,1)S(1)} %get-tuple-element.38), channel_id=1, source_target_pairs={{0,4},{1,5},{2,6},{3,7},{4,0},{5,1},{6,2},{7,3},{8,12},{9,13},{10,... | collective-permute-start | bytes 147464 | tf_op jit(solution)/shard_map/ppermute | solution.py:299
  7.2 11.3 %collective-permute-start.3 = (bf16[32,768]{1,0:T(8,128)(2,1)S(1)}, bf16[32,768]{1,0:T(8,128)(2,1)S(1)}, u32[]{:S(2)}, u32[]{:S(2)}) collective-permute-start(bf16[32,768]{1,0:T(8,128)(2,1)S(1)} %get-tuple-element.38), channel_id=1, source_target_pairs={{0,8},{1,9},{2,10},{3,11},{4,12},{5,13},{6,14},{7,15},{8,0},{9,1},... | collective-permute-start | bytes 147464 | tf_op jit(solution)/shard_map/ppermute | solution.py:299
  9.8 8.7 %collective-permute-start.4 = (bf16[32,768]{1,0:T(8,128)(2,1)S(1)}, bf16[32,768]{1,0:T(8,128)(2,1)S(1)}, u32[]{:S(2)}, u32[]{:S(2)}) collective-permute-start(bf16[32,768]{1,0:T(8,128)(2,1)S(1)} %get-tuple-element.38), channel_id=1, source_target_pairs={{0,12},{1,13},{2,14},{3,15},{4,8},{5,9},{6,10},{7,11},{8,4},{9,5},... | collective-permute-start | bytes 147464 | tf_op jit(solution)/shard_map/ppermute | solution.py:299
  11.5 8.2 %collective-permute-start.9 = (bf16[2,32,768]{2,1,0:T(8,128)(2,1)S(1)}, bf16[2,32,768]{2,1,0:T(8,128)(2,1)S(1)}, u32[]{:S(2)}, u32[]{:S(2)}) collective-permute-start(bf16[2,32,768]{2,1,0:T(8,128)(2,1)S(1)} %get-tuple-element.34), channel_id=1, source_target_pairs={{0,4},{1,5},{2,6},{3,7},{4,0},{5,1},{6,2},{7,3},{8,12},{9,13},{10,... | collective-permute-start | bytes 294920 | tf_op jit(solution)/shard_map/ppermute | solution.py:299
  12.2 7.6 %collective-permute-start.10 = (bf16[2,32,768]{2,1,0:T(8,128)(2,1)S(1)}, bf16[2,32,768]{2,1,0:T(8,128)(2,1)S(1)}, u32[]{:S(2)}, u32[]{:S(2)}) collective-permute-start(bf16[2,32,768]{2,1,0:T(8,128)(2,1)S(1)} %get-tuple-element.34), channel_id=1, source_target_pairs={{0,8},{1,9},{2,10},{3,11},{4,12},{5,13},{6,14},{7,15},{8,0},{9,1},... | collective-permute-start | bytes 294920 | tf_op jit(solution)/shard_map/ppermute | solution.py:299
  18.2 6.5 %collective-permute-start.11 = (bf16[2,32,768]{2,1,0:T(8,128)(2,1)S(1)}, bf16[2,32,768]{2,1,0:T(8,128)(2,1)S(1)}, u32[]{:S(2)}, u32[]{:S(2)}) collective-permute-start(bf16[2,32,768]{2,1,0:T(8,128)(2,1)S(1)} %get-tuple-element.34), channel_id=1, source_target_pairs={{0,12},{1,13},{2,14},{3,15},{4,8},{5,9},{6,10},{7,11},{8,4},{9,5},... | collective-permute-start | bytes 294920 | tf_op jit(solution)/shard_map/ppermute | solution.py:299
  18.6 7.5 %collective-permute-start.6 = (bf16[4,32,768]{2,1,0:T(8,128)(2,1)S(1)}, bf16[4,32,768]{2,1,0:T(8,128)(2,1)S(1)}, u32[]{:S(2)}, u32[]{:S(2)}) collective-permute-start(bf16[4,32,768]{2,1,0:T(8,128)(2,1)S(1)} %pad_maximum_fusion.refs_0_), channel_id=1, source_target_pairs={{0,2},{1,3},{2,0},{3,1},{4,6},{5,7},{6,4},{7,5},{8,10},{9,11},{10,... | collective-permute-start | bytes 589832 | tf_op jit(solution)/shard_map/ppermute | solution.py:299
  25.5 2.6 %collective-permute-start.12 = (bf16[4,2,32,768]{3,2,1,0:T(8,128)(2,1)}, bf16[4,2,32,768]{3,2,1,0:T(8,128)(2,1)}, u32[]{:S(2)}, u32[]{:S(2)}) collective-permute-start(bf16[4,2,32,768]{3,2,1,0:T(8,128)(2,1)} %maximum_add_fusion.refs_4_), channel_id=1, source_target_pairs={{0,1},{1,0},{2,3},{3,2},{4,5},{5,4},{6,7},{7,6},{8,9},{9,8},{10,11... | collective-permute-start | bytes 1179656 | tf_op jit(solution)/shard_map/ppermute | solution.py:299
  25.5 1.9 %collective-permute-start.5 = (bf16[4,32,768]{2,1,0:T(8,128)(2,1)S(1)}, bf16[4,32,768]{2,1,0:T(8,128)(2,1)}, u32[]{:S(2)}, u32[]{:S(2)}) collective-permute-start(bf16[4,32,768]{2,1,0:T(8,128)(2,1)S(1)} %pad_maximum_fusion.refs_0_), channel_id=1, source_target_pairs={{0,1},{1,0},{2,3},{3,2},{4,5},{5,4},{6,7},{7,6},{8,9},{9,8},{10,11... | collective-permute-start | bytes 589832 | tf_op jit(solution)/shard_map/ppermute | solution.py:299
  26.0 1.9 %collective-permute-start.7 = (bf16[4,32,768]{2,1,0:T(8,128)(2,1)S(1)}, bf16[4,32,768]{2,1,0:T(8,128)(2,1)}, u32[]{:S(2)}, u32[]{:S(2)}) collective-permute-start(bf16[4,32,768]{2,1,0:T(8,128)(2,1)S(1)} %collective-permute-done.6.refs_2_), channel_id=1, source_target_pairs={{0,1},{1,0},{2,3},{3,2},{4,5},{5,4},{6,7},{7,6},{8,9},{9,8},{10,11... | collective-permute-start | bytes 589832 | tf_op jit(solution)/shard_map/ppermute | solution.py:299
  41.3 6.6 %collective-permute-start.13 = (bf16[512,128]{1,0:T(8,128)(2,1)S(1)}, bf16[512,128]{1,0:T(8,128)(2,1)S(1)}, u32[]{:S(2)}, u32[]{:S(2)}) collective-permute-start(bf16[512,128]{1,0:T(8,128)(2,1)S(1)} %get-tuple-element.21), channel_id=1, source_target_pairs={{0,2},{1,3},{2,0},{3,1},{4,6},{5,7},{6,4},{7,5},{8,10},{9,11},{10,... | collective-permute-start | bytes 393224 | tf_op jit(solution)/shard_map/ppermute | solution.py:299
  43.5 11.2 %collective-permute-start.17 = (bf16[512,128]{1,0:T(8,128)(2,1)S(1)}, bf16[512,128]{1,0:T(8,128)(2,1)S(1)}, u32[]{:S(2)}, u32[]{:S(2)}) collective-permute-start(bf16[512,128]{1,0:T(8,128)(2,1)S(1)} %get-tuple-element.25), channel_id=1, source_target_pairs={{0,2},{1,3},{2,0},{3,1},{4,6},{5,7},{6,4},{7,5},{8,10},{9,11},{10,... | collective-permute-start | bytes 393224 | tf_op jit(solution)/shard_map/ppermute | solution.py:299
  43.6 9.9 %collective-permute-start.21 = (bf16[512,128]{1,0:T(8,128)(2,1)S(1)}, bf16[512,128]{1,0:T(8,128)(2,1)S(1)}, u32[]{:S(2)}, u32[]{:S(2)}) collective-permute-start(bf16[512,128]{1,0:T(8,128)(2,1)S(1)} %get-tuple-element.29), channel_id=1, source_target_pairs={{0,2},{1,3},{2,0},{3,1},{4,6},{5,7},{6,4},{7,5},{8,10},{9,11},{10,... | collective-permute-start | bytes 393224 | tf_op jit(solution)/shard_map/ppermute | solution.py:299
  45.6 13.5 %collective-permute-start.15 = (bf16[512,256]{1,0:T(8,128)(2,1)S(1)}, bf16[512,256]{1,0:T(8,128)(2,1)S(1)}, u32[]{:S(2)}, u32[]{:S(2)}) collective-permute-start(bf16[512,256]{1,0:T(8,128)(2,1)S(1)} %get-tuple-element.23), channel_id=1, source_target_pairs={{0,2},{1,3},{2,0},{3,1},{4,6},{5,7},{6,4},{7,5},{8,10},{9,11},{10,... | collective-permute-start | bytes 786440 | tf_op jit(solution)/shard_map/ppermute | solution.py:299
  47.9 8.5 %collective-permute-start.18 = (bf16[512,128]{1,0:T(8,128)(2,1)S(1)}, bf16[512,128]{1,0:T(8,128)(2,1)S(1)}, u32[]{:S(2)}, u32[]{:S(2)}) collective-permute-start(bf16[512,128]{1,0:T(8,128)(2,1)S(1)} %add_convert_fusion.5), channel_id=1, source_target_pairs={{0,4},{1,5},{2,6},{3,7},{4,0},{5,1},{6,2},{7,3},{8,12},{9,13},{10,... | collective-permute-start | bytes 393224 | tf_op jit(solution)/shard_map/ppermute | solution.py:299
  49.8 12.1 %collective-permute-start.20 = (bf16[512,128]{1,0:T(8,128)(2,1)S(1)}, bf16[512,128]{1,0:T(8,128)(2,1)S(1)}, u32[]{:S(2)}, u32[]{:S(2)}) collective-permute-start(bf16[512,128]{1,0:T(8,128)(2,1)S(1)} %broadcast_add_fusion.1), channel_id=1, source_target_pairs={{0,2},{1,3},{2,0},{3,1},{4,6},{5,7},{6,4},{7,5},{8,10},{9,11},{10,... | collective-permute-start | bytes 393224 | tf_op jit(solution)/shard_map/ppermute | solution.py:299
  53.5 8.4 %collective-permute-start.22 = (bf16[512,128]{1,0:T(8,128)(2,1)S(1)}, bf16[512,128]{1,0:T(8,128)(2,1)S(1)}, u32[]{:S(2)}, u32[]{:S(2)}) collective-permute-start(bf16[512,128]{1,0:T(8,128)(2,1)S(1)} %add_convert_fusion.3), channel_id=1, source_target_pairs={{0,4},{1,5},{2,6},{3,7},{4,0},{5,1},{6,2},{7,3},{8,12},{9,13},{10,... | collective-permute-start | bytes 393224 | tf_op jit(solution)/shard_map/ppermute | solution.py:299
  54.8 15.4 %collective-permute-start.14 = (bf16[512,256]{1,0:T(8,128)(2,1)}, bf16[512,256]{1,0:T(8,128)(2,1)}, u32[]{:S(2)}, u32[]{:S(2)}) collective-permute-start(bf16[512,256]{1,0:T(8,128)(2,1)} %broadcast_add_fusion), channel_id=1, source_target_pairs={{0,2},{1,3},{2,0},{3,1},{4,6},{5,7},{6,4},{7,5},{8,10},{9,11},{10,... | collective-permute-start | bytes 786440 | tf_op jit(solution)/shard_map/ppermute | solution.py:299
  57.1 6.4 %collective-permute-start.19 = (bf16[512,128]{1,0:T(8,128)(2,1)}, bf16[512,128]{1,0:T(8,128)(2,1)S(1)}, u32[]{:S(2)}, u32[]{:S(2)}) collective-permute-start(bf16[512,128]{1,0:T(8,128)(2,1)} %add_convert_fusion.4), channel_id=1, source_target_pairs={{0,8},{1,9},{2,10},{3,11},{4,12},{5,13},{6,14},{7,15},{8,0},{9,1},... | collective-permute-start | bytes 393224 | tf_op jit(solution)/shard_map/ppermute | solution.py:299
  59.8 11.9 %collective-permute-start.16 = (bf16[512,256]{1,0:T(8,128)(2,1)}, bf16[512,256]{1,0:T(8,128)(2,1)}, u32[]{:S(2)}, u32[]{:S(2)}) collective-permute-start(bf16[512,256]{1,0:T(8,128)(2,1)} %add_convert_fusion.1), channel_id=1, source_target_pairs={{0,4},{1,5},{2,6},{3,7},{4,0},{5,1},{6,2},{7,3},{8,12},{9,13},{10,... | collective-permute-start | bytes 786440 | tf_op jit(solution)/shard_map/ppermute | solution.py:299
  62.6 7.6 %collective-permute-start.23 = (bf16[512,128]{1,0:T(8,128)(2,1)}, bf16[512,128]{1,0:T(8,128)(2,1)}, u32[]{:S(2)}, u32[]{:S(2)}) collective-permute-start(bf16[512,128]{1,0:T(8,128)(2,1)} %add_convert_fusion.2), channel_id=1, source_target_pairs={{0,8},{1,9},{2,10},{3,11},{4,12},{5,13},{6,14},{7,15},{8,0},{9,1},... | collective-permute-start | bytes 393224 | tf_op jit(solution)/shard_map/ppermute | solution.py:299
  73.1 1.4 %collective-permute-start.24 = (bf16[256,256]{1,0:T(8,128)(2,1)S(1)}, bf16[256,256]{1,0:T(8,128)(2,1)S(1)}, u32[]{:S(2)}, u32[]{:S(2)}) collective-permute-start(bf16[256,256]{1,0:T(8,128)(2,1)S(1)} %get-tuple-element.31), channel_id=1, source_target_pairs={{0,1},{1,0},{2,3},{3,2},{4,5},{5,4},{6,7},{7,6},{8,9},{9,8},{10,11... | collective-permute-start | bytes 393224 | tf_op jit(solution)/shard_map/ppermute | solution.py:299
  (4 other events, 37.0 us)

commit v5 on v4

--- a/solution.py
+++ b/solution.py
@@ -315,7 +315,8 @@
     b_z = {s: permute(b_pair, 4 * s, count) for s in (3, 2, 1)}
     near = jnp.stack([a, a_z[1], a_z[2], a_z[3]])
     far = permute(near, 2, count)
-    late = (other[0, 0, 0] != other[0, 0, 0]).astype(jnp.int32)
+    line = other[0, 0, : numbers.shape[0]]
+    late = (line != line).astype(jnp.int32)
     other_numbers = permute(numbers + late, 1, count)
     nothing = (other_numbers[0] < 0).astype(BF)
     rest = jnp.stack([b_pair, b_z[1], b_z[2], b_z[3]]) + nothing

time: 77.7 us -> 77.9 us (level)
  the two profiles are of different devices: /device:TPU:0 before, /device:TPU:5 now
where the time goes in v5:
time: 77.9 us
  starting transfers between devices  36.3 us (47%)
  waiting for transfers between devices  15.1 us (19%)
  Pallas kernels  14.4 us (18%)
  other arithmetic  6.72 us (9%)
  local copies, waits for them, and re-layouts  3.03 us (4%)
  between operations  2.29 us (3%)
    ppermute x25, starting transfers between devices, permute(): return lax.ppermute(array, 'pan', [(i, i ^ mask) for i in range(count)])  36.3 us
    ppermute x25, waiting for transfers between devices, permute(): return lax.ppermute(array, 'pan', [(i, i ^ mask) for i in range(count)])  15.1 us
    pallas_call x1, Pallas kernels, bra_transform(): pl.pallas_call(functools.partial(bra_kernel, regions, locate, chunk, piec...  11.7 us
    convert_element_type x6, other arithmetic, added(): return result.astype(BF)  3.53 us
    pallas_call x1, Pallas kernels, last_step(): pl.pallas_call(last_kernel, out_shape=jax.ShapeDtypeStruct((rows, orbital...  2.77 us
  transfers between devices with their start and end apart: 25, of which 9 were waited for; matrix products, arithmetic and copies ran while one was open for 10% of the time, Pallas kernels for 0%

profile of v5, /device:TPU:5, one launch (start us, length us, event | category | flops | bytes accessed | tf_op | source)
XLA Modules:
  0.0 77.9 jit_solution(13656476722547281851)
XLA Ops:
  0.7 0.9 %pad_clamp_fusion = s32[1024]{0:T(1024)S(1)} fusion(s32[64]{0:T(128)} %param.15), kind=kLoop, calls=%fused_computation.14 | loop fusion | flops 1024 | bytes 4352 | tf_op jit(solution)/shard_map/gather | solution.py:348
  2.6 1.3 %collective-permute-start.8 = (bf16[32,768]{1,0:T(8,128)(2,1)S(1)}, bf16[32,768]{1,0:T(8,128)(2,1)S(1)}, u32[]{:S(2)}, u32[]{:S(2)}) collective-permute-start(bf16[32,768]{1,0:T(8,128)(2,1)S(1)} %get-tuple-element.37), channel_id=1, source_target_pairs={{0,2},{1,3},{2,0},{3,1},{4,6},{5,7},{6,4},{7,5},{8,10},{9,11},{10,... | collective-permute-start | bytes 147464 | tf_op jit(solution)/shard_map/ppermute | solution.py:299
  3.9 1.3 %collective-permute-start.2 = (bf16[32,768]{1,0:T(8,128)(2,1)S(1)}, bf16[32,768]{1,0:T(8,128)(2,1)S(1)}, u32[]{:S(2)}, u32[]{:S(2)}) collective-permute-start(bf16[32,768]{1,0:T(8,128)(2,1)S(1)} %get-tuple-element.38), channel_id=1, source_target_pairs={{0,4},{1,5},{2,6},{3,7},{4,0},{5,1},{6,2},{7,3},{8,12},{9,13},{10,... | collective-permute-start | bytes 147464 | tf_op jit(solution)/shard_map/ppermute | solution.py:299
  5.2 2.3 %collective-permute-start.3 = (bf16[32,768]{1,0:T(8,128)(2,1)S(1)}, bf16[32,768]{1,0:T(8,128)(2,1)S(1)}, u32[]{:S(2)}, u32[]{:S(2)}) collective-permute-start(bf16[32,768]{1,0:T(8,128)(2,1)S(1)} %get-tuple-element.38), channel_id=1, source_target_pairs={{0,8},{1,9},{2,10},{3,11},{4,12},{5,13},{6,14},{7,15},{8,0},{9,1},... | collective-permute-start | bytes 147464 | tf_op jit(solution)/shard_map/ppermute | solution.py:299
  8.1 0.8 %concatenate.6.mine = s32[89]{0:T(128)S(1)} concatenate(s32[40]{0:T(128)} %param.9, s32[40]{0:T(128)} %param.10, s32[1]{0:T(128)S(6)} %copy.9, s32[4]{0:T(128)} %param.12, s32[4]{0:T(128)} %param.13), dimensions={0} | concatenate | bytes 712 | tf_op jit(solution)/shard_map/concatenate | solution.py:347
  9.4 3.2 %collective-permute-start.10 = (bf16[2,32,768]{2,1,0:T(8,128)(2,1)S(1)}, bf16[2,32,768]{2,1,0:T(8,128)(2,1)S(1)}, u32[]{:S(2)}, u32[]{:S(2)}) collective-permute-start(bf16[2,32,768]{2,1,0:T(8,128)(2,1)S(1)} %get-tuple-element.34), channel_id=1, source_target_pairs={{0,8},{1,9},{2,10},{3,11},{4,12},{5,13},{6,14},{7,15},{8,0},{9,1},... | collective-permute-start | bytes 294920 | tf_op jit(solution)/shard_map/ppermute | solution.py:299
  13.4 2.5 %collective-permute-start.1 = (s32[89]{0:T(128)S(1)}, s32[89]{0:T(128)S(1)}, u32[]{:S(2)}, u32[]{:S(2)}) collective-permute-start(s32[89]{0:T(128)S(1)} %fusion.1), channel_id=1, source_target_pairs={{0,1},{1,0},{2,3},{3,2},{4,5},{5,4},{6,7},{7,6},{8,9},{9,8},{10,11... | collective-permute-start | bytes 1076 | tf_op jit(solution)/shard_map/ppermute | solution.py:299
  16.7 2.4 %collective-permute-done.11 = bf16[2,32,768]{2,1,0:T(8,128)(2,1)S(1)} collective-permute-done((bf16[2,32,768]{2,1,0:T(8,128)(2,1)S(1)}, bf16[2,32,768]{2,1,0:T(8,128)(2,1)S(1)}, u32[]{:S(2)}, u32[]{:S(2)}) %collective-permute-start.11) | collective-permute-done | bytes 98336 | tf_op jit(solution)/shard_map/ppermute | solution.py:299
  19.1 0.8 %maximum_add_fusion.refs_4_ = bf16[4,2,32,768]{3,2,1,0:T(8,128)(2,1)} fusion(bf16[1,2,32,768]{3,2,1,0:T(8,128)(2,1)S(1)} %bitcast.26, bf16[1,2,32,768]{3,2,1,0:T(8,128)(2,1)S(1)} %bitcast.25, bf16[1,2,32,768]{3,2,1,0:T(8,128)(2,1)S(1)} %bitcast.24, bf16[1,2,32,768]{3,2,1,0:T(8,128)(2,1)S(1)} %get-tuple-element.33, bf16[]{:T(256)} %bitcast.13), kind=kLoop, calls=%fused_computation.3 | loop fusion | flops 786432 | bytes 786434 | tf_op jit(solution)/shard_map/add | solution.py:322
  19.9 3.0 %collective-permute-start.12 = (bf16[4,2,32,768]{3,2,1,0:T(8,128)(2,1)}, bf16[4,2,32,768]{3,2,1,0:T(8,128)(2,1)}, u32[]{:S(2)}, u32[]{:S(2)}) collective-permute-start(bf16[4,2,32,768]{3,2,1,0:T(8,128)(2,1)} %maximum_add_fusion.refs_4_), channel_id=1, source_target_pairs={{0,1},{1,0},{2,3},{3,2},{4,5},{5,4},{6,7},{7,6},{8,9},{9,8},{10,11... | collective-permute-start | bytes 1179656 | tf_op jit(solution)/shard_map/ppermute | solution.py:299
  23.5 1.1 %collective-permute-done.5.refs_1_ = bf16[4,32,768]{2,1,0:T(8,128)(2,1)} collective-permute-done((bf16[4,32,768]{2,1,0:T(8,128)(2,1)S(1)}, bf16[4,32,768]{2,1,0:T(8,128)(2,1)}, u32[]{:S(2)}, u32[]{:S(2)}) %collective-permute-start.5) | collective-permute-done | bytes 196640 | tf_op jit(solution)/shard_map/ppermute | solution.py:299
  25.2 11.7 %bra_transform.1 = (bf16[512,128]{1,0:T(8,128)(2,1)S(1)}, bf16[512,128]{1,0:T(8,128)(2,1)S(1)}, bf16[512,128]{1,0:T(8,128)(2,1)S(1)}, bf16[512,128]{1,0:T(8,128)...) custom-call(s32[1]{0:T(128)} %bitcast.me_ref, ...), custom_call_target="tpu_custom_call" | custom-call | flops 2684354560 | bytes 8388608 | tf_op jit(solution)/shard_map/bra_transform/pallas_call | solution.py:211
  37.5 1.5 %collective-permute-start.17 = (bf16[512,128]{1,0:T(8,128)(2,1)S(1)}, bf16[512,128]{1,0:T(8,128)(2,1)S(1)}, u32[]{:S(2)}, u32[]{:S(2)}) collective-permute-start(bf16[512,128]{1,0:T(8,128)(2,1)S(1)} %get-tuple-element.25), channel_id=1, source_target_pairs={{0,2},{1,3},{2,0},{3,1},{4,6},{5,7},{6,4},{7,5},{8,10},{9,11},{10,... | collective-permute-start | bytes 393224 | tf_op jit(solution)/shard_map/ppermute | solution.py:299
  39.1 1.4 %collective-permute-start.15 = (bf16[512,256]{1,0:T(8,128)(2,1)S(1)}, bf16[512,256]{1,0:T(8,128)(2,1)S(1)}, u32[]{:S(2)}, u32[]{:S(2)}) collective-permute-start(bf16[512,256]{1,0:T(8,128)(2,1)S(1)} %get-tuple-element.23), channel_id=1, source_target_pairs={{0,2},{1,3},{2,0},{3,1},{4,6},{5,7},{6,4},{7,5},{8,10},{9,11},{10,... | collective-permute-start | bytes 786440 | tf_op jit(solution)/shard_map/ppermute | solution.py:299
  40.5 1.8 %collective-permute-done.13 = bf16[512,128]{1,0:T(8,128)(2,1)S(1)} collective-permute-done((bf16[512,128]{1,0:T(8,128)(2,1)S(1)}, bf16[512,128]{1,0:T(8,128)(2,1)S(1)}, u32[]{:S(2)}, u32[]{:S(2)}) %collective-permute-start.13) | collective-permute-done | bytes 131104 | tf_op jit(solution)/shard_map/ppermute | solution.py:299
  44.6 3.3 %collective-permute-done.21 = bf16[512,128]{1,0:T(8,128)(2,1)S(1)} collective-permute-done((bf16[512,128]{1,0:T(8,128)(2,1)S(1)}, bf16[512,128]{1,0:T(8,128)(2,1)S(1)}, u32[]{:S(2)}, u32[]{:S(2)}) %collective-permute-start.21) | collective-permute-done | bytes 131104 | tf_op jit(solution)/shard_map/ppermute | solution.py:299
  49.8 8.8 %collective-permute-start.19 = (bf16[512,128]{1,0:T(8,128)(2,1)}, bf16[512,128]{1,0:T(8,128)(2,1)S(1)}, u32[]{:S(2)}, u32[]{:S(2)}) collective-permute-start(bf16[512,128]{1,0:T(8,128)(2,1)} %add_convert_fusion.4), channel_id=1, source_target_pairs={{0,8},{1,9},{2,10},{3,11},{4,12},{5,13},{6,14},{7,15},{8,0},{9,1},... | collective-permute-start | bytes 393224 | tf_op jit(solution)/shard_map/ppermute | solution.py:299
  59.4 1.5 %collective-permute-start.16 = (bf16[512,256]{1,0:T(8,128)(2,1)}, bf16[512,256]{1,0:T(8,128)(2,1)}, u32[]{:S(2)}, u32[]{:S(2)}) collective-permute-start(bf16[512,256]{1,0:T(8,128)(2,1)} %add_convert_fusion.1), channel_id=1, source_target_pairs={{0,4},{1,5},{2,6},{3,7},{4,0},{5,1},{6,2},{7,3},{8,12},{9,13},{10,... | collective-permute-start | bytes 786440 | tf_op jit(solution)/shard_map/ppermute | solution.py:299
  61.5 3.5 %collective-permute-start.23 = (bf16[512,128]{1,0:T(8,128)(2,1)}, bf16[512,128]{1,0:T(8,128)(2,1)}, u32[]{:S(2)}, u32[]{:S(2)}) collective-permute-start(bf16[512,128]{1,0:T(8,128)(2,1)} %add_convert_fusion.2), channel_id=1, source_target_pairs={{0,8},{1,9},{2,10},{3,11},{4,12},{5,13},{6,14},{7,15},{8,0},{9,1},... | collective-permute-start | bytes 393224 | tf_op jit(solution)/shard_map/ppermute | solution.py:299
  65.0 4.5 %collective-permute-done.23 = bf16[512,128]{1,0:T(8,128)(2,1)} collective-permute-done((bf16[512,128]{1,0:T(8,128)(2,1)}, bf16[512,128]{1,0:T(8,128)(2,1)}, u32[]{:S(2)}, u32[]{:S(2)}) %collective-permute-start.23) | collective-permute-done | bytes 131104 | tf_op jit(solution)/shard_map/ppermute | solution.py:299
  69.5 1.3 %add_convert_fusion = bf16[512,256]{1,0:T(8,128)(2,1)S(1)} fusion(bf16[512,256]{1,0:T(8,128)(2,1)} %collective-permute-done.16, bf16[512,256]{1,0:T(8,128)(2,1)} %collective-permute-done.14, bf16[512,256]{1,0:T(8,128)(2,1)} %copy-done.2, bf16[512,128]{1,0:T(8,128)(2,1)} %collective-permute-done.23, bf16[512,128]{1,0:T(8,128)(2,1)S(1)} %collective-permute-done.19), kind=kLoop, calls=%fused_computation.1 | loop fusion | flops 1441792 | bytes 1310720 | tf_op jit(solution)/shard_map/convert_element_type | solution.py:306
  70.8 3.2 %collective-permute-start.24 = (bf16[256,256]{1,0:T(8,128)(2,1)S(1)}, bf16[256,256]{1,0:T(8,128)(2,1)S(1)}, u32[]{:S(2)}, u32[]{:S(2)}) collective-permute-start(bf16[256,256]{1,0:T(8,128)(2,1)S(1)} %get-tuple-element.31), channel_id=1, source_target_pairs={{0,1},{1,0},{2,3},{3,2},{4,5},{5,4},{6,7},{7,6},{8,9},{9,8},{10,11... | collective-permute-start | bytes 393224 | tf_op jit(solution)/shard_map/ppermute | solution.py:299
  74.0 1.0 %collective-permute-done.24.other = bf16[256,256]{1,0:T(8,128)(2,1)S(1)} collective-permute-done((bf16[256,256]{1,0:T(8,128)(2,1)S(1)}, bf16[256,256]{1,0:T(8,128)(2,1)S(1)}, u32[]{:S(2)}, u32[]{:S(2)}) %collective-permute-start.24) | collective-permute-done | bytes 131104 | tf_op jit(solution)/shard_map/ppermute | solution.py:299
  75.0 2.8 %last_step.1 = f32[256,4096]{1,0:T(8,128)} custom-call(bf16[256,256]{1,0:T(8,128)(2,1)S(1)} %get-tuple-element.32.own, bf16[256,256]{1,0:T(8,128)(2,1)S(1)} %collective-permute-done.24.other, f32[2,4,64,128]{3,2,1,0:T(8,128)S(1)} %copy-done.1), custom_call_target="tpu_custom_call" | custom-call | tf_op jit(solution)/shard_map/last_step/pallas_call | solution.py:283
  (52 shorter events, 10.0 us)
Async XLA Ops:
  0.0 9.3 %collective-permute-start = (bf16[40,512,128]{2,1,0:T(8,128)(2,1)}, bf16[40,512,128]{2,1,0:T(8,128)(2,1)}, u32[]{:S(2)}, u32[]{:S(2)}) collective-permute-start(bf16[40,512,128]{2,1,0:T(8,128)(2,1)} %refs_6_.1), channel_id=1, source_target_pairs={{0,1},{1,0},{2,3},{3,2},{4,5},{5,4},{6,7},{7,6},{8,9},{9,8},{10,11... | collective-permute-start | bytes 15728648 | tf_op jit(solution)/shard_map/ppermute | solution.py:299
  2.6 6.3 %collective-permute-start.8 = (bf16[32,768]{1,0:T(8,128)(2,1)S(1)}, bf16[32,768]{1,0:T(8,128)(2,1)S(1)}, u32[]{:S(2)}, u32[]{:S(2)}) collective-permute-start(bf16[32,768]{1,0:T(8,128)(2,1)S(1)} %get-tuple-element.37), channel_id=1, source_target_pairs={{0,2},{1,3},{2,0},{3,1},{4,6},{5,7},{6,4},{7,5},{8,10},{9,11},{10,... | collective-permute-start | bytes 147464 | tf_op jit(solution)/shard_map/ppermute | solution.py:299
  3.9 9.4 %collective-permute-start.2 = (bf16[32,768]{1,0:T(8,128)(2,1)S(1)}, bf16[32,768]{1,0:T(8,128)(2,1)S(1)}, u32[]{:S(2)}, u32[]{:S(2)}) collective-permute-start(bf16[32,768]{1,0:T(8,128)(2,1)S(1)} %get-tuple-element.38), channel_id=1, source_target_pairs={{0,4},{1,5},{2,6},{3,7},{4,0},{5,1},{6,2},{7,3},{8,12},{9,13},{10,... | collective-permute-start | bytes 147464 | tf_op jit(solution)/shard_map/ppermute | solution.py:299
  5.2 8.2 %collective-permute-start.3 = (bf16[32,768]{1,0:T(8,128)(2,1)S(1)}, bf16[32,768]{1,0:T(8,128)(2,1)S(1)}, u32[]{:S(2)}, u32[]{:S(2)}) collective-permute-start(bf16[32,768]{1,0:T(8,128)(2,1)S(1)} %get-tuple-element.38), channel_id=1, source_target_pairs={{0,8},{1,9},{2,10},{3,11},{4,12},{5,13},{6,14},{7,15},{8,0},{9,1},... | collective-permute-start | bytes 147464 | tf_op jit(solution)/shard_map/ppermute | solution.py:299
  7.5 8.4 %collective-permute-start.4 = (bf16[32,768]{1,0:T(8,128)(2,1)S(1)}, bf16[32,768]{1,0:T(8,128)(2,1)S(1)}, u32[]{:S(2)}, u32[]{:S(2)}) collective-permute-start(bf16[32,768]{1,0:T(8,128)(2,1)S(1)} %get-tuple-element.38), channel_id=1, source_target_pairs={{0,12},{1,13},{2,14},{3,15},{4,8},{5,9},{6,10},{7,11},{8,4},{9,5},... | collective-permute-start | bytes 147464 | tf_op jit(solution)/shard_map/ppermute | solution.py:299
  8.9 7.8 %collective-permute-start.9 = (bf16[2,32,768]{2,1,0:T(8,128)(2,1)S(1)}, bf16[2,32,768]{2,1,0:T(8,128)(2,1)S(1)}, u32[]{:S(2)}, u32[]{:S(2)}) collective-permute-start(bf16[2,32,768]{2,1,0:T(8,128)(2,1)S(1)} %get-tuple-element.34), channel_id=1, source_target_pairs={{0,4},{1,5},{2,6},{3,7},{4,0},{5,1},{6,2},{7,3},{8,12},{9,13},{10,... | collective-permute-start | bytes 294920 | tf_op jit(solution)/shard_map/ppermute | solution.py:299
  9.4 7.4 %collective-permute-start.10 = (bf16[2,32,768]{2,1,0:T(8,128)(2,1)S(1)}, bf16[2,32,768]{2,1,0:T(8,128)(2,1)S(1)}, u32[]{:S(2)}, u32[]{:S(2)}) collective-permute-start(bf16[2,32,768]{2,1,0:T(8,128)(2,1)S(1)} %get-tuple-element.34), channel_id=1, source_target_pairs={{0,8},{1,9},{2,10},{3,11},{4,12},{5,13},{6,14},{7,15},{8,0},{9,1},... | collective-permute-start | bytes 294920 | tf_op jit(solution)/shard_map/ppermute | solution.py:299
  13.3 5.9 %collective-permute-start.11 = (bf16[2,32,768]{2,1,0:T(8,128)(2,1)S(1)}, bf16[2,32,768]{2,1,0:T(8,128)(2,1)S(1)}, u32[]{:S(2)}, u32[]{:S(2)}) collective-permute-start(bf16[2,32,768]{2,1,0:T(8,128)(2,1)S(1)} %get-tuple-element.34), channel_id=1, source_target_pairs={{0,12},{1,13},{2,14},{3,15},{4,8},{5,9},{6,10},{7,11},{8,4},{9,5},... | collective-permute-start | bytes 294920 | tf_op jit(solution)/shard_map/ppermute | solution.py:299
  13.4 3.3 %collective-permute-start.1 = (s32[89]{0:T(128)S(1)}, s32[89]{0:T(128)S(1)}, u32[]{:S(2)}, u32[]{:S(2)}) collective-permute-start(s32[89]{0:T(128)S(1)} %fusion.1), channel_id=1, source_target_pairs={{0,1},{1,0},{2,3},{3,2},{4,5},{5,4},{6,7},{7,6},{8,9},{9,8},{10,11... | collective-permute-start | bytes 1076 | tf_op jit(solution)/shard_map/ppermute | solution.py:299
  15.9 7.1 %collective-permute-start.6 = (bf16[4,32,768]{2,1,0:T(8,128)(2,1)S(1)}, bf16[4,32,768]{2,1,0:T(8,128)(2,1)S(1)}, u32[]{:S(2)}, u32[]{:S(2)}) collective-permute-start(bf16[4,32,768]{2,1,0:T(8,128)(2,1)S(1)} %pad_maximum_fusion.refs_0_), channel_id=1, source_target_pairs={{0,2},{1,3},{2,0},{3,1},{4,6},{5,7},{6,4},{7,5},{8,10},{9,11},{10,... | collective-permute-start | bytes 589832 | tf_op jit(solution)/shard_map/ppermute | solution.py:299
  19.9 5.2 %collective-permute-start.12 = (bf16[4,2,32,768]{3,2,1,0:T(8,128)(2,1)}, bf16[4,2,32,768]{3,2,1,0:T(8,128)(2,1)}, u32[]{:S(2)}, u32[]{:S(2)}) collective-permute-start(bf16[4,2,32,768]{3,2,1,0:T(8,128)(2,1)} %maximum_add_fusion.refs_4_), channel_id=1, source_target_pairs={{0,1},{1,0},{2,3},{3,2},{4,5},{5,4},{6,7},{7,6},{8,9},{9,8},{10,11... | collective-permute-start | bytes 1179656 | tf_op jit(solution)/shard_map/ppermute | solution.py:299
  23.0 2.0 %collective-permute-start.7 = (bf16[4,32,768]{2,1,0:T(8,128)(2,1)S(1)}, bf16[4,32,768]{2,1,0:T(8,128)(2,1)}, u32[]{:S(2)}, u32[]{:S(2)}) collective-permute-start(bf16[4,32,768]{2,1,0:T(8,128)(2,1)S(1)} %collective-permute-done.6.refs_2_), channel_id=1, source_target_pairs={{0,1},{1,0},{2,3},{3,2},{4,5},{5,4},{6,7},{7,6},{8,9},{9,8},{10,11... | collective-permute-start | bytes 589832 | tf_op jit(solution)/shard_map/ppermute | solution.py:299
  37.5 4.7 %collective-permute-start.13 = (bf16[512,128]{1,0:T(8,128)(2,1)S(1)}, bf16[512,128]{1,0:T(8,128)(2,1)S(1)}, u32[]{:S(2)}, u32[]{:S(2)}) collective-permute-start(bf16[512,128]{1,0:T(8,128)(2,1)S(1)} %get-tuple-element.21), channel_id=1, source_target_pairs={{0,2},{1,3},{2,0},{3,1},{4,6},{5,7},{6,4},{7,5},{8,10},{9,11},{10,... | collective-permute-start | bytes 393224 | tf_op jit(solution)/shard_map/ppermute | solution.py:299
  37.5 11.2 %collective-permute-start.17 = (bf16[512,128]{1,0:T(8,128)(2,1)S(1)}, bf16[512,128]{1,0:T(8,128)(2,1)S(1)}, u32[]{:S(2)}, u32[]{:S(2)}) collective-permute-start(bf16[512,128]{1,0:T(8,128)(2,1)S(1)} %get-tuple-element.25), channel_id=1, source_target_pairs={{0,2},{1,3},{2,0},{3,1},{4,6},{5,7},{6,4},{7,5},{8,10},{9,11},{10,... | collective-permute-start | bytes 393224 | tf_op jit(solution)/shard_map/ppermute | solution.py:299
  39.0 8.9 %collective-permute-start.21 = (bf16[512,128]{1,0:T(8,128)(2,1)S(1)}, bf16[512,128]{1,0:T(8,128)(2,1)S(1)}, u32[]{:S(2)}, u32[]{:S(2)}) collective-permute-start(bf16[512,128]{1,0:T(8,128)(2,1)S(1)} %get-tuple-element.29), channel_id=1, source_target_pairs={{0,2},{1,3},{2,0},{3,1},{4,6},{5,7},{6,4},{7,5},{8,10},{9,11},{10,... | collective-permute-start | bytes 393224 | tf_op jit(solution)/shard_map/ppermute | solution.py:299
  39.1 19.5 %collective-permute-start.15 = (bf16[512,256]{1,0:T(8,128)(2,1)S(1)}, bf16[512,256]{1,0:T(8,128)(2,1)S(1)}, u32[]{:S(2)}, u32[]{:S(2)}) collective-permute-start(bf16[512,256]{1,0:T(8,128)(2,1)S(1)} %get-tuple-element.23), channel_id=1, source_target_pairs={{0,2},{1,3},{2,0},{3,1},{4,6},{5,7},{6,4},{7,5},{8,10},{9,11},{10,... | collective-permute-start | bytes 786440 | tf_op jit(solution)/shard_map/ppermute | solution.py:299
  42.3 6.8 %collective-permute-start.18 = (bf16[512,128]{1,0:T(8,128)(2,1)S(1)}, bf16[512,128]{1,0:T(8,128)(2,1)S(1)}, u32[]{:S(2)}, u32[]{:S(2)}) collective-permute-start(bf16[512,128]{1,0:T(8,128)(2,1)S(1)} %add_convert_fusion.5), channel_id=1, source_target_pairs={{0,4},{1,5},{2,6},{3,7},{4,0},{5,1},{6,2},{7,3},{8,12},{9,13},{10,... | collective-permute-start | bytes 393224 | tf_op jit(solution)/shard_map/ppermute | solution.py:299
  44.2 16.6 %collective-permute-start.20 = (bf16[512,128]{1,0:T(8,128)(2,1)S(1)}, bf16[512,128]{1,0:T(8,128)(2,1)S(1)}, u32[]{:S(2)}, u32[]{:S(2)}) collective-permute-start(bf16[512,128]{1,0:T(8,128)(2,1)S(1)} %broadcast_add_fusion.1), channel_id=1, source_target_pairs={{0,2},{1,3},{2,0},{3,1},{4,6},{5,7},{6,4},{7,5},{8,10},{9,11},{10,... | collective-permute-start | bytes 393224 | tf_op jit(solution)/shard_map/ppermute | solution.py:299
  47.9 12.9 %collective-permute-start.22 = (bf16[512,128]{1,0:T(8,128)(2,1)S(1)}, bf16[512,128]{1,0:T(8,128)(2,1)S(1)}, u32[]{:S(2)}, u32[]{:S(2)}) collective-permute-start(bf16[512,128]{1,0:T(8,128)(2,1)S(1)} %add_convert_fusion.3), channel_id=1, source_target_pairs={{0,4},{1,5},{2,6},{3,7},{4,0},{5,1},{6,2},{7,3},{8,12},{9,13},{10,... | collective-permute-start | bytes 393224 | tf_op jit(solution)/shard_map/ppermute | solution.py:299
  48.7 20.8 %collective-permute-start.14 = (bf16[512,256]{1,0:T(8,128)(2,1)}, bf16[512,256]{1,0:T(8,128)(2,1)}, u32[]{:S(2)}, u32[]{:S(2)}) collective-permute-start(bf16[512,256]{1,0:T(8,128)(2,1)} %broadcast_add_fusion), channel_id=1, source_target_pairs={{0,2},{1,3},{2,0},{3,1},{4,6},{5,7},{6,4},{7,5},{8,10},{9,11},{10,... | collective-permute-start | bytes 786440 | tf_op jit(solution)/shard_map/ppermute | solution.py:299
  49.8 15.2 %collective-permute-start.19 = (bf16[512,128]{1,0:T(8,128)(2,1)}, bf16[512,128]{1,0:T(8,128)(2,1)S(1)}, u32[]{:S(2)}, u32[]{:S(2)}) collective-permute-start(bf16[512,128]{1,0:T(8,128)(2,1)} %add_convert_fusion.4), channel_id=1, source_target_pairs={{0,8},{1,9},{2,10},{3,11},{4,12},{5,13},{6,14},{7,15},{8,0},{9,1},... | collective-permute-start | bytes 393224 | tf_op jit(solution)/shard_map/ppermute | solution.py:299
  59.4 10.1 %collective-permute-start.16 = (bf16[512,256]{1,0:T(8,128)(2,1)}, bf16[512,256]{1,0:T(8,128)(2,1)}, u32[]{:S(2)}, u32[]{:S(2)}) collective-permute-start(bf16[512,256]{1,0:T(8,128)(2,1)} %add_convert_fusion.1), channel_id=1, source_target_pairs={{0,4},{1,5},{2,6},{3,7},{4,0},{5,1},{6,2},{7,3},{8,12},{9,13},{10,... | collective-permute-start | bytes 786440 | tf_op jit(solution)/shard_map/ppermute | solution.py:299
  61.5 8.0 %collective-permute-start.23 = (bf16[512,128]{1,0:T(8,128)(2,1)}, bf16[512,128]{1,0:T(8,128)(2,1)}, u32[]{:S(2)}, u32[]{:S(2)}) collective-permute-start(bf16[512,128]{1,0:T(8,128)(2,1)} %add_convert_fusion.2), channel_id=1, source_target_pairs={{0,8},{1,9},{2,10},{3,11},{4,12},{5,13},{6,14},{7,15},{8,0},{9,1},... | collective-permute-start | bytes 393224 | tf_op jit(solution)/shard_map/ppermute | solution.py:299
  70.8 4.2 %collective-permute-start.24 = (bf16[256,256]{1,0:T(8,128)(2,1)S(1)}, bf16[256,256]{1,0:T(8,128)(2,1)S(1)}, u32[]{:S(2)}, u32[]{:S(2)}) collective-permute-start(bf16[256,256]{1,0:T(8,128)(2,1)S(1)} %get-tuple-element.31), channel_id=1, source_target_pairs={{0,1},{1,0},{2,3},{3,2},{4,5},{5,4},{6,7},{7,6},{8,9},{9,8},{10,11... | collective-permute-start | bytes 393224 | tf_op jit(solution)/shard_map/ppermute | solution.py:299
  (4 other events, 41.6 us)

commit v6 on v5

--- a/solution.py
+++ b/solution.py
@@ -277,7 +277,7 @@
 def last_step(own, other, ket):
     rows, kh = own.shape
     orbitals = ket.shape[2]
-    group = 8
+    group = 4
     count = orbitals // group
     vmem = pl.BlockSpec(memory_space=pltpu.VMEM)
     return pl.pallas_call(
@@ -345,7 +345,8 @@
     swap = functools.partial(permute, mask=1, count=count)
 
     numbers = jnp.concatenate([first_block, second_block, slot_counts, ket_first, ket_second])
-    mine = coefficients.T.at[mo_index].get(
+    wanted = mo_index + (numbers[-mo_index.shape[0] :] < 0).astype(jnp.int32)
+    mine = coefficients.T.at[wanted].get(
         mode="promise_in_bounds", wrap_negative_indices=False
     )
     orbitals = mine.shape[0]

time: 77.9 us -> 75 us (0.963)
  the two profiles are of different devices: /device:TPU:5 before, /device:TPU:0 now
where the time goes in v6:
time: 75 us; the launch traced here: 74 us
  starting transfers between devices  33.4 us (45%)
  waiting for transfers between devices  18.8 us (25%)
  Pallas kernels  9.98 us (13%)
  other arithmetic  6.55 us (9%)
  local copies, waits for them, and re-layouts  2.75 us (4%)
  between operations  2.51 us (3%)
    ppermute x25, starting transfers between devices, permute(): return lax.ppermute(array, 'pan', [(i, i ^ mask) for i in range(count)])  33.4 us
    ppermute x25, waiting for transfers between devices, permute(): return lax.ppermute(array, 'pan', [(i, i ^ mask) for i in range(count)])  18.8 us
    pallas_call x1, Pallas kernels, bra_transform(): pl.pallas_call(functools.partial(bra_kernel, regions, locate, chunk, piec...  7.35 us
    convert_element_type x6, other arithmetic, added(): return result.astype(BF)  3.53 us
    pallas_call x1, Pallas kernels, last_step(): pl.pallas_call(last_kernel, out_shape=jax.ShapeDtypeStruct((rows, orbital...  2.63 us
  transfers between devices with their start and end apart: 25, of which 10 were waited for; matrix products, arithmetic and copies ran while one was open for 10% of the time, Pallas kernels for 0%

profile of v6, /device:TPU:0, one launch (start us, length us, event | category | flops | bytes accessed | tf_op | source)
XLA Modules:
  0.0 74.0 jit_solution(6019790924126025925)
XLA Ops:
  1.3 0.8 %concatenate.6.mine = s32[89]{0:T(128)S(1)} concatenate(s32[40]{0:T(128)} %param.9, s32[40]{0:T(128)} %param.10, s32[1]{0:T(128)S(6)} %copy.9, s32[4]{0:T(128)} %param.12, s32[4]{0:T(128)} %param.13), dimensions={0} | concatenate | bytes 712 | tf_op jit(solution)/shard_map/concatenate | solution.py:347
  3.6 2.6 %collective-permute-start.8 = (bf16[32,768]{1,0:T(8,128)(2,1)S(1)}, bf16[32,768]{1,0:T(8,128)(2,1)S(1)}, u32[]{:S(2)}, u32[]{:S(2)}) collective-permute-start(bf16[32,768]{1,0:T(8,128)(2,1)S(1)} %get-tuple-element.37), channel_id=1, source_target_pairs={{0,2},{1,3},{2,0},{3,1},{4,6},{5,7},{6,4},{7,5},{8,10},{9,11},{10,... | collective-permute-start | bytes 147464 | tf_op jit(solution)/shard_map/ppermute | solution.py:299
  6.2 1.6 %collective-permute-start.2 = (bf16[32,768]{1,0:T(8,128)(2,1)S(1)}, bf16[32,768]{1,0:T(8,128)(2,1)S(1)}, u32[]{:S(2)}, u32[]{:S(2)}) collective-permute-start(bf16[32,768]{1,0:T(8,128)(2,1)S(1)} %get-tuple-element.38), channel_id=1, source_target_pairs={{0,4},{1,5},{2,6},{3,7},{4,0},{5,1},{6,2},{7,3},{8,12},{9,13},{10,... | collective-permute-start | bytes 147464 | tf_op jit(solution)/shard_map/ppermute | solution.py:299
  7.8 2.6 %collective-permute-start.3 = (bf16[32,768]{1,0:T(8,128)(2,1)S(1)}, bf16[32,768]{1,0:T(8,128)(2,1)S(1)}, u32[]{:S(2)}, u32[]{:S(2)}) collective-permute-start(bf16[32,768]{1,0:T(8,128)(2,1)S(1)} %get-tuple-element.38), channel_id=1, source_target_pairs={{0,8},{1,9},{2,10},{3,11},{4,12},{5,13},{6,14},{7,15},{8,0},{9,1},... | collective-permute-start | bytes 147464 | tf_op jit(solution)/shard_map/ppermute | solution.py:299
  11.4 3.5 %collective-permute-start.10 = (bf16[2,32,768]{2,1,0:T(8,128)(2,1)S(1)}, bf16[2,32,768]{2,1,0:T(8,128)(2,1)S(1)}, u32[]{:S(2)}, u32[]{:S(2)}) collective-permute-start(bf16[2,32,768]{2,1,0:T(8,128)(2,1)S(1)} %get-tuple-element.34), channel_id=1, source_target_pairs={{0,8},{1,9},{2,10},{3,11},{4,12},{5,13},{6,14},{7,15},{8,0},{9,1},... | collective-permute-start | bytes 294920 | tf_op jit(solution)/shard_map/ppermute | solution.py:299
  15.8 1.2 %collective-permute-done.4 = bf16[32,768]{1,0:T(8,128)(2,1)S(1)} collective-permute-done((bf16[32,768]{1,0:T(8,128)(2,1)S(1)}, bf16[32,768]{1,0:T(8,128)(2,1)S(1)}, u32[]{:S(2)}, u32[]{:S(2)}) %collective-permute-start.4) | collective-permute-done | bytes 49184 | tf_op jit(solution)/shard_map/ppermute | solution.py:299
  17.7 5.1 %collective-permute-done.10 = bf16[2,32,768]{2,1,0:T(8,128)(2,1)S(1)} collective-permute-done((bf16[2,32,768]{2,1,0:T(8,128)(2,1)S(1)}, bf16[2,32,768]{2,1,0:T(8,128)(2,1)S(1)}, u32[]{:S(2)}, u32[]{:S(2)}) %collective-permute-start.10) | collective-permute-done | bytes 98336 | tf_op jit(solution)/shard_map/ppermute | solution.py:299
  22.7 0.8 %maximum_add_fusion.refs_4_ = bf16[4,2,32,768]{3,2,1,0:T(8,128)(2,1)} fusion(bf16[1,2,32,768]{3,2,1,0:T(8,128)(2,1)S(1)} %bitcast.26, bf16[1,2,32,768]{3,2,1,0:T(8,128)(2,1)S(1)} %bitcast.25, bf16[1,2,32,768]{3,2,1,0:T(8,128)(2,1)S(1)} %bitcast.24, bf16[1,2,32,768]{3,2,1,0:T(8,128)(2,1)S(1)} %get-tuple-element.33, bf16[]{:T(256)} %bitcast.13), kind=kLoop, calls=%fused_computation.3 | loop fusion | flops 786432 | bytes 786434 | tf_op jit(solution)/shard_map/add | solution.py:322
  24.0 1.4 %collective-permute-done.5.refs_1_ = bf16[4,32,768]{2,1,0:T(8,128)(2,1)} collective-permute-done((bf16[4,32,768]{2,1,0:T(8,128)(2,1)S(1)}, bf16[4,32,768]{2,1,0:T(8,128)(2,1)}, u32[]{:S(2)}, u32[]{:S(2)}) %collective-permute-start.5) | collective-permute-done | bytes 196640 | tf_op jit(solution)/shard_map/ppermute | solution.py:299
  26.1 7.3 %bra_transform.1 = (bf16[512,128]{1,0:T(8,128)(2,1)S(1)}, bf16[512,128]{1,0:T(8,128)(2,1)S(1)}, bf16[512,128]{1,0:T(8,128)(2,1)S(1)}, bf16[512,128]{1,0:T(8,128)...) custom-call(s32[1]{0:T(128)} %bitcast.me_ref, ...), custom_call_target="tpu_custom_call" | custom-call | flops 2684354560 | bytes 8388608 | tf_op jit(solution)/shard_map/bra_transform/pallas_call | solution.py:211
  34.2 5.2 %collective-permute-start.13 = (bf16[512,128]{1,0:T(8,128)(2,1)S(1)}, bf16[512,128]{1,0:T(8,128)(2,1)S(1)}, u32[]{:S(2)}, u32[]{:S(2)}) collective-permute-start(bf16[512,128]{1,0:T(8,128)(2,1)S(1)} %get-tuple-element.21), channel_id=1, source_target_pairs={{0,2},{1,3},{2,0},{3,1},{4,6},{5,7},{6,4},{7,5},{8,10},{9,11},{10,... | collective-permute-start | bytes 393224 | tf_op jit(solution)/shard_map/ppermute | solution.py:299
  39.4 2.0 %collective-permute-start.21 = (bf16[512,128]{1,0:T(8,128)(2,1)S(1)}, bf16[512,128]{1,0:T(8,128)(2,1)S(1)}, u32[]{:S(2)}, u32[]{:S(2)}) collective-permute-start(bf16[512,128]{1,0:T(8,128)(2,1)S(1)} %get-tuple-element.29), channel_id=1, source_target_pairs={{0,2},{1,3},{2,0},{3,1},{4,6},{5,7},{6,4},{7,5},{8,10},{9,11},{10,... | collective-permute-start | bytes 393224 | tf_op jit(solution)/shard_map/ppermute | solution.py:299
  41.5 2.2 %collective-permute-done.13 = bf16[512,128]{1,0:T(8,128)(2,1)S(1)} collective-permute-done((bf16[512,128]{1,0:T(8,128)(2,1)S(1)}, bf16[512,128]{1,0:T(8,128)(2,1)S(1)}, u32[]{:S(2)}, u32[]{:S(2)}) %collective-permute-start.13) | collective-permute-done | bytes 131104 | tf_op jit(solution)/shard_map/ppermute | solution.py:299
  43.7 3.0 %collective-permute-start.18 = (bf16[512,128]{1,0:T(8,128)(2,1)S(1)}, bf16[512,128]{1,0:T(8,128)(2,1)S(1)}, u32[]{:S(2)}, u32[]{:S(2)}) collective-permute-start(bf16[512,128]{1,0:T(8,128)(2,1)S(1)} %add_convert_fusion.5), channel_id=1, source_target_pairs={{0,4},{1,5},{2,6},{3,7},{4,0},{5,1},{6,2},{7,3},{8,12},{9,13},{10,... | collective-permute-start | bytes 393224 | tf_op jit(solution)/shard_map/ppermute | solution.py:299
  49.4 3.0 %collective-permute-start.22 = (bf16[512,128]{1,0:T(8,128)(2,1)S(1)}, bf16[512,128]{1,0:T(8,128)(2,1)S(1)}, u32[]{:S(2)}, u32[]{:S(2)}) collective-permute-start(bf16[512,128]{1,0:T(8,128)(2,1)S(1)} %add_convert_fusion.3), channel_id=1, source_target_pairs={{0,4},{1,5},{2,6},{3,7},{4,0},{5,1},{6,2},{7,3},{8,12},{9,13},{10,... | collective-permute-start | bytes 393224 | tf_op jit(solution)/shard_map/ppermute | solution.py:299
  53.8 1.8 %collective-permute-start.19 = (bf16[512,128]{1,0:T(8,128)(2,1)}, bf16[512,128]{1,0:T(8,128)(2,1)S(1)}, u32[]{:S(2)}, u32[]{:S(2)}) collective-permute-start(bf16[512,128]{1,0:T(8,128)(2,1)} %add_convert_fusion.4), channel_id=1, source_target_pairs={{0,8},{1,9},{2,10},{3,11},{4,12},{5,13},{6,14},{7,15},{8,0},{9,1},... | collective-permute-start | bytes 393224 | tf_op jit(solution)/shard_map/ppermute | solution.py:299
  55.6 0.8 %add_convert_fusion.1 = bf16[512,256]{1,0:T(8,128)(2,1)} fusion(bf16[512,256]{1,0:T(8,128)(2,1)S(1)} %collective-permute-done.15, bf16[512,256]{1,0:T(8,128)(2,1)S(1)} %get-tuple-element.22), kind=kLoop, calls=%fused_computation.2 | loop fusion | flops 524288 | bytes 786432 | tf_op jit(solution)/shard_map/convert_element_type | solution.py:306
  56.3 2.3 %collective-permute-start.16 = (bf16[512,256]{1,0:T(8,128)(2,1)}, bf16[512,256]{1,0:T(8,128)(2,1)}, u32[]{:S(2)}, u32[]{:S(2)}) collective-permute-start(bf16[512,256]{1,0:T(8,128)(2,1)} %add_convert_fusion.1), channel_id=1, source_target_pairs={{0,4},{1,5},{2,6},{3,7},{4,0},{5,1},{6,2},{7,3},{8,12},{9,13},{10,... | collective-permute-start | bytes 786440 | tf_op jit(solution)/shard_map/ppermute | solution.py:299
  59.3 2.9 %collective-permute-start.23 = (bf16[512,128]{1,0:T(8,128)(2,1)}, bf16[512,128]{1,0:T(8,128)(2,1)}, u32[]{:S(2)}, u32[]{:S(2)}) collective-permute-start(bf16[512,128]{1,0:T(8,128)(2,1)} %add_convert_fusion.2), channel_id=1, source_target_pairs={{0,8},{1,9},{2,10},{3,11},{4,12},{5,13},{6,14},{7,15},{8,0},{9,1},... | collective-permute-start | bytes 393224 | tf_op jit(solution)/shard_map/ppermute | solution.py:299
  62.3 4.6 %collective-permute-done.23 = bf16[512,128]{1,0:T(8,128)(2,1)} collective-permute-done((bf16[512,128]{1,0:T(8,128)(2,1)}, bf16[512,128]{1,0:T(8,128)(2,1)}, u32[]{:S(2)}, u32[]{:S(2)}) %collective-permute-start.23) | collective-permute-done | bytes 131104 | tf_op jit(solution)/shard_map/ppermute | solution.py:299
  66.9 1.6 %collective-permute-done.16 = bf16[512,256]{1,0:T(8,128)(2,1)} collective-permute-done((bf16[512,256]{1,0:T(8,128)(2,1)}, bf16[512,256]{1,0:T(8,128)(2,1)}, u32[]{:S(2)}, u32[]{:S(2)}) %collective-permute-start.16) | collective-permute-done | bytes 262176 | tf_op jit(solution)/shard_map/ppermute | solution.py:299
  68.5 1.3 %add_convert_fusion = bf16[512,256]{1,0:T(8,128)(2,1)S(1)} fusion(bf16[512,256]{1,0:T(8,128)(2,1)} %collective-permute-done.16, bf16[512,256]{1,0:T(8,128)(2,1)} %collective-permute-done.14, bf16[512,256]{1,0:T(8,128)(2,1)} %copy-done.2, bf16[512,128]{1,0:T(8,128)(2,1)} %collective-permute-done.23, bf16[512,128]{1,0:T(8,128)(2,1)S(1)} %collective-permute-done.19), kind=kLoop, calls=%fused_computation.1 | loop fusion | flops 1441792 | bytes 1310720 | tf_op jit(solution)/shard_map/convert_element_type | solution.py:306
  69.9 1.3 %collective-permute-done.24.other = bf16[256,256]{1,0:T(8,128)(2,1)S(1)} collective-permute-done((bf16[256,256]{1,0:T(8,128)(2,1)S(1)}, bf16[256,256]{1,0:T(8,128)(2,1)S(1)}, u32[]{:S(2)}, u32[]{:S(2)}) %collective-permute-start.24) | collective-permute-done | bytes 131104 | tf_op jit(solution)/shard_map/ppermute | solution.py:299
  71.2 2.6 %last_step.1 = f32[256,4096]{1,0:T(8,128)} custom-call(bf16[256,256]{1,0:T(8,128)(2,1)S(1)} %get-tuple-element.32.own, bf16[256,256]{1,0:T(8,128)(2,1)S(1)} %collective-permute-done.24.other, f32[2,4,64,128]{3,2,1,0:T(8,128)S(1)} %copy-done.1), custom_call_target="tpu_custom_call" | custom-call | tf_op jit(solution)/shard_map/last_step/pallas_call | solution.py:283
  (53 shorter events, 10.1 us)
Async XLA Ops:
  0.0 11.4 %collective-permute-start = (bf16[40,512,128]{2,1,0:T(8,128)(2,1)}, bf16[40,512,128]{2,1,0:T(8,128)(2,1)}, u32[]{:S(2)}, u32[]{:S(2)}) collective-permute-start(bf16[40,512,128]{2,1,0:T(8,128)(2,1)} %refs_6_.1), channel_id=1, source_target_pairs={{0,1},{1,0},{2,3},{3,2},{4,5},{5,4},{6,7},{7,6},{8,9},{9,8},{10,11... | collective-permute-start | bytes 15728648 | tf_op jit(solution)/shard_map/ppermute | solution.py:299
  3.6 7.0 %collective-permute-start.8 = (bf16[32,768]{1,0:T(8,128)(2,1)S(1)}, bf16[32,768]{1,0:T(8,128)(2,1)S(1)}, u32[]{:S(2)}, u32[]{:S(2)}) collective-permute-start(bf16[32,768]{1,0:T(8,128)(2,1)S(1)} %get-tuple-element.37), channel_id=1, source_target_pairs={{0,2},{1,3},{2,0},{3,1},{4,6},{5,7},{6,4},{7,5},{8,10},{9,11},{10,... | collective-permute-start | bytes 147464 | tf_op jit(solution)/shard_map/ppermute | solution.py:299
  6.2 9.3 %collective-permute-start.2 = (bf16[32,768]{1,0:T(8,128)(2,1)S(1)}, bf16[32,768]{1,0:T(8,128)(2,1)S(1)}, u32[]{:S(2)}, u32[]{:S(2)}) collective-permute-start(bf16[32,768]{1,0:T(8,128)(2,1)S(1)} %get-tuple-element.38), channel_id=1, source_target_pairs={{0,4},{1,5},{2,6},{3,7},{4,0},{5,1},{6,2},{7,3},{8,12},{9,13},{10,... | collective-permute-start | bytes 147464 | tf_op jit(solution)/shard_map/ppermute | solution.py:299
  7.8 8.0 %collective-permute-start.3 = (bf16[32,768]{1,0:T(8,128)(2,1)S(1)}, bf16[32,768]{1,0:T(8,128)(2,1)S(1)}, u32[]{:S(2)}, u32[]{:S(2)}) collective-permute-start(bf16[32,768]{1,0:T(8,128)(2,1)S(1)} %get-tuple-element.38), channel_id=1, source_target_pairs={{0,8},{1,9},{2,10},{3,11},{4,12},{5,13},{6,14},{7,15},{8,0},{9,1},... | collective-permute-start | bytes 147464 | tf_op jit(solution)/shard_map/ppermute | solution.py:299
  10.4 6.5 %collective-permute-start.4 = (bf16[32,768]{1,0:T(8,128)(2,1)S(1)}, bf16[32,768]{1,0:T(8,128)(2,1)S(1)}, u32[]{:S(2)}, u32[]{:S(2)}) collective-permute-start(bf16[32,768]{1,0:T(8,128)(2,1)S(1)} %get-tuple-element.38), channel_id=1, source_target_pairs={{0,12},{1,13},{2,14},{3,15},{4,8},{5,9},{6,10},{7,11},{8,4},{9,5},... | collective-permute-start | bytes 147464 | tf_op jit(solution)/shard_map/ppermute | solution.py:299
  10.6 7.0 %collective-permute-start.9 = (bf16[2,32,768]{2,1,0:T(8,128)(2,1)S(1)}, bf16[2,32,768]{2,1,0:T(8,128)(2,1)S(1)}, u32[]{:S(2)}, u32[]{:S(2)}) collective-permute-start(bf16[2,32,768]{2,1,0:T(8,128)(2,1)S(1)} %get-tuple-element.34), channel_id=1, source_target_pairs={{0,4},{1,5},{2,6},{3,7},{4,0},{5,1},{6,2},{7,3},{8,12},{9,13},{10,... | collective-permute-start | bytes 294920 | tf_op jit(solution)/shard_map/ppermute | solution.py:299
  11.4 11.4 %collective-permute-start.10 = (bf16[2,32,768]{2,1,0:T(8,128)(2,1)S(1)}, bf16[2,32,768]{2,1,0:T(8,128)(2,1)S(1)}, u32[]{:S(2)}, u32[]{:S(2)}) collective-permute-start(bf16[2,32,768]{2,1,0:T(8,128)(2,1)S(1)} %get-tuple-element.34), channel_id=1, source_target_pairs={{0,8},{1,9},{2,10},{3,11},{4,12},{5,13},{6,14},{7,15},{8,0},{9,1},... | collective-permute-start | bytes 294920 | tf_op jit(solution)/shard_map/ppermute | solution.py:299
  15.5 7.2 %collective-permute-start.11 = (bf16[2,32,768]{2,1,0:T(8,128)(2,1)S(1)}, bf16[2,32,768]{2,1,0:T(8,128)(2,1)S(1)}, u32[]{:S(2)}, u32[]{:S(2)}) collective-permute-start(bf16[2,32,768]{2,1,0:T(8,128)(2,1)S(1)} %get-tuple-element.34), channel_id=1, source_target_pairs={{0,12},{1,13},{2,14},{3,15},{4,8},{5,9},{6,10},{7,11},{8,4},{9,5},... | collective-permute-start | bytes 294920 | tf_op jit(solution)/shard_map/ppermute | solution.py:299
  15.8 1.8 %collective-permute-start.1 = (s32[89]{0:T(128)S(1)}, s32[89]{0:T(128)S(1)}, u32[]{:S(2)}, u32[]{:S(2)}) collective-permute-start(s32[89]{0:T(128)S(1)} %fusion.1), channel_id=1, source_target_pairs={{0,1},{1,0},{2,3},{3,2},{4,5},{5,4},{6,7},{7,6},{8,9},{9,8},{10,11... | collective-permute-start | bytes 1076 | tf_op jit(solution)/shard_map/ppermute | solution.py:299
  16.9 7.1 %collective-permute-start.6 = (bf16[4,32,768]{2,1,0:T(8,128)(2,1)S(1)}, bf16[4,32,768]{2,1,0:T(8,128)(2,1)S(1)}, u32[]{:S(2)}, u32[]{:S(2)}) collective-permute-start(bf16[4,32,768]{2,1,0:T(8,128)(2,1)S(1)} %pad_maximum_fusion.refs_0_), channel_id=1, source_target_pairs={{0,2},{1,3},{2,0},{3,1},{4,6},{5,7},{6,4},{7,5},{8,10},{9,11},{10,... | collective-permute-start | bytes 589832 | tf_op jit(solution)/shard_map/ppermute | solution.py:299
  23.5 2.6 %collective-permute-start.12 = (bf16[4,2,32,768]{3,2,1,0:T(8,128)(2,1)}, bf16[4,2,32,768]{3,2,1,0:T(8,128)(2,1)}, u32[]{:S(2)}, u32[]{:S(2)}) collective-permute-start(bf16[4,2,32,768]{3,2,1,0:T(8,128)(2,1)} %maximum_add_fusion.refs_4_), channel_id=1, source_target_pairs={{0,1},{1,0},{2,3},{3,2},{4,5},{5,4},{6,7},{7,6},{8,9},{9,8},{10,11... | collective-permute-start | bytes 1179656 | tf_op jit(solution)/shard_map/ppermute | solution.py:299
  23.5 1.9 %collective-permute-start.5 = (bf16[4,32,768]{2,1,0:T(8,128)(2,1)S(1)}, bf16[4,32,768]{2,1,0:T(8,128)(2,1)}, u32[]{:S(2)}, u32[]{:S(2)}) collective-permute-start(bf16[4,32,768]{2,1,0:T(8,128)(2,1)S(1)} %pad_maximum_fusion.refs_0_), channel_id=1, source_target_pairs={{0,1},{1,0},{2,3},{3,2},{4,5},{5,4},{6,7},{7,6},{8,9},{9,8},{10,11... | collective-permute-start | bytes 589832 | tf_op jit(solution)/shard_map/ppermute | solution.py:299
  24.0 1.9 %collective-permute-start.7 = (bf16[4,32,768]{2,1,0:T(8,128)(2,1)S(1)}, bf16[4,32,768]{2,1,0:T(8,128)(2,1)}, u32[]{:S(2)}, u32[]{:S(2)}) collective-permute-start(bf16[4,32,768]{2,1,0:T(8,128)(2,1)S(1)} %collective-permute-done.6.refs_2_), channel_id=1, source_target_pairs={{0,1},{1,0},{2,3},{3,2},{4,5},{5,4},{6,7},{7,6},{8,9},{9,8},{10,11... | collective-permute-start | bytes 589832 | tf_op jit(solution)/shard_map/ppermute | solution.py:299
  34.2 9.5 %collective-permute-start.13 = (bf16[512,128]{1,0:T(8,128)(2,1)S(1)}, bf16[512,128]{1,0:T(8,128)(2,1)S(1)}, u32[]{:S(2)}, u32[]{:S(2)}) collective-permute-start(bf16[512,128]{1,0:T(8,128)(2,1)S(1)} %get-tuple-element.21), channel_id=1, source_target_pairs={{0,2},{1,3},{2,0},{3,1},{4,6},{5,7},{6,4},{7,5},{8,10},{9,11},{10,... | collective-permute-start | bytes 393224 | tf_op jit(solution)/shard_map/ppermute | solution.py:299
  39.4 13.7 %collective-permute-start.17 = (bf16[512,128]{1,0:T(8,128)(2,1)S(1)}, bf16[512,128]{1,0:T(8,128)(2,1)S(1)}, u32[]{:S(2)}, u32[]{:S(2)}) collective-permute-start(bf16[512,128]{1,0:T(8,128)(2,1)S(1)} %get-tuple-element.25), channel_id=1, source_target_pairs={{0,2},{1,3},{2,0},{3,1},{4,6},{5,7},{6,4},{7,5},{8,10},{9,11},{10,... | collective-permute-start | bytes 393224 | tf_op jit(solution)/shard_map/ppermute | solution.py:299
  39.4 9.9 %collective-permute-start.21 = (bf16[512,128]{1,0:T(8,128)(2,1)S(1)}, bf16[512,128]{1,0:T(8,128)(2,1)S(1)}, u32[]{:S(2)}, u32[]{:S(2)}) collective-permute-start(bf16[512,128]{1,0:T(8,128)(2,1)S(1)} %get-tuple-element.29), channel_id=1, source_target_pairs={{0,2},{1,3},{2,0},{3,1},{4,6},{5,7},{6,4},{7,5},{8,10},{9,11},{10,... | collective-permute-start | bytes 393224 | tf_op jit(solution)/shard_map/ppermute | solution.py:299
  41.4 14.1 %collective-permute-start.15 = (bf16[512,256]{1,0:T(8,128)(2,1)S(1)}, bf16[512,256]{1,0:T(8,128)(2,1)S(1)}, u32[]{:S(2)}, u32[]{:S(2)}) collective-permute-start(bf16[512,256]{1,0:T(8,128)(2,1)S(1)} %get-tuple-element.23), channel_id=1, source_target_pairs={{0,2},{1,3},{2,0},{3,1},{4,6},{5,7},{6,4},{7,5},{8,10},{9,11},{10,... | collective-permute-start | bytes 786440 | tf_op jit(solution)/shard_map/ppermute | solution.py:299
  43.7 9.3 %collective-permute-start.18 = (bf16[512,128]{1,0:T(8,128)(2,1)S(1)}, bf16[512,128]{1,0:T(8,128)(2,1)S(1)}, u32[]{:S(2)}, u32[]{:S(2)}) collective-permute-start(bf16[512,128]{1,0:T(8,128)(2,1)S(1)} %add_convert_fusion.5), channel_id=1, source_target_pairs={{0,4},{1,5},{2,6},{3,7},{4,0},{5,1},{6,2},{7,3},{8,12},{9,13},{10,... | collective-permute-start | bytes 393224 | tf_op jit(solution)/shard_map/ppermute | solution.py:299
  48.6 10.1 %collective-permute-start.20 = (bf16[512,128]{1,0:T(8,128)(2,1)S(1)}, bf16[512,128]{1,0:T(8,128)(2,1)S(1)}, u32[]{:S(2)}, u32[]{:S(2)}) collective-permute-start(bf16[512,128]{1,0:T(8,128)(2,1)S(1)} %broadcast_add_fusion.1), channel_id=1, source_target_pairs={{0,2},{1,3},{2,0},{3,1},{4,6},{5,7},{6,4},{7,5},{8,10},{9,11},{10,... | collective-permute-start | bytes 393224 | tf_op jit(solution)/shard_map/ppermute | solution.py:299
  49.4 9.3 %collective-permute-start.22 = (bf16[512,128]{1,0:T(8,128)(2,1)S(1)}, bf16[512,128]{1,0:T(8,128)(2,1)S(1)}, u32[]{:S(2)}, u32[]{:S(2)}) collective-permute-start(bf16[512,128]{1,0:T(8,128)(2,1)S(1)} %add_convert_fusion.3), channel_id=1, source_target_pairs={{0,4},{1,5},{2,6},{3,7},{4,0},{5,1},{6,2},{7,3},{8,12},{9,13},{10,... | collective-permute-start | bytes 393224 | tf_op jit(solution)/shard_map/ppermute | solution.py:299
  53.1 13.8 %collective-permute-start.14 = (bf16[512,256]{1,0:T(8,128)(2,1)}, bf16[512,256]{1,0:T(8,128)(2,1)}, u32[]{:S(2)}, u32[]{:S(2)}) collective-permute-start(bf16[512,256]{1,0:T(8,128)(2,1)} %broadcast_add_fusion), channel_id=1, source_target_pairs={{0,2},{1,3},{2,0},{3,1},{4,6},{5,7},{6,4},{7,5},{8,10},{9,11},{10,... | collective-permute-start | bytes 786440 | tf_op jit(solution)/shard_map/ppermute | solution.py:299
  53.8 8.5 %collective-permute-start.19 = (bf16[512,128]{1,0:T(8,128)(2,1)}, bf16[512,128]{1,0:T(8,128)(2,1)S(1)}, u32[]{:S(2)}, u32[]{:S(2)}) collective-permute-start(bf16[512,128]{1,0:T(8,128)(2,1)} %add_convert_fusion.4), channel_id=1, source_target_pairs={{0,8},{1,9},{2,10},{3,11},{4,12},{5,13},{6,14},{7,15},{8,0},{9,1},... | collective-permute-start | bytes 393224 | tf_op jit(solution)/shard_map/ppermute | solution.py:299
  56.3 12.2 %collective-permute-start.16 = (bf16[512,256]{1,0:T(8,128)(2,1)}, bf16[512,256]{1,0:T(8,128)(2,1)}, u32[]{:S(2)}, u32[]{:S(2)}) collective-permute-start(bf16[512,256]{1,0:T(8,128)(2,1)} %add_convert_fusion.1), channel_id=1, source_target_pairs={{0,4},{1,5},{2,6},{3,7},{4,0},{5,1},{6,2},{7,3},{8,12},{9,13},{10,... | collective-permute-start | bytes 786440 | tf_op jit(solution)/shard_map/ppermute | solution.py:299
  59.3 7.6 %collective-permute-start.23 = (bf16[512,128]{1,0:T(8,128)(2,1)}, bf16[512,128]{1,0:T(8,128)(2,1)}, u32[]{:S(2)}, u32[]{:S(2)}) collective-permute-start(bf16[512,128]{1,0:T(8,128)(2,1)} %add_convert_fusion.2), channel_id=1, source_target_pairs={{0,8},{1,9},{2,10},{3,11},{4,12},{5,13},{6,14},{7,15},{8,0},{9,1},... | collective-permute-start | bytes 393224 | tf_op jit(solution)/shard_map/ppermute | solution.py:299
  (4 other events, 42.0 us)

commit v7 on v6

--- a/solution.py
+++ b/solution.py
@@ -387,7 +387,8 @@
     if small:
         chunk, side = orbitals // 8, kh // 2
         order = ((3, 0, side), (2, 0, side), (3, side, kh), (2, side, kh), (1, 0, kh), (0, 0, kh))
-        pieces = order + tuple((s + 4, a, b) for s, a, b in order)
+        pieces = order + tuple((s + 4, a, b) for s, a, b in order[:5])
+        pieces += ((4, 0, side), (4, side, kh))
         *partial, ket = bra(chunk, pieces, BF)
         there, here = partial[:6], partial[6:]
         three_a = added(here[0], permute(there[0], 2, count))
@@ -398,7 +399,7 @@
         one = permute(added(here[4], permute(there[4], 2, count)), 4, count)
         zero = permute(there[5] + nothing, 2, count)
         two = jnp.concatenate([permute(two_a, 8, count), permute(two_b, 8, count)], axis=1)
-        done = added(here[5], zero, one, two)
+        done = added(jnp.concatenate(here[5:], axis=1), zero, one, two)
     else:
         partial, ket = bra(orbitals, ((0, 0, kh),), F32)
         sides = [list(range(c, count, 2)) for c in range(2)]

time: 75 us -> 76.2 us (1.016)
  the two profiles are of different devices: /device:TPU:0 before, /device:TPU:5 now
where the time goes in v7:
time: 76.2 us; the launch traced here: 76.1 us
  starting transfers between devices  36.2 us (48%)
  waiting for transfers between devices  17.2 us (23%)
  Pallas kernels  11.6 us (15%)
  other arithmetic  6.57 us (9%)
  between operations  2.55 us (3%)
  local copies, waits for them, and re-layouts  2.06 us (3%)
    ppermute x25, starting transfers between devices, permute(): return lax.ppermute(array, 'pan', [(i, i ^ mask) for i in range(count)])  36.2 us
    ppermute x25, waiting for transfers between devices, permute(): return lax.ppermute(array, 'pan', [(i, i ^ mask) for i in range(count)])  17.2 us
    pallas_call x1, Pallas kernels, bra_transform(): pl.pallas_call(functools.partial(bra_kernel, regions, locate, chunk, piec...  8.98 us
    convert_element_type x6, other arithmetic, added(): return result.astype(BF)  3.57 us
    pallas_call x1, Pallas kernels, last_step(): pl.pallas_call(last_kernel, out_shape=jax.ShapeDtypeStruct((rows, orbital...  2.63 us
  transfers between devices with their start and end apart: 25, of which 12 were waited for; matrix products, arithmetic and copies ran while one was open for 10% of the time, Pallas kernels for 0%

profile of v7, /device:TPU:5, one launch (start us, length us, event | category | flops | bytes accessed | tf_op | source)
XLA Modules:
  0.0 76.1 jit_solution(18290226718715684786)
XLA Ops:
  3.8 1.3 %collective-permute-start.8 = (bf16[32,768]{1,0:T(8,128)(2,1)S(1)}, bf16[32,768]{1,0:T(8,128)(2,1)S(1)}, u32[]{:S(2)}, u32[]{:S(2)}) collective-permute-start(bf16[32,768]{1,0:T(8,128)(2,1)S(1)} %get-tuple-element.39), channel_id=1, source_target_pairs={{0,2},{1,3},{2,0},{3,1},{4,6},{5,7},{6,4},{7,5},{8,10},{9,11},{10,... | collective-permute-start | bytes 147464 | tf_op jit(solution)/shard_map/ppermute | solution.py:299
  5.1 1.3 %collective-permute-start.2 = (bf16[32,768]{1,0:T(8,128)(2,1)S(1)}, bf16[32,768]{1,0:T(8,128)(2,1)S(1)}, u32[]{:S(2)}, u32[]{:S(2)}) collective-permute-start(bf16[32,768]{1,0:T(8,128)(2,1)S(1)} %get-tuple-element.40), channel_id=1, source_target_pairs={{0,4},{1,5},{2,6},{3,7},{4,0},{5,1},{6,2},{7,3},{8,12},{9,13},{10,... | collective-permute-start | bytes 147464 | tf_op jit(solution)/shard_map/ppermute | solution.py:299
  6.4 2.3 %collective-permute-start.3 = (bf16[32,768]{1,0:T(8,128)(2,1)S(1)}, bf16[32,768]{1,0:T(8,128)(2,1)S(1)}, u32[]{:S(2)}, u32[]{:S(2)}) collective-permute-start(bf16[32,768]{1,0:T(8,128)(2,1)S(1)} %get-tuple-element.40), channel_id=1, source_target_pairs={{0,8},{1,9},{2,10},{3,11},{4,12},{5,13},{6,14},{7,15},{8,0},{9,1},... | collective-permute-start | bytes 147464 | tf_op jit(solution)/shard_map/ppermute | solution.py:299
  9.3 3.0 %collective-permute-start.10 = (bf16[2,32,768]{2,1,0:T(8,128)(2,1)S(1)}, bf16[2,32,768]{2,1,0:T(8,128)(2,1)S(1)}, u32[]{:S(2)}, u32[]{:S(2)}) collective-permute-start(bf16[2,32,768]{2,1,0:T(8,128)(2,1)S(1)} %get-tuple-element.36), channel_id=1, source_target_pairs={{0,8},{1,9},{2,10},{3,11},{4,12},{5,13},{6,14},{7,15},{8,0},{9,1},... | collective-permute-start | bytes 294920 | tf_op jit(solution)/shard_map/ppermute | solution.py:299
  13.4 1.6 %collective-permute-start.1 = (s32[89]{0:T(128)S(1)}, s32[89]{0:T(128)S(1)}, u32[]{:S(2)}, u32[]{:S(2)}) collective-permute-start(s32[89]{0:T(128)S(1)} %fusion.1), channel_id=1, source_target_pairs={{0,1},{1,0},{2,3},{3,2},{4,5},{5,4},{6,7},{7,6},{8,9},{9,8},{10,11... | collective-permute-start | bytes 1076 | tf_op jit(solution)/shard_map/ppermute | solution.py:299
  15.9 3.4 %collective-permute-done.11 = bf16[2,32,768]{2,1,0:T(8,128)(2,1)S(1)} collective-permute-done((bf16[2,32,768]{2,1,0:T(8,128)(2,1)S(1)}, bf16[2,32,768]{2,1,0:T(8,128)(2,1)S(1)}, u32[]{:S(2)}, u32[]{:S(2)}) %collective-permute-start.11) | collective-permute-done | bytes 98336 | tf_op jit(solution)/shard_map/ppermute | solution.py:299
  20.1 2.7 %collective-permute-start.12 = (bf16[4,2,32,768]{3,2,1,0:T(8,128)(2,1)}, bf16[4,2,32,768]{3,2,1,0:T(8,128)(2,1)}, u32[]{:S(2)}, u32[]{:S(2)}) collective-permute-start(bf16[4,2,32,768]{3,2,1,0:T(8,128)(2,1)} %maximum_add_fusion.refs_4_), channel_id=1, source_target_pairs={{0,1},{1,0},{2,3},{3,2},{4,5},{5,4},{6,7},{7,6},{8,9},{9,8},{10,11... | collective-permute-start | bytes 1179656 | tf_op jit(solution)/shard_map/ppermute | solution.py:299
  23.3 1.1 %collective-permute-done.5.refs_1_ = bf16[4,32,768]{2,1,0:T(8,128)(2,1)} collective-permute-done((bf16[4,32,768]{2,1,0:T(8,128)(2,1)S(1)}, bf16[4,32,768]{2,1,0:T(8,128)(2,1)}, u32[]{:S(2)}, u32[]{:S(2)}) %collective-permute-start.5) | collective-permute-done | bytes 196640 | tf_op jit(solution)/shard_map/ppermute | solution.py:299
  25.0 9.0 %bra_transform.1 = (bf16[512,128]{1,0:T(8,128)(2,1)S(1)}, bf16[512,128]{1,0:T(8,128)(2,1)S(1)}, bf16[512,128]{1,0:T(8,128)(2,1)S(1)}, bf16[512,128]{1,0:T(8,128)...) custom-call(s32[1]{0:T(128)} %bitcast.me_ref, ...), custom_call_target="tpu_custom_call" | custom-call | flops 2684354560 | bytes 8388608 | tf_op jit(solution)/shard_map/bra_transform/pallas_call | solution.py:211
  34.0 2.6 %collective-permute-start.13 = (bf16[512,128]{1,0:T(8,128)(2,1)S(1)}, bf16[512,128]{1,0:T(8,128)(2,1)S(1)}, u32[]{:S(2)}, u32[]{:S(2)}) collective-permute-start(bf16[512,128]{1,0:T(8,128)(2,1)S(1)} %get-tuple-element.23), channel_id=1, source_target_pairs={{0,2},{1,3},{2,0},{3,1},{4,6},{5,7},{6,4},{7,5},{8,10},{9,11},{10,... | collective-permute-start | bytes 393224 | tf_op jit(solution)/shard_map/ppermute | solution.py:299
  36.7 1.4 %collective-permute-start.21 = (bf16[512,128]{1,0:T(8,128)(2,1)S(1)}, bf16[512,128]{1,0:T(8,128)(2,1)S(1)}, u32[]{:S(2)}, u32[]{:S(2)}) collective-permute-start(bf16[512,128]{1,0:T(8,128)(2,1)S(1)} %get-tuple-element.31), channel_id=1, source_target_pairs={{0,2},{1,3},{2,0},{3,1},{4,6},{5,7},{6,4},{7,5},{8,10},{9,11},{10,... | collective-permute-start | bytes 393224 | tf_op jit(solution)/shard_map/ppermute | solution.py:299
  38.2 2.0 %collective-permute-done.13 = bf16[512,128]{1,0:T(8,128)(2,1)S(1)} collective-permute-done((bf16[512,128]{1,0:T(8,128)(2,1)S(1)}, bf16[512,128]{1,0:T(8,128)(2,1)S(1)}, u32[]{:S(2)}, u32[]{:S(2)}) %collective-permute-start.13) | collective-permute-done | bytes 131104 | tf_op jit(solution)/shard_map/ppermute | solution.py:299
  40.2 2.0 %collective-permute-start.18 = (bf16[512,128]{1,0:T(8,128)(2,1)S(1)}, bf16[512,128]{1,0:T(8,128)(2,1)S(1)}, u32[]{:S(2)}, u32[]{:S(2)}) collective-permute-start(bf16[512,128]{1,0:T(8,128)(2,1)S(1)} %add_convert_fusion.5), channel_id=1, source_target_pairs={{0,4},{1,5},{2,6},{3,7},{4,0},{5,1},{6,2},{7,3},{8,12},{9,13},{10,... | collective-permute-start | bytes 393224 | tf_op jit(solution)/shard_map/ppermute | solution.py:299
  44.1 1.2 %collective-permute-start.20 = (bf16[512,128]{1,0:T(8,128)(2,1)S(1)}, bf16[512,128]{1,0:T(8,128)(2,1)S(1)}, u32[]{:S(2)}, u32[]{:S(2)}) collective-permute-start(bf16[512,128]{1,0:T(8,128)(2,1)S(1)} %broadcast_add_fusion.1), channel_id=1, source_target_pairs={{0,2},{1,3},{2,0},{3,1},{4,6},{5,7},{6,4},{7,5},{8,10},{9,11},{10,... | collective-permute-start | bytes 393224 | tf_op jit(solution)/shard_map/ppermute | solution.py:299
  45.9 2.0 %collective-permute-start.22 = (bf16[512,128]{1,0:T(8,128)(2,1)S(1)}, bf16[512,128]{1,0:T(8,128)(2,1)S(1)}, u32[]{:S(2)}, u32[]{:S(2)}) collective-permute-start(bf16[512,128]{1,0:T(8,128)(2,1)S(1)} %add_convert_fusion.3), channel_id=1, source_target_pairs={{0,4},{1,5},{2,6},{3,7},{4,0},{5,1},{6,2},{7,3},{8,12},{9,13},{10,... | collective-permute-start | bytes 393224 | tf_op jit(solution)/shard_map/ppermute | solution.py:299
  48.6 1.1 %collective-permute-start.14 = (bf16[512,256]{1,0:T(8,128)(2,1)}, bf16[512,256]{1,0:T(8,128)(2,1)}, u32[]{:S(2)}, u32[]{:S(2)}) collective-permute-start(bf16[512,256]{1,0:T(8,128)(2,1)} %broadcast_add_fusion), channel_id=1, source_target_pairs={{0,2},{1,3},{2,0},{3,1},{4,6},{5,7},{6,4},{7,5},{8,10},{9,11},{10,... | collective-permute-start | bytes 786440 | tf_op jit(solution)/shard_map/ppermute | solution.py:299
  50.4 6.0 %collective-permute-start.19 = (bf16[512,128]{1,0:T(8,128)(2,1)}, bf16[512,128]{1,0:T(8,128)(2,1)S(1)}, u32[]{:S(2)}, u32[]{:S(2)}) collective-permute-start(bf16[512,128]{1,0:T(8,128)(2,1)} %add_convert_fusion.4), channel_id=1, source_target_pairs={{0,8},{1,9},{2,10},{3,11},{4,12},{5,13},{6,14},{7,15},{8,0},{9,1},... | collective-permute-start | bytes 393224 | tf_op jit(solution)/shard_map/ppermute | solution.py:299
  58.0 2.9 %collective-permute-start.23 = (bf16[512,128]{1,0:T(8,128)(2,1)}, bf16[512,128]{1,0:T(8,128)(2,1)}, u32[]{:S(2)}, u32[]{:S(2)}) collective-permute-start(bf16[512,128]{1,0:T(8,128)(2,1)} %add_convert_fusion.2), channel_id=1, source_target_pairs={{0,8},{1,9},{2,10},{3,11},{4,12},{5,13},{6,14},{7,15},{8,0},{9,1},... | collective-permute-start | bytes 393224 | tf_op jit(solution)/shard_map/ppermute | solution.py:299
  60.9 1.5 %collective-permute-done.19 = bf16[512,128]{1,0:T(8,128)(2,1)S(1)} collective-permute-done((bf16[512,128]{1,0:T(8,128)(2,1)}, bf16[512,128]{1,0:T(8,128)(2,1)S(1)}, u32[]{:S(2)}, u32[]{:S(2)}) %collective-permute-start.19) | collective-permute-done | bytes 131104 | tf_op jit(solution)/shard_map/ppermute | solution.py:299
  62.4 3.1 %collective-permute-done.23 = bf16[512,128]{1,0:T(8,128)(2,1)} collective-permute-done((bf16[512,128]{1,0:T(8,128)(2,1)}, bf16[512,128]{1,0:T(8,128)(2,1)}, u32[]{:S(2)}, u32[]{:S(2)}) %collective-permute-start.23) | collective-permute-done | bytes 131104 | tf_op jit(solution)/shard_map/ppermute | solution.py:299
  65.5 3.5 %collective-permute-done.16 = bf16[512,256]{1,0:T(8,128)(2,1)} collective-permute-done((bf16[512,256]{1,0:T(8,128)(2,1)}, bf16[512,256]{1,0:T(8,128)(2,1)}, u32[]{:S(2)}, u32[]{:S(2)}) %collective-permute-start.16) | collective-permute-done | bytes 262176 | tf_op jit(solution)/shard_map/ppermute | solution.py:299
  69.0 1.3 %add_convert_fusion = bf16[512,256]{1,0:T(8,128)(2,1)S(1)} fusion(bf16[512,256]{1,0:T(8,128)(2,1)} %collective-permute-done.16, bf16[512,256]{1,0:T(8,128)(2,1)} %collective-permute-done.14, bf16[512,128]{1,0:T(8,128)(2,1)} %copy-done.3, bf16[512,128]{1,0:T(8,128)(2,1)} %copy-done.2, bf16[512,128]{1,0:T(8,128)(2,1)} %collective-permute-done.23, ...), kind=kLoop, calls=%fused_computation.1 | loop fusion | flops 1835008 | bytes 1310720 | tf_op jit(solution)/shard_map/convert_element_type | solution.py:306
  70.4 2.0 %collective-permute-start.24 = (bf16[256,256]{1,0:T(8,128)(2,1)S(1)}, bf16[256,256]{1,0:T(8,128)(2,1)S(1)}, u32[]{:S(2)}, u32[]{:S(2)}) collective-permute-start(bf16[256,256]{1,0:T(8,128)(2,1)S(1)} %get-tuple-element.33), channel_id=1, source_target_pairs={{0,1},{1,0},{2,3},{3,2},{4,5},{5,4},{6,7},{7,6},{8,9},{9,8},{10,11... | collective-permute-start | bytes 393224 | tf_op jit(solution)/shard_map/ppermute | solution.py:299
  73.3 2.6 %last_step.1 = f32[256,4096]{1,0:T(8,128)} custom-call(bf16[256,256]{1,0:T(8,128)(2,1)S(1)} %get-tuple-element.34.own, bf16[256,256]{1,0:T(8,128)(2,1)S(1)} %collective-permute-done.24.other, f32[2,4,64,128]{3,2,1,0:T(8,128)S(1)} %copy-done.1), custom_call_target="tpu_custom_call" | custom-call | tf_op jit(solution)/shard_map/last_step/pallas_call | solution.py:283
  (55 shorter events, 12.5 us)
Async XLA Ops:
  0.0 9.3 %collective-permute-start = (bf16[40,512,128]{2,1,0:T(8,128)(2,1)}, bf16[40,512,128]{2,1,0:T(8,128)(2,1)}, u32[]{:S(2)}, u32[]{:S(2)}) collective-permute-start(bf16[40,512,128]{2,1,0:T(8,128)(2,1)} %refs_6_.1), channel_id=1, source_target_pairs={{0,1},{1,0},{2,3},{3,2},{4,5},{5,4},{6,7},{7,6},{8,9},{9,8},{10,11... | collective-permute-start | bytes 15728648 | tf_op jit(solution)/shard_map/ppermute | solution.py:299
  3.8 4.9 %collective-permute-start.8 = (bf16[32,768]{1,0:T(8,128)(2,1)S(1)}, bf16[32,768]{1,0:T(8,128)(2,1)S(1)}, u32[]{:S(2)}, u32[]{:S(2)}) collective-permute-start(bf16[32,768]{1,0:T(8,128)(2,1)S(1)} %get-tuple-element.39), channel_id=1, source_target_pairs={{0,2},{1,3},{2,0},{3,1},{4,6},{5,7},{6,4},{7,5},{8,10},{9,11},{10,... | collective-permute-start | bytes 147464 | tf_op jit(solution)/shard_map/ppermute | solution.py:299
  5.1 7.9 %collective-permute-start.2 = (bf16[32,768]{1,0:T(8,128)(2,1)S(1)}, bf16[32,768]{1,0:T(8,128)(2,1)S(1)}, u32[]{:S(2)}, u32[]{:S(2)}) collective-permute-start(bf16[32,768]{1,0:T(8,128)(2,1)S(1)} %get-tuple-element.40), channel_id=1, source_target_pairs={{0,4},{1,5},{2,6},{3,7},{4,0},{5,1},{6,2},{7,3},{8,12},{9,13},{10,... | collective-permute-start | bytes 147464 | tf_op jit(solution)/shard_map/ppermute | solution.py:299
  6.4 7.0 %collective-permute-start.3 = (bf16[32,768]{1,0:T(8,128)(2,1)S(1)}, bf16[32,768]{1,0:T(8,128)(2,1)S(1)}, u32[]{:S(2)}, u32[]{:S(2)}) collective-permute-start(bf16[32,768]{1,0:T(8,128)(2,1)S(1)} %get-tuple-element.40), channel_id=1, source_target_pairs={{0,8},{1,9},{2,10},{3,11},{4,12},{5,13},{6,14},{7,15},{8,0},{9,1},... | collective-permute-start | bytes 147464 | tf_op jit(solution)/shard_map/ppermute | solution.py:299
  8.7 6.3 %collective-permute-start.4 = (bf16[32,768]{1,0:T(8,128)(2,1)S(1)}, bf16[32,768]{1,0:T(8,128)(2,1)S(1)}, u32[]{:S(2)}, u32[]{:S(2)}) collective-permute-start(bf16[32,768]{1,0:T(8,128)(2,1)S(1)} %get-tuple-element.40), channel_id=1, source_target_pairs={{0,12},{1,13},{2,14},{3,15},{4,8},{5,9},{6,10},{7,11},{8,4},{9,5},... | collective-permute-start | bytes 147464 | tf_op jit(solution)/shard_map/ppermute | solution.py:299
  8.7 7.1 %collective-permute-start.9 = (bf16[2,32,768]{2,1,0:T(8,128)(2,1)S(1)}, bf16[2,32,768]{2,1,0:T(8,128)(2,1)S(1)}, u32[]{:S(2)}, u32[]{:S(2)}) collective-permute-start(bf16[2,32,768]{2,1,0:T(8,128)(2,1)S(1)} %get-tuple-element.36), channel_id=1, source_target_pairs={{0,4},{1,5},{2,6},{3,7},{4,0},{5,1},{6,2},{7,3},{8,12},{9,13},{10,... | collective-permute-start | bytes 294920 | tf_op jit(solution)/shard_map/ppermute | solution.py:299
  9.3 6.6 %collective-permute-start.10 = (bf16[2,32,768]{2,1,0:T(8,128)(2,1)S(1)}, bf16[2,32,768]{2,1,0:T(8,128)(2,1)S(1)}, u32[]{:S(2)}, u32[]{:S(2)}) collective-permute-start(bf16[2,32,768]{2,1,0:T(8,128)(2,1)S(1)} %get-tuple-element.36), channel_id=1, source_target_pairs={{0,8},{1,9},{2,10},{3,11},{4,12},{5,13},{6,14},{7,15},{8,0},{9,1},... | collective-permute-start | bytes 294920 | tf_op jit(solution)/shard_map/ppermute | solution.py:299
  13.0 6.2 %collective-permute-start.11 = (bf16[2,32,768]{2,1,0:T(8,128)(2,1)S(1)}, bf16[2,32,768]{2,1,0:T(8,128)(2,1)S(1)}, u32[]{:S(2)}, u32[]{:S(2)}) collective-permute-start(bf16[2,32,768]{2,1,0:T(8,128)(2,1)S(1)} %get-tuple-element.36), channel_id=1, source_target_pairs={{0,12},{1,13},{2,14},{3,15},{4,8},{5,9},{6,10},{7,11},{8,4},{9,5},... | collective-permute-start | bytes 294920 | tf_op jit(solution)/shard_map/ppermute | solution.py:299
  13.4 2.4 %collective-permute-start.1 = (s32[89]{0:T(128)S(1)}, s32[89]{0:T(128)S(1)}, u32[]{:S(2)}, u32[]{:S(2)}) collective-permute-start(s32[89]{0:T(128)S(1)} %fusion.1), channel_id=1, source_target_pairs={{0,1},{1,0},{2,3},{3,2},{4,5},{5,4},{6,7},{7,6},{8,9},{9,8},{10,11... | collective-permute-start | bytes 1076 | tf_op jit(solution)/shard_map/ppermute | solution.py:299
  15.0 7.7 %collective-permute-start.6 = (bf16[4,32,768]{2,1,0:T(8,128)(2,1)S(1)}, bf16[4,32,768]{2,1,0:T(8,128)(2,1)S(1)}, u32[]{:S(2)}, u32[]{:S(2)}) collective-permute-start(bf16[4,32,768]{2,1,0:T(8,128)(2,1)S(1)} %pad_maximum_fusion.refs_0_), channel_id=1, source_target_pairs={{0,2},{1,3},{2,0},{3,1},{4,6},{5,7},{6,4},{7,5},{8,10},{9,11},{10,... | collective-permute-start | bytes 589832 | tf_op jit(solution)/shard_map/ppermute | solution.py:299
  20.1 4.9 %collective-permute-start.12 = (bf16[4,2,32,768]{3,2,1,0:T(8,128)(2,1)}, bf16[4,2,32,768]{3,2,1,0:T(8,128)(2,1)}, u32[]{:S(2)}, u32[]{:S(2)}) collective-permute-start(bf16[4,2,32,768]{3,2,1,0:T(8,128)(2,1)} %maximum_add_fusion.refs_4_), channel_id=1, source_target_pairs={{0,1},{1,0},{2,3},{3,2},{4,5},{5,4},{6,7},{7,6},{8,9},{9,8},{10,11... | collective-permute-start | bytes 1179656 | tf_op jit(solution)/shard_map/ppermute | solution.py:299
  22.8 2.0 %collective-permute-start.7 = (bf16[4,32,768]{2,1,0:T(8,128)(2,1)S(1)}, bf16[4,32,768]{2,1,0:T(8,128)(2,1)}, u32[]{:S(2)}, u32[]{:S(2)}) collective-permute-start(bf16[4,32,768]{2,1,0:T(8,128)(2,1)S(1)} %collective-permute-done.6.refs_2_), channel_id=1, source_target_pairs={{0,1},{1,0},{2,3},{3,2},{4,5},{5,4},{6,7},{7,6},{8,9},{9,8},{10,11... | collective-permute-start | bytes 589832 | tf_op jit(solution)/shard_map/ppermute | solution.py:299
  34.0 6.2 %collective-permute-start.13 = (bf16[512,128]{1,0:T(8,128)(2,1)S(1)}, bf16[512,128]{1,0:T(8,128)(2,1)S(1)}, u32[]{:S(2)}, u32[]{:S(2)}) collective-permute-start(bf16[512,128]{1,0:T(8,128)(2,1)S(1)} %get-tuple-element.23), channel_id=1, source_target_pairs={{0,2},{1,3},{2,0},{3,1},{4,6},{5,7},{6,4},{7,5},{8,10},{9,11},{10,... | collective-permute-start | bytes 393224 | tf_op jit(solution)/shard_map/ppermute | solution.py:299
  36.6 11.9 %collective-permute-start.17 = (bf16[512,128]{1,0:T(8,128)(2,1)S(1)}, bf16[512,128]{1,0:T(8,128)(2,1)S(1)}, u32[]{:S(2)}, u32[]{:S(2)}) collective-permute-start(bf16[512,128]{1,0:T(8,128)(2,1)S(1)} %get-tuple-element.27), channel_id=1, source_target_pairs={{0,2},{1,3},{2,0},{3,1},{4,6},{5,7},{6,4},{7,5},{8,10},{9,11},{10,... | collective-permute-start | bytes 393224 | tf_op jit(solution)/shard_map/ppermute | solution.py:299
  36.7 9.1 %collective-permute-start.21 = (bf16[512,128]{1,0:T(8,128)(2,1)S(1)}, bf16[512,128]{1,0:T(8,128)(2,1)S(1)}, u32[]{:S(2)}, u32[]{:S(2)}) collective-permute-start(bf16[512,128]{1,0:T(8,128)(2,1)S(1)} %get-tuple-element.31), channel_id=1, source_target_pairs={{0,2},{1,3},{2,0},{3,1},{4,6},{5,7},{6,4},{7,5},{8,10},{9,11},{10,... | collective-permute-start | bytes 393224 | tf_op jit(solution)/shard_map/ppermute | solution.py:299
  38.1 18.3 %collective-permute-start.15 = (bf16[512,256]{1,0:T(8,128)(2,1)S(1)}, bf16[512,256]{1,0:T(8,128)(2,1)S(1)}, u32[]{:S(2)}, u32[]{:S(2)}) collective-permute-start(bf16[512,256]{1,0:T(8,128)(2,1)S(1)} %get-tuple-element.25), channel_id=1, source_target_pairs={{0,2},{1,3},{2,0},{3,1},{4,6},{5,7},{6,4},{7,5},{8,10},{9,11},{10,... | collective-permute-start | bytes 786440 | tf_op jit(solution)/shard_map/ppermute | solution.py:299
  40.2 9.5 %collective-permute-start.18 = (bf16[512,128]{1,0:T(8,128)(2,1)S(1)}, bf16[512,128]{1,0:T(8,128)(2,1)S(1)}, u32[]{:S(2)}, u32[]{:S(2)}) collective-permute-start(bf16[512,128]{1,0:T(8,128)(2,1)S(1)} %add_convert_fusion.5), channel_id=1, source_target_pairs={{0,4},{1,5},{2,6},{3,7},{4,0},{5,1},{6,2},{7,3},{8,12},{9,13},{10,... | collective-permute-start | bytes 393224 | tf_op jit(solution)/shard_map/ppermute | solution.py:299
  44.1 13.2 %collective-permute-start.20 = (bf16[512,128]{1,0:T(8,128)(2,1)S(1)}, bf16[512,128]{1,0:T(8,128)(2,1)S(1)}, u32[]{:S(2)}, u32[]{:S(2)}) collective-permute-start(bf16[512,128]{1,0:T(8,128)(2,1)S(1)} %broadcast_add_fusion.1), channel_id=1, source_target_pairs={{0,2},{1,3},{2,0},{3,1},{4,6},{5,7},{6,4},{7,5},{8,10},{9,11},{10,... | collective-permute-start | bytes 393224 | tf_op jit(solution)/shard_map/ppermute | solution.py:299
  45.9 11.4 %collective-permute-start.22 = (bf16[512,128]{1,0:T(8,128)(2,1)S(1)}, bf16[512,128]{1,0:T(8,128)(2,1)S(1)}, u32[]{:S(2)}, u32[]{:S(2)}) collective-permute-start(bf16[512,128]{1,0:T(8,128)(2,1)S(1)} %add_convert_fusion.3), channel_id=1, source_target_pairs={{0,4},{1,5},{2,6},{3,7},{4,0},{5,1},{6,2},{7,3},{8,12},{9,13},{10,... | collective-permute-start | bytes 393224 | tf_op jit(solution)/shard_map/ppermute | solution.py:299
  48.6 16.9 %collective-permute-start.14 = (bf16[512,256]{1,0:T(8,128)(2,1)}, bf16[512,256]{1,0:T(8,128)(2,1)}, u32[]{:S(2)}, u32[]{:S(2)}) collective-permute-start(bf16[512,256]{1,0:T(8,128)(2,1)} %broadcast_add_fusion), channel_id=1, source_target_pairs={{0,2},{1,3},{2,0},{3,1},{4,6},{5,7},{6,4},{7,5},{8,10},{9,11},{10,... | collective-permute-start | bytes 786440 | tf_op jit(solution)/shard_map/ppermute | solution.py:299
  50.4 11.9 %collective-permute-start.19 = (bf16[512,128]{1,0:T(8,128)(2,1)}, bf16[512,128]{1,0:T(8,128)(2,1)S(1)}, u32[]{:S(2)}, u32[]{:S(2)}) collective-permute-start(bf16[512,128]{1,0:T(8,128)(2,1)} %add_convert_fusion.4), channel_id=1, source_target_pairs={{0,8},{1,9},{2,10},{3,11},{4,12},{5,13},{6,14},{7,15},{8,0},{9,1},... | collective-permute-start | bytes 393224 | tf_op jit(solution)/shard_map/ppermute | solution.py:299
  57.2 11.8 %collective-permute-start.16 = (bf16[512,256]{1,0:T(8,128)(2,1)}, bf16[512,256]{1,0:T(8,128)(2,1)}, u32[]{:S(2)}, u32[]{:S(2)}) collective-permute-start(bf16[512,256]{1,0:T(8,128)(2,1)} %add_convert_fusion.1), channel_id=1, source_target_pairs={{0,4},{1,5},{2,6},{3,7},{4,0},{5,1},{6,2},{7,3},{8,12},{9,13},{10,... | collective-permute-start | bytes 786440 | tf_op jit(solution)/shard_map/ppermute | solution.py:299
  58.0 7.6 %collective-permute-start.23 = (bf16[512,128]{1,0:T(8,128)(2,1)}, bf16[512,128]{1,0:T(8,128)(2,1)}, u32[]{:S(2)}, u32[]{:S(2)}) collective-permute-start(bf16[512,128]{1,0:T(8,128)(2,1)} %add_convert_fusion.2), channel_id=1, source_target_pairs={{0,8},{1,9},{2,10},{3,11},{4,12},{5,13},{6,14},{7,15},{8,0},{9,1},... | collective-permute-start | bytes 393224 | tf_op jit(solution)/shard_map/ppermute | solution.py:299
  70.4 3.0 %collective-permute-start.24 = (bf16[256,256]{1,0:T(8,128)(2,1)S(1)}, bf16[256,256]{1,0:T(8,128)(2,1)S(1)}, u32[]{:S(2)}, u32[]{:S(2)}) collective-permute-start(bf16[256,256]{1,0:T(8,128)(2,1)S(1)} %get-tuple-element.33), channel_id=1, source_target_pairs={{0,1},{1,0},{2,3},{3,2},{4,5},{5,4},{6,7},{7,6},{8,9},{9,8},{10,11... | collective-permute-start | bytes 393224 | tf_op jit(solution)/shard_map/ppermute | solution.py:299
  (5 other events, 90.6 us)
